TPU v7x, 128 devices: a whole 4x4x4 slice. The times are simulated.
128 devices in a mesh: seq: 8 (over x, core), dp: 16 (over z, y).
Axes of the slice: x: 4, y: 4, z: 4, core: 2. Of those that a mesh axis runs over, the one named last changes fastest.
Arguments:
- text_rows: bfloat16 [2, 3072, 4096], P(None, 'seq', 'dp'), may hold values from -7 to 7
- latents: bfloat16 [16, 256, 32], P('dp', 'seq'), may hold values from -6 to 6
- image_seq: int32 [16], replicated, may hold values from 0 to 1, as said below
- image_start: int32 [16], replicated, may hold values from 0 to 2816, as said below
- norm_gain: float32 [4096], replicated, may hold values from 0.5 to 1.5
- w_patch: bfloat16 [32, 4096], replicated, may hold values from -1 to 1
- w_query: bfloat16 [4096, 4096], P(None, 'dp'), may hold values from -1 to 1
- w_key: bfloat16 [4096, 4096], P(None, 'dp'), may hold values from -1 to 1
- w_value: bfloat16 [4096, 4096], P(None, 'dp'), may hold values from -0.09375 to 0.09375
- out_grad: bfloat16 [2, 3072, 4096], P(None, 'seq', 'dp'), may hold values from -6 to 6
Outputs:
- attended: bfloat16 [2, 3072, 4096], P(None, 'seq', 'dp')
- latent_grad: float32 [16, 256, 32], P('dp', 'seq')
Inputs may be any that keep to these rules, and one draw needn't show every extreme that they name: `image_seq`: each packed sequence holds exactly 8 images. `image_start`: the positions of a sequence fall into 8 aligned blocks of 384, each holding one whole image of that sequence.
All inputs are finite; a program needn't handle non-finite values.
Results may differ from a plain program's by a relative error of at most 0.028.
Values may be sent and summed in bfloat16 or wider, within the bound.
No kernel may reach another device: no remote copies, remote signals or barrier semaphores. Data moves between devices by JAX's collectives and lax.ppermute only.
A program may use at most 128 MiB of HBM per device.

v0:
```python
import jax
import jax.numpy as jnp
from jax import lax
from jax.sharding import PartitionSpec as P

HD = 128
PATCHES = 256


epsilon = 1e-05


def image_layout(image_seq, image_start, seq_count, places):
    owners = image_seq[None, :] == jnp.arange(seq_count, dtype=jnp.int32)[:, None]
    offset = places[:, None] - image_start[None, :]
    covers = owners[:, None, :] & (offset[None] >= 0) & (offset[None] < PATCHES)
    inside = jnp.any(covers, axis=2)
    labels = jnp.arange(image_seq.shape[0], dtype=jnp.int32)
    member = jnp.where(inside, jnp.sum(jnp.where(covers, labels[None, None, :], 0), axis=2), -1)
    patch_index = jnp.sum(
        jnp.where(covers, labels[None, None, :] * PATCHES + offset[None], 0), axis=2
    )
    return (inside, member, patch_index)


def on_device(
    text_rows,
    latents,
    image_seq,
    image_start,
    norm_gain,
    w_patch,
    w_query,
    w_key,
    w_value,
    out_grad,
):
    tokens = text_rows.shape[1]
    length = tokens * lax.axis_size("seq")
    first_place = lax.axis_index("seq") * tokens
    score_scale = HD ** (-0.5)
    gathered = lax.all_gather(text_rows, "dp", axis=2, tiled=True)
    seq_count = gathered.shape[0]
    images = image_seq.shape[0]
    patches = lax.all_gather(
        latents.reshape(latents.shape[0] * latents.shape[1], latents.shape[2]),
        ("dp", "seq"),
        axis=0,
        tiled=True,
    )
    own_places = first_place + jnp.arange(tokens, dtype=jnp.int32)
    all_places = jnp.arange(length, dtype=jnp.int32)
    inside_all, member_all, patch_all = image_layout(image_seq, image_start, seq_count, all_places)
    inside = lax.dynamic_slice_in_dim(inside_all, first_place, tokens, 1)
    member = lax.dynamic_slice_in_dim(member_all, first_place, tokens, 1)
    patch_index = lax.dynamic_slice_in_dim(patch_all, first_place, tokens, 1)
    picked = jnp.take(patches, patch_index, axis=0)
    embedded = jnp.einsum(
        "srp,pd->srd", picked, w_patch, preferred_element_type=jnp.float32
    ).astype(jnp.bfloat16)
    hidden = jnp.where(inside[:, :, None], embedded, gathered)
    hidden_f = hidden.astype(jnp.float32)
    inv_rms = lax.rsqrt(jnp.mean(hidden_f * hidden_f, axis=-1, keepdims=True) + epsilon)
    unit_rows = hidden_f * inv_rms
    normed = (unit_rows * norm_gain).astype(jnp.bfloat16)
    head_count = w_query.shape[1] // HD

    def project(weight):
        return jnp.einsum("srd,dc->src", normed, weight, preferred_element_type=jnp.float32).astype(
            jnp.bfloat16
        )

    def split_heads(array):
        return array.reshape(array.shape[0], array.shape[1], head_count, HD)

    queries = project(w_query)
    key_rows = project(w_key)
    value_rows = project(w_value)
    key_all, value_all = (
        lax.all_gather(key_rows, "seq", axis=1, tiled=True),
        lax.all_gather(value_rows, "seq", axis=1, tiled=True),
    )

    def attend(inputs):
        query_s, key_s, value_s, grad_s, member_q, member_k, inside_q = inputs
        allowed = (all_places[None, :] <= own_places[:, None]) | (
            member_q[:, None] == member_k[None, :]
        ) & inside_q[:, None]
        scores = (
            jnp.einsum("qhd,khd->hqk", query_s, key_s, preferred_element_type=jnp.float32)
            * score_scale
        )
        masked = jnp.where(allowed[None], scores, -jnp.inf)
        row_max = jnp.max(masked, axis=-1, keepdims=True)
        lifted = jnp.exp(masked - row_max)
        row_total = jnp.sum(lifted, axis=-1, keepdims=True)
        attn_probs = lifted / row_total
        probs_b = attn_probs.astype(jnp.bfloat16)
        out_f = jnp.einsum("hqk,khd->qhd", probs_b, value_s, preferred_element_type=jnp.float32)
        row_delta = jnp.sum(grad_s.astype(jnp.float32) * out_f, axis=-1).T
        d_probs = jnp.einsum("qhd,khd->hqk", grad_s, value_s, preferred_element_type=jnp.float32)
        d_scores = (attn_probs * (d_probs - row_delta[:, :, None]) * score_scale).astype(
            jnp.bfloat16
        )
        d_query = jnp.einsum(
            "hqk,khd->qhd", d_scores, key_s, preferred_element_type=jnp.float32
        ).astype(jnp.bfloat16)
        part_keys = jnp.einsum(
            "hqk,qhd->khd", d_scores, query_s, preferred_element_type=jnp.float32
        )
        part_values = jnp.einsum(
            "hqk,qhd->khd", probs_b, grad_s, preferred_element_type=jnp.float32
        )
        extra = (part_keys, part_values)
        return (out_f.astype(jnp.bfloat16), d_query) + extra

    results = lax.map(
        attend,
        (
            split_heads(queries),
            split_heads(key_all),
            split_heads(value_all),
            split_heads(out_grad),
            member,
            member_all,
            inside,
        ),
    )
    attended = results[0].reshape(seq_count, tokens, head_count * HD)
    d_query = results[1]
    part_keys = results[2].reshape(seq_count, length, head_count * HD)
    part_values = results[3].reshape(seq_count, length, head_count * HD)
    sum_keys, sum_values = (
        lax.psum_scatter(part_keys, "seq", scatter_dimension=1, tiled=True),
        lax.psum_scatter(part_values, "seq", scatter_dimension=1, tiled=True),
    )
    d_keys = sum_keys.astype(jnp.bfloat16)
    d_values = sum_values.astype(jnp.bfloat16)

    def project_back(grad_heads, weight):
        flat_grad = grad_heads.reshape(seq_count, tokens, head_count * HD)
        return jnp.einsum("src,dc->srd", flat_grad, weight, preferred_element_type=jnp.float32)

    d_normed = (
        project_back(d_query, w_query)
        + project_back(d_keys, w_key)
        + project_back(d_values, w_value)
    )
    gained = norm_gain * d_normed
    d_hidden = inv_rms * (gained - unit_rows * jnp.mean(unit_rows * gained, axis=-1, keepdims=True))
    d_rows = jnp.einsum(
        "srd,pd->srp", d_hidden, w_patch.astype(jnp.float32), precision=lax.Precision.HIGHEST
    )
    targets = jnp.where(inside, patch_index, images * PATCHES)
    contrib = jax.ops.segment_sum(
        d_rows.reshape(seq_count * tokens, d_rows.shape[2]),
        targets.reshape(seq_count * tokens),
        num_segments=images * PATCHES + 1,
    )
    owners_count = lax.axis_size("dp") * lax.axis_size("seq")
    dense_terms = contrib[: images * PATCHES].reshape(
        owners_count, images * PATCHES * d_rows.shape[2] // owners_count
    )
    mine = lax.psum_scatter(dense_terms, ("dp", "seq"), scatter_dimension=0, tiled=True)
    return (attended, mine.reshape(latents.shape))


def solution(mesh):
    in_specs = (
        P(None, "seq", "dp"),
        P("dp", "seq", None),
        P(),
        P(),
        P(),
        P(),
        P(None, "dp"),
        P(None, "dp"),
        P(None, "dp"),
        P(None, "seq", "dp"),
    )
    out_specs = (P(None, "seq", "dp"), P("dp", "seq", None))
    return jax.shard_map(
        on_device, mesh=mesh, in_specs=in_specs, out_specs=out_specs, check_vma=False
    )
```

profile of v0, /device:TPU:1, one launch (start us, length us, event | category | flops | bytes accessed | tf_op | source)
XLA Modules:
  0.0 541.4 jit_solution(3638304887182020937)
XLA Ops:
  11.3 39.6 %all-gather = bf16[1,4096,32]{2,1,0:T(8,128)(2,1)S(1)} all-gather(bf16[1,32,32]{2,1,0:T(8,128)(2,1)} %param.13), channel_id=2, replica_groups=mesh['seq'=8,'dp'=16] {'dp','seq'}, dimensions={1}, use_global_device_ids=true | all-gather | bytes 264192 | tf_op jit(solution)/shard_map/all_gather | solution.py:45
  50.9 1.9 gather_fusion
  52.9 27.7 %all-gather.5.cloned.1.call-done = bf16[2,384,4096]{2,1,0:T(8,128)(2,1)} async-done(((bf16[2,384,256]{2,1,0:T(8,128)(2,1)}), bf16[2,384,4096]{2,1,0:T(8,128)(2,1)}) %all-gather.5.cloned.1.call-update) | async-done | bytes 6291472 | tf_op jit(solution)/shard_map/all_gather | solution.py:42
  80.7 4.7 fusion.51
  85.4 2.7 copy-done.2
  88.1 2.6 fusion.78
  90.8 5.4 fusion.68
  97.3 6.5 %fusion.73 = bf16[2,384,256]{1,2,0:T(8,128)(2,1)} fusion(bf16[4096,256]{1,0:T(8,128)(2,1)} %param.18, bf16[2,384,4096]{2,1,0:T(8,128)(2,1)} %copy-done.2, f32[4096]{0:T(1024)S(1)} %copy-done.17, f32[2,384]{1,0:T(2,128)S(1)} %add_rsqrt_fusion), kind=kOutput, calls=%fused_computation.83 | convolution fusion | flops 1623392256 | bytes 8801280 | tf_op jit(solution)/shard_map/srd,dc->src/dot_general | solution.py:69
  103.7 15.4 %all-gather.9.cloned.1.call-done = bf16[2,3072,256]{2,1,0:T(8,128)(2,1)} async-done(((bf16[2,384,256]{2,1,0:T(8,128)(2,1)}), bf16[2,3072,256]{2,1,0:T(8,128)(2,1)}) %all-gather.9.cloned.1.call-update) | async-done | bytes 3145744 | tf_op jit(solution)/shard_map/all_gather | solution.py:80
  119.1 5.5 %reshape.238 = bf16[2,3072,2,128]{3,2,1,0:T(2,128)(2,1)} reshape(bf16[2,3072,256]{2,1,0:T(8,128)(2,1)} %all-gather.9.cloned.1.call-done) | data formatting | bytes 6291456 | tf_op jit(solution)/shard_map/reshape | solution.py:74
  124.6 24.0 %all-gather.7.cloned.1.call-done = bf16[2,3072,256]{2,1,0:T(8,128)(2,1)} async-done(((bf16[2,384,256]{2,1,0:T(8,128)(2,1)}), bf16[2,3072,256]{2,1,0:T(8,128)(2,1)}) %all-gather.7.cloned.1.call-update) | async-done | bytes 3145744 | tf_op jit(solution)/shard_map/all_gather | solution.py:81
  148.6 4.7 copy.95
  153.3 100.4 %while.17 = (s32[]{:T(128)}, bf16[2,384,2,128]{1,3,2,0:T(8,128)(2,1)}, bf16[2,384,2,128]{1,3,2,0:T(8,128)(2,1)}, f32[2,3072,2,128]{1,3,2,0:T(8,128)}, f32[2,3072...) while((s32[]{:T(128)}, ...), condition=%wide.region_8.9_spmd.clone, body=%wide.region_4.8_spmd.clone.sunk | while | flops 3659762176 | bytes 161873984 | solution.py:117
  153.6 1.7 fusion.131
  155.3 2.8 constant_dynamic-slice_fusion.7
  158.1 6.0 %fusion.129 = f32[2,384,3072]{2,1,0:T(8,128)} fusion(bf16[1,3072,2,128]{3,2,1,0:T(2,128)(2,1)S(1)} %constant_dynamic-slice_fusion.7, bf16[2,384,2,128]{1,3,2,0:T(8,128)(2,1)} %get-tuple-element.341, s32[]{:T(128)S(6)} %copy.124), kind=kOutput, calls=%fused_computation.25.clone.1 | convolution fusion | flops 603979776 | bytes 11206660 | tf_op jit(solution)/shard_map/while/body/eval_jaxpr/qhd,khd->hqk/dot_general | solution.py:90
  164.1 14.5 %fusion.132 = (f32[2,384]{1,0:T(2,128)S(1)}, f32[2,384,3072]{2,1,0:T(8,128)}) fusion(f32[2,384,3072]{2,1,0:T(8,128)} %fusion.129, pred[384,3072]{1,0:T(8,128)(4,1)S(1)} %fusion.131), kind=kOutput, calls=%fused_computation.115.clone.1 | output fusion | flops 14158847 | bytes 20057088 | tf_op jit(solution)/shard_map/while/body/eval_jaxpr/sub | solution.py:95
  178.6 5.3 fusion.133
  183.9 1.6 bitcast_dynamic-update-slice_fusion.2
  185.6 4.9 multiply_convert_fusion.2
  190.5 1.7 fusion.134
  192.2 2.7 fusion.135
  194.9 1.0 fusion.136
  195.9 2.7 copy-done.5
  198.7 1.7 fusion.131
  200.4 2.8 constant_dynamic-slice_fusion.7
  203.3 6.0 %fusion.129 = f32[2,384,3072]{2,1,0:T(8,128)} fusion(bf16[1,3072,2,128]{3,2,1,0:T(2,128)(2,1)S(1)} %constant_dynamic-slice_fusion.7, bf16[2,384,2,128]{1,3,2,0:T(8,128)(2,1)} %get-tuple-element.341, s32[]{:T(128)S(6)} %copy.124), kind=kOutput, calls=%fused_computation.25.clone.1 | convolution fusion | flops 603979776 | bytes 11206660 | tf_op jit(solution)/shard_map/while/body/eval_jaxpr/qhd,khd->hqk/dot_general | solution.py:90
  209.2 14.5 %fusion.132 = (f32[2,384]{1,0:T(2,128)S(1)}, f32[2,384,3072]{2,1,0:T(8,128)}) fusion(f32[2,384,3072]{2,1,0:T(8,128)} %fusion.129, pred[384,3072]{1,0:T(8,128)(4,1)S(1)} %fusion.131), kind=kOutput, calls=%fused_computation.115.clone.1 | output fusion | flops 14158847 | bytes 20057088 | tf_op jit(solution)/shard_map/while/body/eval_jaxpr/sub | solution.py:95
  223.7 5.3 fusion.133
  229.0 1.6 bitcast_dynamic-update-slice_fusion.2
  230.7 4.9 multiply_convert_fusion.2
  235.6 1.7 fusion.134
  237.4 2.7 fusion.135
  240.0 1.0 fusion.136
  241.0 2.7 copy-done.5
  253.6 6.6 %copy.85 = f32[2,3072,256]{2,1,0:T(8,128)} copy(f32[2,3072,256]{1,2,0:T(8,128)} %bitcast.148) | data formatting | bytes 12582912 | tf_op jit(solution)/shard_map/reshape | solution.py:131
  260.3 6.6 %copy.86 = f32[2,3072,256]{2,1,0:T(8,128)} copy(f32[2,3072,256]{1,2,0:T(8,128)} %bitcast.147) | data formatting | bytes 12582912 | tf_op jit(solution)/shard_map/reshape | solution.py:132
  267.9 8.4 %fusion.63 = f32[2,384,4096]{2,1,0:T(8,128)} fusion(bf16[2,384,256]{1,2,0:T(8,128)(2,1)S(1)} %bitcast.152, bf16[4096,256]{1,0:T(8,128)(2,1)} %param.18), kind=kOutput, calls=%fused_computation.77 | convolution fusion | flops 1610612736 | bytes 15073280 | tf_op jit(solution)/shard_map/src,dc->srd/dot_general | solution.py:142
  276.3 25.6 %reduce-scatter.3.cloned.1.call-done = f32[2,384,256]{2,1,0:T(8,128)} async-done(((f32[2,3072,256]{2,1,0:T(8,128)}), f32[2,384,256]{2,1,0:T(8,128)}) %reduce-scatter.3.cloned.1.call-update) | async-done | bytes 786448 | tf_op jit(solution)/shard_map/reduce_scatter | solution.py:134
  301.9 8.2 %fusion.60 = f32[2,384,4096]{2,1,0:T(8,128)} fusion(bf16[4096,256]{1,0:T(8,128)(2,1)} %param.19, f32[2,384,256]{2,1,0:T(8,128)} %reduce-scatter.3.cloned.1.call-done), kind=kOutput, calls=%fused_computation.74 | convolution fusion | flops 1610809344 | bytes 15466496 | tf_op jit(solution)/shard_map/src,dc->srd/dot_general | solution.py:142
  310.1 36.2 %reduce-scatter.5.cloned.1.call-done = f32[2,384,256]{2,1,0:T(8,128)} async-done(((f32[2,3072,256]{2,1,0:T(8,128)}), f32[2,384,256]{2,1,0:T(8,128)}) %reduce-scatter.5.cloned.1.call-update) | async-done | bytes 786448 | tf_op jit(solution)/shard_map/reduce_scatter | solution.py:135
  346.4 14.6 %fusion.46 = (f32[2,384]{1,0:T(2,128)S(1)}, f32[2,384,4096]{2,1,0:T(8,128)}) fusion(bf16[2,384,4096]{2,1,0:T(8,128)(2,1)} %copy-done.2, f32[2,384]{1,0:T(2,128)S(1)} %copy-done.16, bf16[4096,256]{1,0:T(8,128)(2,1)S(1)} %copy-done, f32[2,384,256]{2,1,0:T(8,128)} %reduce-scatter.5.cloned.1.call-done, f32[2,384,4096]{2,1,0:T(8,128)} %fusion.63, ...), kind=kOutput, calls=%fused_computation.61 | convolution fusion | flops 1632828672 | bytes 46946304 | tf_op jit(solution)/shard_map/src,dc->srd/dot_general | solution.py:142
  361.0 11.5 %fusion.49 = f32[2,384,32]{2,1,0:T(8,128)S(1)} fusion(f32[2,384,4096]{2,1,0:T(8,128)} %get-tuple-element.215, bf16[2,384,4096]{2,1,0:T(8,128)(2,1)} %copy-done.2, f32[2,384]{1,0:T(2,128)S(1)} %broadcast_multiply_fusion, f32[2,384]{1,0:T(2,128)S(1)} %copy-done.16, bf16[32,4096]{1,0:T(8,128)(2,1)S(1)} %copy-done.14), kind=kOutput, calls=%fused_computation.64 | convolution fusion | flops 1223688192 | bytes 19240960 | tf_op jit(solution)/shard_map/reshape | solution.py:156
  372.6 7.8 %scatter_custom_fusion = f32[4097,32]{1,0:T(8,128)} fusion(s32[768]{0:T(1024)S(1)} %reshape.257, f32[768,32]{1,0:T(8,128)S(1)} %bitcast.153, f32[]{:T(128)} %constant.37.clone.1), kind=kCustom, calls=%fused_computation.85 | custom fusion | flops 24576 | bytes 524420 | tf_op jit(solution)/shard_map/scatter-add | solution.py:155
  380.4 3.0 slice.6
  383.4 3.1 reshape.245
  388.0 144.2 %all-reduce.3.cloned.1.call-done = f32[128,1024]{1,0:T(8,128)} async-done(((f32[128,1024]{1,0:T(8,128)}), f32[128,1024]{1,0:T(8,128)}) %all-reduce.3.cloned.1.call-update) | async-done | bytes 524304
  532.2 1.4 dynamic-slice_reduce_fusion.1
  (113 shorter events, 8.9 us)
Async XLA Ops:
  7.2 83.6 %copy-start = (bf16[4096,256]{1,0:T(8,128)(2,1)S(1)}, bf16[4096,256]{1,0:T(8,128)(2,1)}, u32[]{:S(2)}) copy-start(bf16[4096,256]{1,0:T(8,128)(2,1)} %param.20) | copy-start | bytes 6291460
  7.2 73.5 %all-gather.5.cloned.1.call-start = ((), (), s32[]{:S(2)}) async-start(), calls=%async_computation.2 | async-start | bytes 6684672 | tf_op jit(solution)/shard_map/all_gather | solution.py:42
  7.9 111.2 %all-gather.9.cloned.1.call-start = ((), (), s32[]{:S(2)}) async-start(), calls=%async_computation.4 | async-start | bytes 3538944 | tf_op jit(solution)/shard_map/all_gather | solution.py:80
  9.6 87.6 %copy-start.19 = (pred[2,3072]{1,0:T(4,128)(4,1)}, pred[2,3072]{1,0:T(4,128)(4,1)S(1)}, u32[]{:S(2)}) copy-start(pred[2,3072]{1,0:T(4,128)(4,1)S(1)} %fusion.87) | copy-start | bytes 18436
  10.7 0.6 copy-start.20
  80.7 7.4 %copy-start.6 = (bf16[4096,256]{1,0:T(8,128)(2,1)S(1)}, bf16[4096,256]{1,0:T(8,128)(2,1)}, u32[]{:S(2)}) copy-start(bf16[4096,256]{1,0:T(8,128)(2,1)} %param.19) | copy-start | bytes 6291460
  80.7 7.4 %copy-start.17 = (f32[4096]{0:T(1024)S(1)}, f32[4096]{0:T(1024)}, u32[]{:S(2)}) copy-start(f32[4096]{0:T(1024)} %param.16) | copy-start | bytes 49156
  85.4 2.7 copy-start.2
  85.4 11.9 %copy-start.15 = (f32[2,384]{1,0:T(2,128)}, f32[2,384]{1,0:T(2,128)S(1)}, u32[]{:S(2)}) copy-start(f32[2,384]{1,0:T(2,128)S(1)} %add_rsqrt_fusion) | copy-start | bytes 9220
  90.7 5.6 %copy-start.7 = (bf16[2,384,256]{2,1,0:T(8,128)(2,1)S(1)}, bf16[2,384,256]{2,1,0:T(8,128)(2,1)}, u32[]{:S(2)}) copy-start(bf16[2,384,256]{2,1,0:T(8,128)(2,1)} %param.21) | copy-start | bytes 1179652
  90.7 57.9 %all-gather.7.cloned.1.call-start = ((), (), s32[]{:S(2)}) async-start(), calls=%async_computation.3 | async-start | bytes 3538944 | tf_op jit(solution)/shard_map/all_gather | solution.py:81
  96.2 205.7 %reduce-scatter.3.cloned.1.call-start = ((), (), s32[]{:S(2)}) async-start(), calls=%async_computation.5 | async-start | bytes 7077888 | tf_op jit(solution)/shard_map/reduce_scatter | solution.py:134
  178.6 5.3 copy-start.1
  178.6 5.3 copy-start.8
  183.9 1.6 copy-start.3
  185.5 5.0 copy-start.9
  185.6 4.9 copy-start.11
  190.5 1.7 copy-start.4
  190.5 4.4 slice-start
  192.2 3.7 copy-start.12
  192.2 2.7 slice-start.1
  195.9 2.7 copy-start.5
  223.7 5.3 copy-start.1
  223.7 5.3 copy-start.8
  229.0 1.6 copy-start.3
  230.6 5.0 copy-start.9
  230.7 4.9 copy-start.11
  235.6 1.7 copy-start.4
  235.6 4.4 slice-start
  237.3 3.7 copy-start.12
  237.3 2.7 slice-start.1
  241.0 2.7 copy-start.5
  260.2 86.1 %reduce-scatter.5.cloned.1.call-start = ((), (), s32[]{:S(2)}) async-start(), calls=%async_computation.6 | async-start | bytes 7077888 | tf_op jit(solution)/shard_map/reduce_scatter | solution.py:135
  266.9 1.0 copy-start.13
  266.9 265.3 %all-reduce.3.cloned.1.call-start = ((), (), s32[]{:S(2)}) async-start(), calls=%async_computation.7 | async-start | bytes 1048576
  276.3 70.1 %copy-start.16 = (f32[2,384]{1,0:T(2,128)S(1)}, f32[2,384]{1,0:T(2,128)}, u32[]{:S(2)}) copy-start(f32[2,384]{1,0:T(2,128)} %copy-done.15) | copy-start | bytes 9220
  276.3 70.1 %copy-start.18 = (f32[4096]{0:T(1024)S(1)}, f32[4096]{0:T(1024)}, u32[]{:S(2)}) copy-start(f32[4096]{0:T(1024)} %param.16) | copy-start | bytes 49156
  310.1 50.9 %copy-start.14 = (bf16[32,4096]{1,0:T(8,128)(2,1)S(1)}, bf16[32,4096]{1,0:T(8,128)(2,1)}, u32[]{:S(2)}) copy-start(bf16[32,4096]{1,0:T(8,128)(2,1)} %param.17) | copy-start | bytes 786436
  372.6 13.9 %copy-start.21 = (u32[128]{0:T(128)S(1)}, u32[128]{0:T(128)}, u32[]{:S(2)}) copy-start(u32[128]{0:T(128)} %constant.80) | copy-start | bytes 1540
  372.6 14.5 %copy-start.10 = (bf16[2,384,2,128]{1,3,2,0:T(8,128)(2,1)S(1)}, bf16[2,384,2,128]{1,3,2,0:T(8,128)(2,1)}, u32[]{:S(2)}) copy-start(bf16[2,384,2,128]{1,3,2,0:T(8,128)(2,1)} %get-tuple-element.77) | copy-start | bytes 1179652
Sparse Core Ops, SparseCore 0:
  10.1 70.4 all-gather.4
  90.8 28.2 all-gather.8
  120.8 27.7 all-gather.6
  260.4 41.5 reduce-scatter.2
  304.2 42.1 reduce-scatter.4
  386.6 145.5 all-reduce.2
where the time goes:
time: 546 us; the launch traced here: 541 us
  waiting for transfers between devices  274 us (50%)
  matrix products  97.5 us (18%)
  other arithmetic  54.2 us (10%)
  local copies, waits for them, and re-layouts  50.8 us (9%)
  blocking collectives  39.6 us (7%)
  between operations  14.5 us (3%)
  loops' own time  10.5 us (2%)
    unnamed x7, waiting for transfers between devices  145 us
    all_gather x1, blocking collectives, on_device(): lax.all_gather(latents.reshape(latents.shape[0] * latents.shape[1], laten...  39.6 us
    reduce_scatter x1, waiting for transfers between devices, on_device(): lax.psum_scatter(part_values, 'seq', scatter_dimension=1, tiled=True)  36.2 us
    dot_general x3, matrix products, project_back(): jnp.einsum('src,dc->srd', flat_grad, weight, preferred_element_type=jnp.f...  31.3 us
    sub x2, other arithmetic, attend(): lifted = jnp.exp(masked - row_max)  29 us
    all_gather x1, waiting for transfers between devices, on_device(): gathered = lax.all_gather(text_rows, 'dp', axis=2, tiled=True)  27.7 us
    reduce_scatter x1, waiting for transfers between devices, on_device(): lax.psum_scatter(part_keys, 'seq', scatter_dimension=1, tiled=True)  25.6 us
    all_gather x1, waiting for transfers between devices, on_device(): lax.all_gather(value_rows, 'seq', axis=1, tiled=True)  24 us
  transfers between devices with their start and end apart: 6, of which 6 were waited for; matrix products, arithmetic and copies ran while one was open for 9% of the time, Pallas kernels for 0%

commit v1 on v0

v1 whole, which is shorter than its diff:
```python
import math

import jax
import jax.numpy as jnp
from jax import lax
from jax.experimental import pallas as pl
from jax.experimental.pallas import tpu as pltpu
from jax.sharding import PartitionSpec as P

HD = 128
PATCHES = 256
PDIM = 32
BLOCK = 384
TEXT = BLOCK - PATCHES
IMAGES = 16
NSEQ = 2
D = 4096
epsilon = 1e-05
SCALE = HD ** (-0.5)
LN2 = math.log(2.0)
BF = jnp.bfloat16
F32 = jnp.float32
SEND_ROWS = NSEQ * TEXT + 16
KV_ROWS = NSEQ * TEXT + 32


def dot_nn(a, b):
    return lax.dot_general(a, b, (((1,), (0,)), ((), ())), preferred_element_type=F32)


def dot_nt(a, b):
    return lax.dot_general(a, b, (((1,), (1,)), ((), ())), preferred_element_type=F32)


def lane_place(a):
    rows = lax.broadcasted_iota(jnp.int32, (PDIM, 128), 0)
    lanes = lax.broadcasted_iota(jnp.int32, (PDIM, 128), 1)
    return jnp.where(lanes == rows + PDIM * a, 1.0, 0.0).astype(BF)


def own_offsets(seq_ref, start_ref, seat):
    offs = [jnp.int32(0), jnp.int32(0)]
    for i in range(IMAGES):
        rel = start_ref[i] - seat * BLOCK
        mine = (rel >= 0) & (rel < BLOCK)
        for g in range(NSEQ):
            offs[g] = jnp.where(mine & (seq_ref[i] == g), rel, offs[g])
    return offs


def pack_kernel(seq_ref, start_ref, seat_ref, text_ref, lat_ref, wp_ref, send_ref, inv_ref, u_ref):
    offs = own_offsets(seq_ref, start_ref, seat_ref[0])
    lat = lat_ref[...]
    wp = wp_ref[...]
    embedded = dot_nn(lat, wp).astype(BF)
    emb_f = embedded.astype(F32)
    inv = lax.rsqrt(jnp.sum(emb_f * emb_f, axis=1, keepdims=True) * (1.0 / D) + epsilon)
    inv_ref[...] = jnp.broadcast_to(inv, inv_ref.shape)
    u_ref[...] = dot_nt(embedded, wp)
    scaled = (lat.astype(F32) * inv).astype(BF)
    rows8 = lax.broadcasted_iota(jnp.int32, (8, PDIM), 0)
    cols8 = lax.broadcasted_iota(jnp.int32, (8, PDIM), 1)
    packed = jnp.zeros((8, 128), F32)
    for a in range(4):
        pick = jnp.where(cols8 == rows8 + 8 * a, 1.0, 0.0).astype(BF)
        part = dot_nn(pick, scaled).astype(BF)
        packed = packed + dot_nn(part, lane_place(a))
    tail = jnp.concatenate([packed, jnp.zeros((8, 128), F32)], axis=0)
    tail = jnp.concatenate([tail, jnp.zeros((16, 128), F32)], axis=1).astype(BF)
    row = lax.broadcasted_iota(jnp.int32, (TEXT, 256), 0)
    texts = []
    for g in range(NSEQ):
        low = text_ref[g, 0:TEXT, :].astype(F32)
        high = text_ref[g, PATCHES:BLOCK, :].astype(F32)
        texts.append(jnp.where(row < offs[g], low, high).astype(BF))
    for d in range(send_ref.shape[0]):
        for g in range(NSEQ):
            send_ref[d, g * TEXT : (g + 1) * TEXT, :] = texts[g]
        send_ref[d, NSEQ * TEXT :, :] = tail


FEATURE_STEP = 2


def project_kernel(x_ref, wq_ref, wk_ref, wv_ref, wp_ref, gain_ref, qt_ref, kv_ref, mt_ref, acc, ssq):
    step = pl.program_id(0)
    rows = NSEQ * TEXT
    lhs = []
    total = jnp.zeros((rows, 128), F32)
    for j in range(FEATURE_STEP):
        gain = gain_ref[:, 256 * j : 256 * (j + 1)]
        x = x_ref[j, 0:rows, :].astype(F32)
        squares = x * x
        total = total + squares[:, :128] + squares[:, 128:]
        text = (x * gain).astype(BF)
        patch = (wp_ref[:, 256 * j : 256 * (j + 1)].astype(F32) * gain).astype(BF)
        lhs.append(jnp.concatenate([text, patch], axis=0))
    left = jnp.concatenate(lhs, axis=1)

    @pl.when(step == 0)
    def _():
        acc[...] = jnp.zeros_like(acc)
        ssq[...] = jnp.zeros_like(ssq)

    ssq[...] += total
    for n, w_ref in enumerate((wq_ref, wk_ref, wv_ref)):
        acc[:, 256 * n : 256 * (n + 1)] += dot_nn(left, w_ref[...])

    @pl.when(step == pl.num_programs(0) - 1)
    def _():
        inv = lax.rsqrt(jnp.sum(ssq[...], axis=1, keepdims=True) * (1.0 / D) + epsilon)
        qt_ref[...] = (acc[0:rows, 0:256] * (inv * (SCALE / LN2))).astype(BF)
        kv_ref[0:rows, :] = (acc[0:rows, 256:768] * inv).astype(BF)
        mt_ref[...] = acc[rows:, :].astype(BF)


def lat_tiles(recv):
    tiles = recv[:, NSEQ * TEXT : NSEQ * TEXT + 8, 0:128]
    tiles = tiles.reshape(4, 4, 8, 128).transpose(0, 2, 1, 3)
    return tiles.reshape(32, 512)


def fold_max(s):
    return jnp.maximum(jnp.maximum(s[:, 0:128], s[:, 128:256]), s[:, 256:384])


def fold_sum(s):
    return s[:, 0:128] + s[:, 128:256] + s[:, 256:384]


def position(index, offset):
    patch = 32 * ((index & 63) >> 3) + 8 * (index >> 6) + (index & 7)
    t = index - PATCHES
    return jnp.where(
        index < PATCHES, offset + patch, jnp.where(t < offset, t, t + PATCHES)
    )


def attend_kernel(
    seq_ref, start_ref, seat_ref, cg_ref, qt_ref, mt_ref, grad_ref,
    out_ref, z_ref,
    labels, tiles, wide, keys, values, scores, probs, q_s, g_s, o_s, m_s, l_s, zt, zq,
):
    seat = seat_ref[0]
    offs = own_offsets(seq_ref, start_ref, seat)
    for i in range(IMAGES):
        labels[seq_ref[i] * 8 + lax.div(start_ref[i], BLOCK)] = i

    wide[...] = jnp.zeros_like(wide)
    for a in range(4):
        wide[128 * a + PDIM * a : 128 * a + PDIM * (a + 1), :] = mt_ref[...]
    for j in range(8):
        part = cg_ref[j, NSEQ * TEXT :, :].astype(F32)
        for i in range(IMAGES):
            tiles[i, 8 * j : 8 * (j + 1), :] = part[
                8 * (i // 4) : 8 * (i // 4 + 1), 128 * (i % 4) : 128 * (i % 4 + 1)
            ]
    zt[...] = jnp.zeros_like(zt)

    rows = lax.broadcasted_iota(jnp.int32, (BLOCK, BLOCK), 0)
    cols = lax.broadcasted_iota(jnp.int32, (BLOCK, BLOCK), 1)

    def heads(h):
        return slice(h * HD, (h + 1) * HD)

    for g in range(NSEQ):
        off = offs[g]
        own = labels[g * 8 + seat]
        own_tile = tiles[own].astype(BF)
        for a in range(4):
            q_s[64 * a : 64 * (a + 1), :] = (
                dot_nn(own_tile, wide[128 * a : 128 * (a + 1), 0:256]) * (SCALE / LN2)
            ).astype(BF)
        q_s[PATCHES:, :] = qt_ref[g * TEXT : (g + 1) * TEXT, :]
        place = jnp.where(cols == position(rows, off), 1.0, 0.0).astype(BF)
        g_s[...] = dot_nn(place, grad_ref[g]).astype(BF)

        def score_block(b, diagonal):
            label = labels[g * 8 + b]
            tile = tiles[label].astype(BF)
            for a in range(4):
                kv = dot_nn(tile, wide[128 * a : 128 * (a + 1), 256:768]).astype(BF)
                keys[b, 64 * a : 64 * (a + 1), :] = kv[:, 0:256]
                values[b, 64 * a : 64 * (a + 1), :] = kv[:, 256:512]
            keys[b, PATCHES:, :] = cg_ref[b, g * TEXT : (g + 1) * TEXT, 0:256]
            values[b, PATCHES:, :] = cg_ref[b, g * TEXT : (g + 1) * TEXT, 256:512]
            for h in range(2):
                s = dot_nt(q_s[:, heads(h)], keys[b, :, heads(h)])
                if diagonal:
                    reach = jnp.where(rows < PATCHES, off + (PATCHES - 1), position(rows, off))
                    s = jnp.where(position(cols, off) <= reach, s, -jnp.inf)
                    m_s[h] = fold_max(s)
                else:
                    m_s[h] = jnp.maximum(m_s[h], fold_max(s))
                scores[h, b] = s

        score_block(seat, True)

        def score_body(b, carry):
            score_block(b, False)
            return carry

        lax.fori_loop(0, seat, score_body, 0)

        o_s[...] = jnp.zeros_like(o_s)
        l_s[...] = jnp.zeros_like(l_s)
        tops = [jnp.max(m_s[h], axis=1, keepdims=True) for h in range(2)]
        for h in range(2):
            m_s[h] = jnp.broadcast_to(tops[h], (BLOCK, 128))

        def prob_body(b, carry):
            for h in range(2):
                top = m_s[h]
                p = jnp.exp2(scores[h, b] - jnp.concatenate([top, top, top], axis=1))
                l_s[h] += fold_sum(p)
                p = p.astype(BF)
                probs[h, b] = p
                o_s[h] += dot_nn(p, values[b, :, heads(h)])
            return carry

        lax.fori_loop(0, seat + 1, prob_body, 0)

        outs = []
        xk = []
        xv = []
        for h in range(2):
            inv = 1.0 / jnp.sum(l_s[h], axis=1, keepdims=True)
            out = o_s[h] * inv
            outs.append(out.astype(BF))
            scaled = (g_s[:, heads(h)].astype(F32) * inv).astype(BF)
            delta = jnp.sum(scaled.astype(F32) * out, axis=1, keepdims=True)
            m_s[h] = jnp.broadcast_to(delta, (BLOCK, 128))
            g_s[:, heads(h)] = scaled
            mk = mt_ref[:, 256 + h * HD : 256 + (h + 1) * HD]
            mv = mt_ref[:, 512 + h * HD : 512 + (h + 1) * HD]
            xk.append((dot_nt(mk, q_s[:, heads(h)]) * LN2).astype(BF))
            xv.append(dot_nt(mv, scaled).astype(BF))
        out_c = jnp.concatenate(outs, axis=1)
        back = jnp.where(rows == position(cols, off), 1.0, 0.0).astype(BF)
        out_ref[g] = dot_nn(back, out_c).astype(BF)
        zq[...] = jnp.zeros_like(zq)

        def grad_body(b, carry):
            label = labels[g * 8 + b]
            total = zt[label]
            for h in range(2):
                delta = m_s[h]
                wide_delta = jnp.concatenate([delta, delta, delta], axis=1)
                value = values[b, :, heads(h)]
                dp = dot_nt(g_s[0:PATCHES, heads(h)], value)
                ds = (probs[h, b, 0:PATCHES, :].astype(F32) * (dp - wide_delta[0:PATCHES])).astype(BF)
                dp_text = dot_nt(g_s[PATCHES:, heads(h)], value[0:PATCHES])
                ds_text = (
                    probs[h, b, PATCHES:, 0:PATCHES].astype(F32)
                    * (dp_text - wide_delta[PATCHES:, 0:PATCHES])
                ).astype(BF)
                mq = mt_ref[:, heads(h)]
                km = (dot_nt(keys[b, :, heads(h)], mq) * SCALE).astype(BF)
                zq[...] += dot_nn(ds, km)
                total = total + dot_nn(xk[h][:, 0:PATCHES], ds[:, 0:PATCHES])
                total = total + dot_nn(xk[h][:, PATCHES:], ds_text)
                total = total + dot_nn(xv[h], probs[h, b, :, 0:PATCHES])
            zt[label] = total
            return carry

        lax.fori_loop(0, seat + 1, grad_body, 0)
        zt[own] += zq[...].T

    for i in range(IMAGES):
        flat = zt[i].T.astype(BF)
        dense = jnp.zeros((64, 128), F32)
        for a in range(4):
            dense = dense + dot_nn(flat[64 * a : 64 * (a + 1)], lane_place(a))
        z_ref[i] = dense.astype(BF)


def finish_kernel(recv_ref, lat_ref, inv_ref, u_ref, out_ref):
    total = jnp.sum(recv_ref[...].astype(F32), axis=0)
    for a in range(4):
        at = slice(8 * a, 8 * (a + 1))
        z = total[:, PDIM * a : PDIM * (a + 1)]
        inv = inv_ref[at, :][:, 0:1]
        inner = jnp.sum(lat_ref[at, :] * z, axis=1, keepdims=True)
        out_ref[at, :] = inv * (z - u_ref[at, :] * (inv * inv * inner * (1.0 / D)))


def gather_by_exchange(block, axis, copies):
    return lax.all_to_all(jnp.broadcast_to(block[None], (copies,) + block.shape), axis, 0, 0)


def on_device(
    text_rows, latents, image_seq, image_start, norm_gain, w_patch, w_query, w_key, w_value, out_grad
):
    seats = lax.axis_size("seq")
    groups = lax.axis_size("dp")
    seat = lax.axis_index("seq").astype(jnp.int32).reshape(1)
    lat = latents.reshape(PDIM, PDIM)
    smem = pl.BlockSpec(memory_space=pltpu.SMEM)
    vmem = pl.BlockSpec(memory_space=pltpu.VMEM)
    send, inv, u = pl.pallas_call(
        pack_kernel,
        out_shape=(
            jax.ShapeDtypeStruct((groups, SEND_ROWS, 256), BF),
            jax.ShapeDtypeStruct((PDIM, 128), F32),
            jax.ShapeDtypeStruct((PDIM, PDIM), F32),
        ),
        in_specs=[smem] * 3 + [vmem] * 3,
        out_specs=(vmem,) * 3,
        compiler_params=pltpu.CompilerParams(vmem_limit_bytes=32 * 2**20),
        name="pack",
    )(image_seq, image_start, seat, text_rows, lat, w_patch)
    recv = lax.all_to_all(send, "dp", 0, 0)

    steps = groups // FEATURE_STEP
    width = 256 * FEATURE_STEP
    weight_spec = pl.BlockSpec((width, 256), lambda d: (d, 0))
    qt, kv, mt = pl.pallas_call(
        project_kernel,
        grid=(steps,),
        out_shape=(
            jax.ShapeDtypeStruct((NSEQ * TEXT, 256), BF),
            jax.ShapeDtypeStruct((NSEQ * TEXT, 512), BF),
            jax.ShapeDtypeStruct((PDIM, 768), BF),
        ),
        in_specs=[
            pl.BlockSpec((FEATURE_STEP, SEND_ROWS, 256), lambda d: (d, 0, 0)),
            weight_spec,
            weight_spec,
            weight_spec,
            pl.BlockSpec((PDIM, width), lambda d: (0, d)),
            pl.BlockSpec((1, width), lambda d: (0, d)),
        ],
        out_specs=(
            pl.BlockSpec((NSEQ * TEXT, 256), lambda d: (0, 0)),
            pl.BlockSpec((NSEQ * TEXT, 512), lambda d: (0, 0)),
            pl.BlockSpec((PDIM, 768), lambda d: (0, 0)),
        ),
        scratch_shapes=[
            pltpu.VMEM((NSEQ * TEXT + PDIM, 768), F32),
            pltpu.VMEM((NSEQ * TEXT, 128), F32),
        ],
        compiler_params=pltpu.CompilerParams(vmem_limit_bytes=32 * 2**20),
        name="project",
    )(recv, w_query, w_key, w_value, w_patch, norm_gain.reshape(1, D))
    gathered = gather_by_exchange(jnp.concatenate([kv, lat_tiles(recv)], axis=0), "seq", seats)

    attended, z = pl.pallas_call(
        attend_kernel,
        out_shape=(
            jax.ShapeDtypeStruct((NSEQ, BLOCK, 256), BF),
            jax.ShapeDtypeStruct((IMAGES, 64, 128), BF),
        ),
        in_specs=[smem] * 3 + [vmem] * 4,
        out_specs=(vmem,) * 2,
        scratch_shapes=[
            pltpu.SMEM((IMAGES,), jnp.int32),
            pltpu.VMEM((IMAGES, 64, 128), F32),
            pltpu.VMEM((512, 768), BF),
            pltpu.VMEM((8, BLOCK, 256), BF),
            pltpu.VMEM((8, BLOCK, 256), BF),
            pltpu.VMEM((2, 8, BLOCK, BLOCK), F32),
            pltpu.VMEM((2, 8, BLOCK, BLOCK), BF),
            pltpu.VMEM((BLOCK, 256), BF),
            pltpu.VMEM((BLOCK, 256), BF),
            pltpu.VMEM((2, BLOCK, HD), F32),
            pltpu.VMEM((2, BLOCK, 128), F32),
            pltpu.VMEM((2, BLOCK, 128), F32),
            pltpu.VMEM((IMAGES, PDIM, PATCHES), F32),
            pltpu.VMEM((PATCHES, PDIM), F32),
        ],
        compiler_params=pltpu.CompilerParams(vmem_limit_bytes=48 * 2**20),
        name="attend",
    )(image_seq, image_start, seat, gathered, qt, mt, out_grad)

    parts = lax.all_to_all(z.reshape(groups * seats, 8, 128), ("dp", "seq"), 0, 0)
    grad = pl.pallas_call(
        finish_kernel,
        out_shape=jax.ShapeDtypeStruct((PDIM, PDIM), F32),
        in_specs=[vmem] * 4,
        out_specs=vmem,
        compiler_params=pltpu.CompilerParams(vmem_limit_bytes=32 * 2**20),
        name="finish",
    )(parts, lat.astype(F32), inv, u)
    return (attended, grad.reshape(latents.shape))


def solution(mesh):
    in_specs = (
        P(None, "seq", "dp"),
        P("dp", "seq", None),
        P(),
        P(),
        P(),
        P(),
        P(None, "dp"),
        P(None, "dp"),
        P(None, "dp"),
        P(None, "seq", "dp"),
    )
    out_specs = (P(None, "seq", "dp"), P("dp", "seq", None))
    return jax.shard_map(
        on_device, mesh=mesh, in_specs=in_specs, out_specs=out_specs, check_vma=False
    )
```

time: 546 us -> 133 us (0.24)
  waiting for transfers between devices: 274 us -> 11.1 us
  matrix products: 97.5 us -> 0 us
  other arithmetic: 54.2 us -> 0.03 us
  local copies, waits for them, and re-layouts: 50.8 us -> 5.78 us
  blocking collectives: 39.6 us -> 73 us
  starting transfers between devices: 0.24 us -> 24.2 us
  Pallas kernels: 0 us -> 17.4 us
  between operations: 14.5 us -> 0.8 us
  loops' own time: 10.5 us -> 0 us
    unnamed x7 -> x0, waiting for transfers between devices: 145 us -> none
    dot_general x19 -> x0, matrix products: 86 us -> none  [the longest x3 31.3 us: project_back(): jnp.einsum('src,dc->srd', flat_grad, weight, preferred_element_type=jnp.f...]
    all_to_all x0 -> x2, blocking collectives: none -> 73 us  [the longest x1 37.3 us: on_device(): recv = lax.all_to_all(send, 'dp', 0, 0)]
    all_gather x3 -> x0, waiting for transfers between devices: 67.1 us -> none  [the longest x1 27.7 us: on_device(): gathered = lax.all_gather(text_rows, 'dp', axis=2, tiled=True)]
    reduce_scatter x2 -> x0, waiting for transfers between devices: 61.9 us -> none  [the longest x1 36.2 us: on_device(): lax.psum_scatter(part_values, 'seq', scatter_dimension=1, tiled=True)]
    all_gather x1 -> x0, blocking collectives: 39.6 us -> none  [on_device(): lax.all_gather(latents.reshape(latents.shape[0] * latents.shape[1], laten...]
    sub x2 -> x0, other arithmetic: 29 us -> none  [attend(): lifted = jnp.exp(masked - row_max)]
    all_to_all x0 -> x1, starting transfers between devices: none -> 24.2 us  [on_device(): lax.all_to_all(z.reshape(groups * seats, 8, 128), ('dp', 'seq'), 0, 0)]
  transfers between devices with their start and end apart: 6 -> 1, of which waited for: 6 -> 1; matrix products, arithmetic and copies ran while one was open for 9% -> 0% of each run, Pallas kernels for 0% -> 0%
where the time goes in v1:
time: 133 us; the launch traced here: 132 us
  blocking collectives  73 us (55%)
  starting transfers between devices  24.2 us (18%)
  Pallas kernels  17.4 us (13%)
  waiting for transfers between devices  11.1 us (8%)
  local copies, waits for them, and re-layouts  5.78 us (4%)
    all_to_all x1, blocking collectives, on_device(): recv = lax.all_to_all(send, 'dp', 0, 0)  37.3 us
    all_to_all x1, blocking collectives, gather_by_exchange(): lax.all_to_all(jnp.broadcast_to(block[None], (copies,) + block.shape), ax...  35.6 us
    all_to_all x1, starting transfers between devices, on_device(): lax.all_to_all(z.reshape(groups * seats, 8, 128), ('dp', 'seq'), 0, 0)  24.2 us
    all_to_all x1, waiting for transfers between devices, on_device(): lax.all_to_all(z.reshape(groups * seats, 8, 128), ('dp', 'seq'), 0, 0)  11.1 us
    pallas_call x1, Pallas kernels, on_device(): pl.pallas_call(attend_kernel, out_shape=(jax.ShapeDtypeStruct((NSEQ, BLOC...  10.5 us
    unnamed x28, local copies, waits for them, and re-layouts  5.58 us
    pallas_call x1, Pallas kernels, on_device(): pl.pallas_call(project_kernel, grid=(steps,), out_shape=(jax.ShapeDtypeSt...  4.49 us
  transfers between devices with their start and end apart: 1, of which 1 were waited for; matrix products, arithmetic and copies ran while one was open for 0% of the time, Pallas kernels for 0%

profile of v1, /device:TPU:1, one launch (start us, length us, event | category | flops | bytes accessed | tf_op | source)
XLA Modules:
  0.0 132.3 jit_solution(4664367964162897692)
XLA Ops:
  0.6 0.0 copy-start.3
  0.6 0.9 copy-done.3
  1.6 0.0 copy-start.5
  1.6 1.0 copy-done.5
  2.6 0.0 copy-start.7
  2.6 0.7 copy-done.7
  3.3 0.0 copy-start.10
  3.3 0.7 copy-done.10
  3.9 0.0 copy-start.12
  3.9 0.7 copy-done.12
  4.6 1.4 %pack.1 = (bf16[16,272,256]{2,1,0:T(8,128)(2,1)S(1)}, f32[32,128]{1,0:T(8,128)S(1)}, f32[32,32]{1,0:T(8,128)S(1)}) custom-call(s32[16]{0:T(128)S(1)} %copy-done.10, s32[16]{0:T(128)S(1)} %copy-done.12, s32[1]{0:T(128)} %bitcast.seat_ref, bf16[2,384,256]{2,1,0:T(8,128)(2,1)S(1)} %copy-done.5, bf16[32,32]{1,0:T(8,128)(2,1)S(1)} %bitcast.11, ...), custom_call_target="tpu_custom_call" | custom-call | tf_op jit(solution)/shard_map/pack/pallas_call | solution.py:300
  6.0 0.0 copy-start
  6.0 0.0 copy-start.1
  6.0 0.0 copy-start.4
  6.0 0.0 copy-start.9
  6.0 37.3 %all_to_all.15.x_ref = bf16[16,272,256]{2,1,0:T(8,128)(2,1)S(1)} all-to-all(bf16[16,272,256]{2,1,0:T(8,128)(2,1)S(1)} %get-tuple-element.10), channel_id=1, replica_groups=mesh['seq'=8,'dp'=16] {'dp'}, dimensions={0} | all-to-all | bytes 4456448 | tf_op jit(solution)/shard_map/all_to_all | solution.py:312
  43.4 0.0 copy-done
  43.4 0.0 copy-done.1
  43.4 0.0 copy-done.4
  43.4 0.0 copy-done.9
  43.4 0.0 copy-start.2
  43.4 1.6 %copy-done.2 = bf16[4096,256]{1,0:T(8,128)(2,1)S(1)} copy-done((bf16[4096,256]{1,0:T(8,128)(2,1)S(1)}, bf16[4096,256]{1,0:T(8,128)(2,1)}, u32[]{:S(2)}) %copy-start.2) | copy-done | bytes 2097176
  45.0 4.5 %project.1 = (bf16[256,256]{1,0:T(8,128)(2,1)S(1)}, bf16[256,512]{1,0:T(8,128)(2,1)S(1)}, bf16[32,768]{1,0:T(8,128)(2,1)S(1)}) custom-call(bf16[16,272,256]{2,1,0:T(8,128)(2,1)S(1)} %all_to_all.15.x_ref, bf16[4096,256]{1,0:T(8,128)(2,1)S(1)} %copy-done, bf16[4096,256]{1,0:T(8,128)(2,1)S(1)} %copy-done.1, bf16[4096,256]{1,0:T(8,128)(2,1)S(1)} %copy-done.2, ...), custom_call_target="tpu_custom_call" | custom-call | tf_op jit(solution)/shard_map/project/pallas_call | solution.py:317
  49.5 0.2 broadcast_in_dim.2
  49.7 0.0 copy-start.6
  49.7 0.0 copy-start.11
  49.7 0.0 copy-start.13
  49.8 35.6 %all_to_all.16.cg_ref = bf16[8,288,512]{2,1,0:T(8,128)(2,1)S(1)} all-to-all(bf16[8,288,512]{2,1,0:T(8,128)(2,1)S(1)} %broadcast_in_dim.2), channel_id=1, replica_groups=mesh['seq'=8,'dp'=16] {'seq'}, dimensions={0} | all-to-all | bytes 4718592 | tf_op jit(solution)/shard_map/all_to_all | solution.py:288
  85.4 0.0 copy-start.8
  85.4 0.0 copy-done.6
  85.4 0.0 copy-done.11
  85.4 0.0 copy-done.13
  85.4 10.5 %attend.1 = (bf16[2,384,256]{2,1,0:T(8,128)(2,1)}, bf16[16,64,128]{2,1,0:T(8,128)(2,1)}) custom-call(s32[16]{0:T(128)S(1)} %copy-done.11, s32[16]{0:T(128)S(1)} %copy-done.13, s32[1]{0:T(128)} %bitcast.seat_ref, bf16[8,288,512]{2,1,0:T(8,128)(2,1)S(1)} %all_to_all.16.cg_ref, bf16[256,256]{1,0:T(8,128)(2,1)S(1)} %get-tuple-element.12.qt_ref, ...), custom_call_target="tpu_custom_call" | custom-call | tf_op jit(solution)/shard_map/attend/pallas_call | solution.py:347
  95.9 24.2 %all-to-all-start.2 = ((bf16[128,8,128]{2,1,0:T(8,128)(2,1)}), bf16[128,8,128]{2,1,0:T(8,128)(2,1)S(1)}, u32[]{:S(2)}, u32[]{:S(2)}) async-start(bf16[128,8,128]{2,1,0:T(8,128)(2,1)} %bitcast.6), calls=%async_computation.2 | async-start | bytes 524288 | tf_op jit(solution)/shard_map/all_to_all | solution.py:375
  120.1 0.0 copy-done.8
  120.1 11.1 %all-to-all-done.2.recv_ref = bf16[128,8,128]{2,1,0:T(8,128)(2,1)S(1)} async-done(((bf16[128,8,128]{2,1,0:T(8,128)(2,1)}), bf16[128,8,128]{2,1,0:T(8,128)(2,1)S(1)}, u32[]{:S(2)}, u32[]{:S(2)}) %all-to-all-start.2) | async-done | bytes 262176 | tf_op jit(solution)/shard_map/all_to_all | solution.py:375
  131.2 1.1 finish.1
  (3 shorter events, 0.0 us)
Async XLA Ops:
  0.6 1.0 copy-start.3
  1.6 1.0 copy-start.5
  2.6 0.7 copy-start.7
  3.3 0.7 copy-start.10
  3.9 0.7 copy-start.12
  6.0 37.4 %copy-start = (bf16[4096,256]{1,0:T(8,128)(2,1)S(1)}, bf16[4096,256]{1,0:T(8,128)(2,1)}, u32[]{:S(2)}) copy-start(bf16[4096,256]{1,0:T(8,128)(2,1)} %wq_ref.1) | copy-start | bytes 6291460
  6.0 37.4 %copy-start.1 = (bf16[4096,256]{1,0:T(8,128)(2,1)S(1)}, bf16[4096,256]{1,0:T(8,128)(2,1)}, u32[]{:S(2)}) copy-start(bf16[4096,256]{1,0:T(8,128)(2,1)} %wk_ref.1) | copy-start | bytes 6291460
  6.0 37.4 %copy-start.4 = (bf16[32,4096]{1,0:T(8,128)(2,1)S(1)}, bf16[32,4096]{1,0:T(8,128)(2,1)}, u32[]{:S(2)}) copy-start(bf16[32,4096]{1,0:T(8,128)(2,1)} %wp_ref.3) | copy-start | bytes 786436
  6.0 37.4 %copy-start.9 = (f32[4096]{0:T(1024)S(1)}, f32[4096]{0:T(1024)}, u32[]{:S(2)}) copy-start(f32[4096]{0:T(1024)} %param.14) | copy-start | bytes 49156
  43.4 1.6 %copy-start.2 = (bf16[4096,256]{1,0:T(8,128)(2,1)S(1)}, bf16[4096,256]{1,0:T(8,128)(2,1)}, u32[]{:S(2)}) copy-start(bf16[4096,256]{1,0:T(8,128)(2,1)} %wv_ref.1) | copy-start | bytes 6291460
  49.7 35.7 %copy-start.6 = (bf16[2,384,256]{2,1,0:T(8,128)(2,1)S(1)}, bf16[2,384,256]{2,1,0:T(8,128)(2,1)}, u32[]{:S(2)}) copy-start(bf16[2,384,256]{2,1,0:T(8,128)(2,1)} %grad_ref.1) | copy-start | bytes 1179652
  49.7 35.7 %copy-start.11 = (s32[16]{0:T(128)S(1)}, s32[16]{0:T(128)}, u32[]{:S(2)}) copy-start(s32[16]{0:T(128)} %seq_ref.3) | copy-start | bytes 196
  49.7 35.7 %copy-start.13 = (s32[16]{0:T(128)S(1)}, s32[16]{0:T(128)}, u32[]{:S(2)}) copy-start(s32[16]{0:T(128)} %start_ref.3) | copy-start | bytes 196
  85.4 34.7 %copy-start.8 = (bf16[1,32,32]{2,1,0:T(8,128)(2,1)S(1)}, bf16[1,32,32]{2,1,0:T(8,128)(2,1)}, u32[]{:S(2)}) copy-start(bf16[1,32,32]{2,1,0:T(8,128)(2,1)} %param.11) | copy-start | bytes 6148
  95.9 35.3 %all-to-all-start.2 = ((bf16[128,8,128]{2,1,0:T(8,128)(2,1)}), bf16[128,8,128]{2,1,0:T(8,128)(2,1)S(1)}, u32[]{:S(2)}, u32[]{:S(2)}) async-start(bf16[128,8,128]{2,1,0:T(8,128)(2,1)} %bitcast.6), calls=%async_computation.2 | async-start | bytes 524288 | tf_op jit(solution)/shard_map/all_to_all | solution.py:375

commit v2 on v1

v2 whole, which is shorter than its diff:
```python
import functools
import math

import jax
import jax.numpy as jnp
from jax import lax
from jax.experimental import pallas as pl
from jax.experimental.pallas import tpu as pltpu
from jax.sharding import PartitionSpec as P

HD = 128
PATCHES = 256
PDIM = 32
BLOCK = 384
TEXT = BLOCK - PATCHES
IMAGES = 16
NSEQ = 2
D = 4096
epsilon = 1e-05
SCALE = HD ** (-0.5)
LN2 = math.log(2.0)
BF = jnp.bfloat16
F32 = jnp.float32
SEND_ROWS = NSEQ * TEXT + 16
KV_ROWS = NSEQ * TEXT + 32


def dot_nn(a, b):
    return lax.dot_general(a, b, (((1,), (0,)), ((), ())), preferred_element_type=F32)


def dot_nt(a, b):
    return lax.dot_general(a, b, (((1,), (1,)), ((), ())), preferred_element_type=F32)


def own_offsets(seq_ref, start_ref, seat):
    offs = [jnp.int32(0), jnp.int32(0)]
    for i in range(IMAGES):
        rel = start_ref[i] - seat * BLOCK
        mine = (rel >= 0) & (rel < BLOCK)
        for g in range(NSEQ):
            offs[g] = jnp.where(mine & (seq_ref[i] == g), rel, offs[g])
    return offs


def pack_kernel(
    seq_hbm, start_hbm, seat_ref, text_hbm, lat_hbm, wp_hbm,
    send_ref, inv_ref, u_ref,
    seq_ref, start_ref, text_ref, lat_ref, wp_ref, sems,
):
    pairs = (
        (seq_hbm, seq_ref), (start_hbm, start_ref), (lat_hbm, lat_ref), (wp_hbm, wp_ref),
        (text_hbm, text_ref),
    )
    copies = [pltpu.make_async_copy(a, b, sems.at[n]) for n, (a, b) in enumerate(pairs)]
    for copy in copies:
        copy.start()
    copies[2].wait()
    copies[3].wait()
    lat = lat_ref[...]
    wp = wp_ref[...]
    embedded = dot_nn(lat, wp).astype(BF)
    emb_f = embedded.astype(F32)
    inv = lax.rsqrt(jnp.sum(emb_f * emb_f, axis=1, keepdims=True) * (1.0 / D) + epsilon)
    inv_ref[...] = jnp.broadcast_to(inv, inv_ref.shape)
    u_ref[...] = dot_nt(embedded, wp)
    scaled = lat.astype(F32) * inv
    packed = jnp.concatenate([scaled[8 * a : 8 * (a + 1)] for a in range(4)], axis=1)
    tail = jnp.concatenate([packed, jnp.zeros((8, 128), F32)], axis=0)
    tail = jnp.concatenate([tail, jnp.zeros((16, 128), F32)], axis=1).astype(BF)
    copies[0].wait()
    copies[1].wait()
    offs = own_offsets(seq_ref, start_ref, seat_ref[0])
    copies[4].wait()
    row = lax.broadcasted_iota(jnp.int32, (TEXT, 256), 0)
    texts = []
    for g in range(NSEQ):
        low = text_ref[g, 0:TEXT, :].astype(F32)
        high = text_ref[g, PATCHES:BLOCK, :].astype(F32)
        texts.append(jnp.where(row < offs[g], low, high).astype(BF))
    for d in range(send_ref.shape[0]):
        for g in range(NSEQ):
            send_ref[d, g * TEXT : (g + 1) * TEXT, :] = texts[g]
        send_ref[d, NSEQ * TEXT :, :] = tail


def project_kernel(
    x_ref, wq_ref, wk_ref, wv_hbm, wp_ref, gain_ref, qt_ref, block_ref, mt_ref, left, wv_ref, sem
):
    copy = pltpu.make_async_copy(wv_hbm, wv_ref, sem)
    copy.start()
    rows = NSEQ * TEXT
    ssq = jnp.zeros((rows, 128), F32)
    tiles = []
    for d in range(x_ref.shape[0]):
        at = slice(256 * d, 256 * (d + 1))
        gain = gain_ref[:, at]
        x = x_ref[d, 0:rows, :].astype(F32)
        squares = x * x
        ssq = ssq + squares[:, :128] + squares[:, 128:]
        left[0:rows, at] = (x * gain).astype(BF)
        left[rows:, at] = (wp_ref[:, at].astype(F32) * gain).astype(BF)
        tiles.append(x_ref[d, rows : rows + 16, 0:128].astype(F32)[0:8])
    inv = lax.rsqrt(jnp.sum(ssq, axis=1, keepdims=True) * (1.0 / D) + epsilon)
    lat = [jnp.concatenate(tiles[4 * n : 4 * (n + 1)], axis=1) for n in range(4)]
    block_ref[rows:, :] = jnp.concatenate(lat, axis=0).astype(BF)
    query = dot_nn(left[...], wq_ref[...])
    qt_ref[...] = (query[0:rows] * (inv * (SCALE / LN2))).astype(BF)
    mt_ref[:, 0:256] = query[rows:].astype(BF)
    key = dot_nn(left[...], wk_ref[...])
    block_ref[0:rows, 0:256] = (key[0:rows] * inv).astype(BF)
    mt_ref[:, 256:512] = key[rows:].astype(BF)
    copy.wait()
    value = dot_nn(left[...], wv_ref[...])
    block_ref[0:rows, 256:512] = (value[0:rows] * inv).astype(BF)
    mt_ref[:, 512:768] = value[rows:].astype(BF)


def fold_max(s):
    return functools.reduce(jnp.maximum, [s[:, 128 * n : 128 * (n + 1)] for n in range(6)])


def fold_sum(s):
    return functools.reduce(jnp.add, [s[:, 128 * n : 128 * (n + 1)] for n in range(6)])


def position(index, offset):
    patch = 32 * ((index & 63) >> 3) + 8 * (index >> 6) + (index & 7)
    t = index - PATCHES
    return jnp.where(
        index < PATCHES, offset + patch, jnp.where(t < offset, t, t + PATCHES)
    )


def heads(h):
    return slice(h * HD, (h + 1) * HD)


CHAINS = [(g, h) for g in range(NSEQ) for h in range(2)]


def attend_kernel(
    seq_ref, start_ref, seat_ref, same_ref, other_ref, qt_ref, mt_ref, grad_ref,
    out_ref, z_ref,
    labels, tiles, wide, keys, values, scores, probs, q_s, g_s, o_s, m_s, l_s, zt, zq,
):
    seat = seat_ref[0]
    chip, core = seat >> 1, seat & 1
    offs = own_offsets(seq_ref, start_ref, seat)
    for i in range(IMAGES):
        labels[seq_ref[i] * 8 + lax.div(start_ref[i], BLOCK)] = i

    wide[...] = jnp.zeros_like(wide)
    for a in range(4):
        wide[128 * a + PDIM * a : 128 * a + PDIM * (a + 1), :] = mt_ref[...]
    for k in range(4):
        pair = (chip - k) & 3
        for ref, parity in ((same_ref, core), (other_ref, 1 - core)):
            part = ref[k, NSEQ * TEXT :, :].astype(F32)
            at = pl.multiple_of((2 * pair + parity) * 8, 8)
            for i in range(IMAGES):
                tiles[i, pl.ds(at, 8), :] = part[
                    8 * (i // 4) : 8 * (i // 4 + 1), 128 * (i % 4) : 128 * (i % 4 + 1)
                ]
            at = pl.ds(pl.multiple_of(2 * PATCHES + TEXT * parity, TEXT), TEXT)
            for g in range(NSEQ):
                keys[g, pair, at, :] = ref[k, g * TEXT : (g + 1) * TEXT, 0:256]
                values[g, pair, at, :] = ref[k, g * TEXT : (g + 1) * TEXT, 256:512]

    rows = lax.broadcasted_iota(jnp.int32, (BLOCK, BLOCK), 0)
    cols = lax.broadcasted_iota(jnp.int32, (BLOCK, BLOCK), 1)
    for g in range(NSEQ):
        own_tile = tiles[labels[g * 8 + seat]].astype(BF)
        in_order = jnp.concatenate([tiles[labels[g * 8 + b]] for b in range(8)], axis=0).astype(BF)
        for a in range(4):
            patch = wide[128 * a : 128 * (a + 1), :]
            q_s[g, 64 * a : 64 * (a + 1), :] = (
                dot_nn(own_tile, patch[:, 0:256]) * (SCALE / LN2)
            ).astype(BF)
            kv = dot_nn(in_order, patch[:, 256:768]).astype(BF)
            for b in range(8):
                at = slice(PATCHES * (b % 2) + 64 * a, PATCHES * (b % 2) + 64 * (a + 1))
                keys[g, b // 2, at, :] = kv[64 * b : 64 * (b + 1), 0:256]
                values[g, b // 2, at, :] = kv[64 * b : 64 * (b + 1), 256:512]
        q_s[g, PATCHES:, :] = qt_ref[g * TEXT : (g + 1) * TEXT, :]
        place = jnp.where(cols == position(rows, offs[g]), 1.0, 0.0).astype(BF)
        g_s[g] = dot_nn(place, grad_ref[g]).astype(BF)

    def each(count, body):
        def step(p, carry):
            body(p)
            return carry

        lax.fori_loop(0, count, step, 0)

    q_row = lax.broadcasted_iota(jnp.int32, (BLOCK, 2 * BLOCK), 0)
    k_col = lax.broadcasted_iota(jnp.int32, (BLOCK, 2 * BLOCK), 1)
    in_image = k_col < 2 * PATCHES
    second = jnp.where(in_image, k_col >> 8, (k_col - 2 * PATCHES) >> 7)
    k_row = jnp.where(in_image, k_col & (PATCHES - 1), PATCHES + (k_col & (TEXT - 1)))

    def score(p, diagonal=False):
        for n, (g, h) in enumerate(CHAINS):
            s = dot_nt(q_s[g, :, heads(h)], keys[g, p, :, heads(h)])
            if diagonal:
                off = offs[g]
                reach = jnp.where(q_row < PATCHES, off + (PATCHES - 1), position(q_row, off))
                place = position(k_row, off) + BLOCK * (second - core)
                s = jnp.where(place <= reach, s, -jnp.inf)
                m_s[n] = fold_max(s)
            else:
                m_s[n] = jnp.maximum(m_s[n], fold_max(s))
            scores[n, p] = s

    score(chip, True)
    each(chip, score)

    o_s[...] = jnp.zeros_like(o_s)
    l_s[...] = jnp.zeros_like(l_s)
    for n in range(4):
        m_s[n] = jnp.broadcast_to(jnp.max(m_s[n], axis=1, keepdims=True), (BLOCK, 128))

    def weigh(p):
        for n, (g, h) in enumerate(CHAINS):
            top = m_s[n]
            lifted = jnp.exp2(scores[n, p] - jnp.concatenate([top] * 6, axis=1))
            l_s[n] += fold_sum(lifted)
            lifted = lifted.astype(BF)
            o_s[n] += dot_nn(lifted, values[g, p, :, heads(h)])
            probs[n, p] = lifted

    each(chip + 1, weigh)

    xs = []
    for g in range(NSEQ):
        outs = []
        x = []
        for h in range(2):
            n = 2 * g + h
            inv = 1.0 / jnp.sum(l_s[n], axis=1, keepdims=True)
            out = o_s[n] * inv
            outs.append(out.astype(BF))
            scaled = (g_s[g, :, heads(h)].astype(F32) * inv).astype(BF)
            delta = jnp.sum(scaled.astype(F32) * out, axis=1, keepdims=True)
            m_s[n] = jnp.broadcast_to(delta, (BLOCK, 128))
            g_s[g, :, heads(h)] = scaled
            mk = mt_ref[:, 256 + h * HD : 256 + (h + 1) * HD]
            mv = mt_ref[:, 512 + h * HD : 512 + (h + 1) * HD]
            x.append((dot_nt(mk, q_s[g, :, heads(h)]) * LN2).astype(BF))
            x.append(dot_nt(mv, scaled).astype(BF))
        xs.append(jnp.concatenate(x, axis=1))
        out_c = jnp.concatenate(outs, axis=1)
        back = jnp.where(rows == position(cols, offs[g]), 1.0, 0.0).astype(BF)
        out_ref[g] = dot_nn(back, out_c).astype(BF)
    zq[...] = jnp.zeros_like(zq)
    zt[...] = jnp.zeros_like(zt)

    def differentiate(p):
        for g in range(NSEQ):
            stack = []
            for h in range(2):
                n = 2 * g + h
                delta = jnp.concatenate([m_s[n]] * 6, axis=1)
                value = values[g, p, :, heads(h)]
                dp = dot_nt(g_s[g, 0:PATCHES, heads(h)], value)
                ds = (probs[n, p, 0:PATCHES, :].astype(F32) * (dp - delta[0:PATCHES])).astype(BF)
                dp_text = dot_nt(g_s[g, PATCHES:, heads(h)], value[0 : 2 * PATCHES])
                ds_text = (
                    probs[n, p, PATCHES:, 0 : 2 * PATCHES].astype(F32)
                    * (dp_text - delta[PATCHES:, 0 : 2 * PATCHES])
                ).astype(BF)
                zq[n] += dot_nn(ds, keys[g, p, :, heads(h)])
                stack += [ds[:, 0 : 2 * PATCHES], ds_text, probs[n, p, :, 0 : 2 * PATCHES]]
            zt[g, p] = dot_nn(xs[g], jnp.concatenate(stack, axis=0))

    each(chip + 1, differentiate)

    for g in range(NSEQ):
        own = jnp.zeros((PDIM, PATCHES), F32)
        for h in range(2):
            own = own + dot_nt(mt_ref[:, heads(h)], (zq[2 * g + h] * SCALE).astype(BF))
        for b in range(8):
            flat = zt[g, b // 2, :, PATCHES * (b % 2) : PATCHES * (b % 2 + 1)]
            flat = flat + jnp.where(seat == b, own, 0.0)
            dense = jnp.concatenate([flat[:, 64 * a : 64 * (a + 1)] for a in range(4)], axis=0).T
            z_ref[labels[g * 8 + b]] = dense.astype(BF)


def attend(seq, start, seat, same, other, qt, mt, grad):
    smem = pl.BlockSpec(memory_space=pltpu.SMEM)
    vmem = pl.BlockSpec(memory_space=pltpu.VMEM)
    return pl.pallas_call(
        attend_kernel,
        out_shape=(
            jax.ShapeDtypeStruct((NSEQ, BLOCK, 256), BF),
            jax.ShapeDtypeStruct((IMAGES, 64, 128), BF),
        ),
        in_specs=[smem] * 3 + [vmem] * 5,
        out_specs=(vmem,) * 2,
        scratch_shapes=[
            pltpu.SMEM((IMAGES,), jnp.int32),
            pltpu.VMEM((IMAGES, 64, 128), F32),
            pltpu.VMEM((512, 768), BF),
            pltpu.VMEM((NSEQ, 4, 2 * BLOCK, 256), BF),
            pltpu.VMEM((NSEQ, 4, 2 * BLOCK, 256), BF),
            pltpu.VMEM((4, 4, BLOCK, 2 * BLOCK), F32),
            pltpu.VMEM((4, 4, BLOCK, 2 * BLOCK), BF),
            pltpu.VMEM((NSEQ, BLOCK, 256), BF),
            pltpu.VMEM((NSEQ, BLOCK, 256), BF),
            pltpu.VMEM((4, BLOCK, HD), F32),
            pltpu.VMEM((4, BLOCK, 128), F32),
            pltpu.VMEM((4, BLOCK, 128), F32),
            pltpu.VMEM((NSEQ, 4, PDIM, 2 * PATCHES), F32),
            pltpu.VMEM((4, PATCHES, HD), F32),
        ],
        compiler_params=pltpu.CompilerParams(vmem_limit_bytes=52 * 2**20),
        name="attend",
    )(seq, start, seat, same, other, qt, mt, grad)


def finish_kernel(recv_ref, lat_ref, inv_ref, u_ref, out_ref):
    total = jnp.sum(recv_ref[...].astype(F32), axis=0)
    lat = lat_ref[...].astype(F32)
    for a in range(4):
        at = slice(8 * a, 8 * (a + 1))
        z = total[:, PDIM * a : PDIM * (a + 1)]
        inv = inv_ref[at, :][:, 0:1]
        inner = jnp.sum(lat[at] * z, axis=1, keepdims=True)
        out_ref[at, :] = inv * (z - u_ref[at, :] * (inv * inv * inner * (1.0 / D)))


def on_device(
    text_rows, latents, image_seq, image_start, norm_gain, w_patch, w_query, w_key, w_value, out_grad
):
    seats = lax.axis_size("seq")
    groups = lax.axis_size("dp")
    seat = lax.axis_index("seq").astype(jnp.int32).reshape(1)
    lat = latents.reshape(PDIM, PDIM)
    smem = pl.BlockSpec(memory_space=pltpu.SMEM)
    vmem = pl.BlockSpec(memory_space=pltpu.VMEM)
    hbm = pl.BlockSpec(memory_space=pltpu.HBM)
    send, inv, u = pl.pallas_call(
        pack_kernel,
        out_shape=(
            jax.ShapeDtypeStruct((groups, SEND_ROWS, 256), BF),
            jax.ShapeDtypeStruct((PDIM, 128), F32),
            jax.ShapeDtypeStruct((PDIM, PDIM), F32),
        ),
        in_specs=[hbm, hbm, smem, hbm, hbm, hbm],
        out_specs=(vmem,) * 3,
        scratch_shapes=[
            pltpu.SMEM((IMAGES,), jnp.int32),
            pltpu.SMEM((IMAGES,), jnp.int32),
            pltpu.VMEM((NSEQ, BLOCK, 256), BF),
            pltpu.VMEM((PDIM, PDIM), BF),
            pltpu.VMEM((PDIM, D), BF),
            pltpu.SemaphoreType.DMA((5,)),
        ],
        compiler_params=pltpu.CompilerParams(vmem_limit_bytes=32 * 2**20),
        name="pack",
    )(image_seq, image_start, seat, text_rows, lat, w_patch)
    recv = lax.all_to_all(send, "dp", 0, 0)

    qt, block, mt = pl.pallas_call(
        project_kernel,
        out_shape=(
            jax.ShapeDtypeStruct((NSEQ * TEXT, 256), BF),
            jax.ShapeDtypeStruct((KV_ROWS, 512), BF),
            jax.ShapeDtypeStruct((PDIM, 768), BF),
        ),
        in_specs=[vmem, vmem, vmem, hbm, vmem, vmem],
        out_specs=(vmem,) * 3,
        scratch_shapes=[
            pltpu.VMEM((NSEQ * TEXT + PDIM, D), BF),
            pltpu.VMEM((D, 256), BF),
            pltpu.SemaphoreType.DMA,
        ],
        compiler_params=pltpu.CompilerParams(vmem_limit_bytes=40 * 2**20),
        name="project",
    )(recv, w_query, w_key, w_value, w_patch, norm_gain.reshape(1, D))
    hops = [block] + [
        lax.ppermute(block, "seq", [(i, (i + 2 * k) % seats) for i in range(seats)])
        for k in range(1, seats // 2)
    ]
    same = jnp.stack(hops)
    other = lax.ppermute(same, "seq", [(i, i ^ 1) for i in range(seats)])

    attended, z = attend(image_seq, image_start, seat, same, other, qt, mt, out_grad)
    parts = lax.all_to_all(z.reshape(groups * seats, 8, 128), ("dp", "seq"), 0, 0)
    grad = pl.pallas_call(
        finish_kernel,
        out_shape=jax.ShapeDtypeStruct((PDIM, PDIM), F32),
        in_specs=[vmem] * 4,
        out_specs=vmem,
        compiler_params=pltpu.CompilerParams(vmem_limit_bytes=32 * 2**20),
        name="finish",
    )(parts, lat, inv, u)
    return (attended, grad.reshape(latents.shape))


def solution(mesh):
    in_specs = (
        P(None, "seq", "dp"),
        P("dp", "seq", None),
        P(),
        P(),
        P(),
        P(),
        P(None, "dp"),
        P(None, "dp"),
        P(None, "dp"),
        P(None, "seq", "dp"),
    )
    out_specs = (P(None, "seq", "dp"), P("dp", "seq", None))
    return jax.shard_map(
        on_device, mesh=mesh, in_specs=in_specs, out_specs=out_specs, check_vma=False
    )
```

time: 133 us -> 106 us (0.80)
  starting transfers between devices: 24.2 us -> 4.25 us
  blocking collectives: 73 us -> 61.5 us
  waiting for transfers between devices: 11.1 us -> 18.1 us
  Pallas kernels: 17.4 us -> 14.1 us
    all_to_all x1 -> x0, starting transfers between devices: 24.2 us -> none  [on_device(): lax.all_to_all(z.reshape(groups * seats, 8, 128), ('dp', 'seq'), 0, 0)]
    ppermute x0 -> x4, waiting for transfers between devices: none -> 18.1 us  [the longest x3 15.6 us: on_device(): lax.ppermute(block, 'seq', [(i, (i + 2 * k) % seats) for i in range(seats)])]
    all_to_all x1, blocking collectives: 35.6 us -> 24.2 us  [on_device(): lax.all_to_all(z.reshape(groups * seats, 8, 128), ('dp', 'seq'), 0, 0)]
    all_to_all x1 -> x0, waiting for transfers between devices: 11.1 us -> none  [on_device(): lax.all_to_all(z.reshape(groups * seats, 8, 128), ('dp', 'seq'), 0, 0)]
    ppermute x0 -> x4, starting transfers between devices: none -> 4.25 us  [the longest x3 3.67 us: on_device(): lax.ppermute(block, 'seq', [(i, (i + 2 * k) % seats) for i in range(seats)])]
    pallas_call x2, Pallas kernels: 14.9 us -> 12.1 us  [the longest x1 8.56 us: attend(): pl.pallas_call(attend_kernel, out_shape=(jax.ShapeDtypeStruct((NSEQ, BLOC...]
    unnamed x28 -> x30, local copies, waits for them, and re-layouts: 5.58 us -> 6.61 us
  transfers between devices with their start and end apart: 1 -> 4, of which waited for: 1 -> 4; matrix products, arithmetic and copies ran while one was open for 0% -> 0% of each run, Pallas kernels for 0% -> 0%
where the time goes in v2:
time: 106 us; the launch traced here: 105 us
  blocking collectives  61.5 us (58%)
  waiting for transfers between devices  18.1 us (17%)
  Pallas kernels  14.1 us (13%)
  local copies, waits for them, and re-layouts  6.61 us (6%)
  starting transfers between devices  4.25 us (4%)
    all_to_all x1, blocking collectives, on_device(): recv = lax.all_to_all(send, 'dp', 0, 0)  37.3 us
    all_to_all x1, blocking collectives, on_device(): lax.all_to_all(z.reshape(groups * seats, 8, 128), ('dp', 'seq'), 0, 0)  24.2 us
    ppermute x3, waiting for transfers between devices, on_device(): lax.ppermute(block, 'seq', [(i, (i + 2 * k) % seats) for i in range(seats)])  15.6 us
    pallas_call x1, Pallas kernels, attend(): pl.pallas_call(attend_kernel, out_shape=(jax.ShapeDtypeStruct((NSEQ, BLOC...  8.56 us
    unnamed x30, local copies, waits for them, and re-layouts  6.61 us
    ppermute x3, starting transfers between devices, on_device(): lax.ppermute(block, 'seq', [(i, (i + 2 * k) % seats) for i in range(seats)])  3.67 us
    pallas_call x1, Pallas kernels, on_device(): pl.pallas_call(project_kernel, out_shape=(jax.ShapeDtypeStruct((NSEQ * TE...  3.56 us
    ppermute x1, waiting for transfers between devices, on_device(): other = lax.ppermute(same, 'seq', [(i, i ^ 1) for i in range(seats)])  2.47 us
  transfers between devices with their start and end apart: 4, of which 4 were waited for; matrix products, arithmetic and copies ran while one was open for 0% of the time, Pallas kernels for 0%

profile of v2, /device:TPU:1, one launch (start us, length us, event | category | flops | bytes accessed | tf_op | source)
XLA Modules:
  0.0 105.5 jit_solution(3237887645521082795)
XLA Ops:
  0.6 0.0 copy-start.3
  0.6 0.9 copy-done.3
  1.6 0.0 copy-start.5
  1.6 1.0 copy-done.5
  2.6 0.0 copy-start.7
  2.6 0.7 copy-done.7
  3.3 0.0 copy-start.10
  3.3 0.7 copy-done.10
  3.9 0.0 copy-start.12
  3.9 0.7 copy-done.12
  4.6 0.0 copy-start.9
  4.6 0.9 pack.1
  5.5 0.0 copy-start
  5.5 0.0 copy-start.1
  5.5 0.0 copy-start.4
  5.5 37.3 %all_to_all.10.x_ref = bf16[16,272,256]{2,1,0:T(8,128)(2,1)S(1)} all-to-all(bf16[16,272,256]{2,1,0:T(8,128)(2,1)S(1)} %get-tuple-element.10), channel_id=1, replica_groups=mesh['seq'=8,'dp'=16] {'dp'}, dimensions={0} | all-to-all | bytes 4456448 | tf_op jit(solution)/shard_map/all_to_all | solution.py:362
  42.8 0.0 copy-done.9
  42.8 0.0 copy-done
  42.9 0.0 copy-done.1
  42.9 0.0 copy-done.4
  42.9 0.0 copy-start.2
  42.9 1.6 %copy-done.2 = bf16[4096,256]{1,0:T(8,128)(2,1)S(1)} copy-done((bf16[4096,256]{1,0:T(8,128)(2,1)S(1)}, bf16[4096,256]{1,0:T(8,128)(2,1)}, u32[]{:S(2)}) %copy-start.2) | copy-done | bytes 2097176
  44.5 3.6 %project.1 = (bf16[256,256]{1,0:T(8,128)(2,1)S(1)}, bf16[288,512]{1,0:T(8,128)(2,1)S(1)}, bf16[32,768]{1,0:T(8,128)(2,1)S(1)}) custom-call(bf16[16,272,256]{2,1,0:T(8,128)(2,1)S(1)} %all_to_all.10.x_ref, bf16[4096,256]{1,0:T(8,128)(2,1)S(1)} %copy-done, bf16[4096,256]{1,0:T(8,128)(2,1)S(1)} %copy-done.1, bf16[4096,256]{1,0:T(8,128)(2,1)S(1)} %copy-done.2, ...), custom_call_target="tpu_custom_call" | custom-call | tf_op jit(solution)/shard_map/project/pallas_call | solution.py:364
  48.0 2.6 %collective-permute-start.2 = (bf16[288,512]{1,0:T(8,128)(2,1)S(1)}, bf16[288,512]{1,0:T(8,128)(2,1)S(1)}, u32[]{:S(2)}, u32[]{:S(2)}) collective-permute-start(bf16[288,512]{1,0:T(8,128)(2,1)S(1)} %get-tuple-element.11), channel_id=1, source_target_pairs={{0,96},{16,112},{32,0},{48,16},{64,32},{80,48},{96,64},{112,80},{1... | collective-permute-start | bytes 884744 | tf_op jit(solution)/shard_map/ppermute | solution.py:382
  50.6 0.5 collective-permute-start.1
  51.1 0.6 collective-permute-start
  51.7 4.0 %collective-permute-done.2 = bf16[288,512]{1,0:T(8,128)(2,1)S(1)} collective-permute-done((bf16[288,512]{1,0:T(8,128)(2,1)S(1)}, bf16[288,512]{1,0:T(8,128)(2,1)S(1)}, u32[]{:S(2)}, u32[]{:S(2)}) %collective-permute-start.2) | collective-permute-done | bytes 294944 | tf_op jit(solution)/shard_map/ppermute | solution.py:382
  55.7 2.6 %collective-permute-done.1 = bf16[288,512]{1,0:T(8,128)(2,1)S(1)} collective-permute-done((bf16[288,512]{1,0:T(8,128)(2,1)S(1)}, bf16[288,512]{1,0:T(8,128)(2,1)S(1)}, u32[]{:S(2)}, u32[]{:S(2)}) %collective-permute-start.1) | collective-permute-done | bytes 294944 | tf_op jit(solution)/shard_map/ppermute | solution.py:382
  58.3 9.0 %collective-permute-done = bf16[288,512]{1,0:T(8,128)(2,1)S(1)} collective-permute-done((bf16[288,512]{1,0:T(8,128)(2,1)S(1)}, bf16[288,512]{1,0:T(8,128)(2,1)S(1)}, u32[]{:S(2)}, u32[]{:S(2)}) %collective-permute-start) | collective-permute-done | bytes 294944 | tf_op jit(solution)/shard_map/ppermute | solution.py:382
  67.3 0.0 copy-start.6
  67.3 0.0 copy-start.11
  67.3 0.0 copy-start.13
  67.3 0.1 pad_maximum_fusion.same_ref
  67.5 0.6 collective-permute-start.3
  68.1 2.5 %collective-permute-done.3.other_ref = bf16[4,288,512]{2,1,0:T(8,128)(2,1)S(1)} collective-permute-done((bf16[4,288,512]{2,1,0:T(8,128)(2,1)S(1)}, bf16[4,288,512]{2,1,0:T(8,128)(2,1)S(1)}, u32[]{:S(2)}, u32[]{:S(2)}) %collective-permute-start.3) | collective-permute-done | bytes 1179680 | tf_op jit(solution)/shard_map/ppermute | solution.py:386
  70.5 0.0 copy-start.14
  70.5 1.0 copy-done.14
  71.6 0.0 copy-done.6
  71.6 0.0 copy-done.11
  71.6 0.0 copy-done.13
  71.6 0.0 copy-start.8
  71.6 8.6 %attend.1 = (bf16[2,384,256]{2,1,0:T(8,128)(2,1)}, bf16[16,64,128]{2,1,0:T(8,128)(2,1)S(1)}) custom-call(s32[16]{0:T(128)S(1)} %copy-done.11, s32[16]{0:T(128)S(1)} %copy-done.13, s32[1]{0:T(128)} %bitcast.seat_ref, bf16[4,288,512]{2,1,0:T(8,128)(2,1)S(1)} %pad_maximum_fusion.same_ref, bf16[4,288,512]{2,1,0:T(8,128)(2,1)} %copy-done.14, ...), custom_call_target="tpu_custom_call" | custom-call | tf_op jit(solution)/shard_map/attend/pallas_call | solution.py:292
  80.2 24.2 %all_to_all.11.recv_ref = bf16[128,8,128]{2,1,0:T(8,128)(2,1)S(1)} all-to-all(bf16[128,8,128]{2,1,0:T(8,128)(2,1)S(1)} %bitcast.10), channel_id=1, replica_groups=mesh['seq'=8,'dp'=16] {'dp','seq'}, dimensions={0} | all-to-all | bytes 524288 | tf_op jit(solution)/shard_map/all_to_all | solution.py:389
  104.4 0.0 copy-done.8
  104.4 1.1 %finish.1 = f32[32,32]{1,0:T(8,128)} custom-call(bf16[128,8,128]{2,1,0:T(8,128)(2,1)S(1)} %all_to_all.11.recv_ref, bf16[32,32]{1,0:T(8,128)(2,1)S(1)} %bitcast.12, f32[32,128]{1,0:T(8,128)S(1)} %get-tuple-element.16.inv_ref, f32[32,32]{1,0:T(8,128)S(1)} %get-tuple-element.17.u_ref), custom_call_target="tpu_custom_call" | custom-call | tf_op jit(solution)/shard_map/finish/pallas_call | solution.py:390
Async XLA Ops:
  0.6 1.0 copy-start.3
  1.6 1.0 copy-start.5
  2.6 0.7 copy-start.7
  3.3 0.7 copy-start.10
  3.9 0.7 copy-start.12
  4.6 38.3 %copy-start.9 = (f32[4096]{0:T(1024)S(1)}, f32[4096]{0:T(1024)}, u32[]{:S(2)}) copy-start(f32[4096]{0:T(1024)} %param.14) | copy-start | bytes 49156
  5.5 37.4 %copy-start = (bf16[4096,256]{1,0:T(8,128)(2,1)S(1)}, bf16[4096,256]{1,0:T(8,128)(2,1)}, u32[]{:S(2)}) copy-start(bf16[4096,256]{1,0:T(8,128)(2,1)} %wq_ref.1) | copy-start | bytes 6291460
  5.5 37.3 %copy-start.1 = (bf16[4096,256]{1,0:T(8,128)(2,1)S(1)}, bf16[4096,256]{1,0:T(8,128)(2,1)}, u32[]{:S(2)}) copy-start(bf16[4096,256]{1,0:T(8,128)(2,1)} %wk_ref.1) | copy-start | bytes 6291460
  5.5 37.3 %copy-start.4 = (bf16[32,4096]{1,0:T(8,128)(2,1)S(1)}, bf16[32,4096]{1,0:T(8,128)(2,1)}, u32[]{:S(2)}) copy-start(bf16[32,4096]{1,0:T(8,128)(2,1)} %wp_ref.1) | copy-start | bytes 786436
  42.9 1.6 %copy-start.2 = (bf16[4096,256]{1,0:T(8,128)(2,1)S(1)}, bf16[4096,256]{1,0:T(8,128)(2,1)}, u32[]{:S(2)}) copy-start(bf16[4096,256]{1,0:T(8,128)(2,1)} %wv_hbm.1) | copy-start | bytes 6291460
  48.0 7.7 %collective-permute-start.2 = (bf16[288,512]{1,0:T(8,128)(2,1)S(1)}, bf16[288,512]{1,0:T(8,128)(2,1)S(1)}, u32[]{:S(2)}, u32[]{:S(2)}) collective-permute-start(bf16[288,512]{1,0:T(8,128)(2,1)S(1)} %get-tuple-element.11), channel_id=1, source_target_pairs={{0,96},{16,112},{32,0},{48,16},{64,32},{80,48},{96,64},{112,80},{1... | collective-permute-start | bytes 884744 | tf_op jit(solution)/shard_map/ppermute | solution.py:382
  50.6 7.7 %collective-permute-start.1 = (bf16[288,512]{1,0:T(8,128)(2,1)S(1)}, bf16[288,512]{1,0:T(8,128)(2,1)S(1)}, u32[]{:S(2)}, u32[]{:S(2)}) collective-permute-start(bf16[288,512]{1,0:T(8,128)(2,1)S(1)} %get-tuple-element.11), channel_id=1, source_target_pairs={{0,64},{16,80},{32,96},{48,112},{64,0},{80,16},{96,32},{112,48},{1... | collective-permute-start | bytes 884744 | tf_op jit(solution)/shard_map/ppermute | solution.py:382
  51.1 16.2 %collective-permute-start = (bf16[288,512]{1,0:T(8,128)(2,1)S(1)}, bf16[288,512]{1,0:T(8,128)(2,1)S(1)}, u32[]{:S(2)}, u32[]{:S(2)}) collective-permute-start(bf16[288,512]{1,0:T(8,128)(2,1)S(1)} %get-tuple-element.11), channel_id=1, source_target_pairs={{0,32},{16,48},{32,64},{48,80},{64,96},{80,112},{96,0},{112,16},{1... | collective-permute-start | bytes 884744 | tf_op jit(solution)/shard_map/ppermute | solution.py:382
  67.3 4.2 %copy-start.6 = (bf16[2,384,256]{2,1,0:T(8,128)(2,1)S(1)}, bf16[2,384,256]{2,1,0:T(8,128)(2,1)}, u32[]{:S(2)}) copy-start(bf16[2,384,256]{2,1,0:T(8,128)(2,1)} %grad_ref.1) | copy-start | bytes 1179652
  67.3 4.3 %copy-start.11 = (s32[16]{0:T(128)S(1)}, s32[16]{0:T(128)}, u32[]{:S(2)}) copy-start(s32[16]{0:T(128)} %seq_ref.1) | copy-start | bytes 196
  67.3 4.3 %copy-start.13 = (s32[16]{0:T(128)S(1)}, s32[16]{0:T(128)}, u32[]{:S(2)}) copy-start(s32[16]{0:T(128)} %start_ref.1) | copy-start | bytes 196
  67.5 3.0 %collective-permute-start.3 = (bf16[4,288,512]{2,1,0:T(8,128)(2,1)S(1)}, bf16[4,288,512]{2,1,0:T(8,128)(2,1)S(1)}, u32[]{:S(2)}, u32[]{:S(2)}) collective-permute-start(bf16[4,288,512]{2,1,0:T(8,128)(2,1)S(1)} %pad_maximum_fusion.same_ref), channel_id=1, source_target_pairs={{0,16},{16,0},{32,48},{48,32},{64,80},{80,64},{96,112},{112,96},{1... | collective-permute-start | bytes 3538952 | tf_op jit(solution)/shard_map/ppermute | solution.py:386
  70.5 1.0 copy-start.14
  71.6 32.8 %copy-start.8 = (bf16[1,32,32]{2,1,0:T(8,128)(2,1)S(1)}, bf16[1,32,32]{2,1,0:T(8,128)(2,1)}, u32[]{:S(2)}) copy-start(bf16[1,32,32]{2,1,0:T(8,128)(2,1)} %param.11) | copy-start | bytes 6148

commit v3 on v2

--- a/solution.py
+++ b/solution.py
@@ -136,27 +136,31 @@
     return slice(h * HD, (h + 1) * HD)
 
 
+def pinned(x):
+    return pltpu.with_memory_space_constraint(x, pltpu.HBM)
+
+
 CHAINS = [(g, h) for g in range(NSEQ) for h in range(2)]
 
 
 def attend_kernel(
-    seq_ref, start_ref, seat_ref, same_ref, other_ref, qt_ref, mt_ref, grad_ref,
+    seq_hbm, start_hbm, seat_ref, s0, s1, s2, s3, o0, o1, o2, o3, qt_ref, mt_ref, grad_hbm,
     out_ref, z_ref,
-    labels, tiles, wide, keys, values, scores, probs, q_s, g_s, o_s, m_s, l_s, zt, zq,
+    labels, tiles, wide, keys, values, scores, probs, q_s, g_s, o_s, m_s, l_s, zt, zq, grad_ref, seq_ref, start_ref, sems,
 ):
+    pairs = ((seq_hbm, seq_ref), (start_hbm, start_ref), (grad_hbm, grad_ref))
+    copies = [pltpu.make_async_copy(a, b, sems.at[n]) for n, (a, b) in enumerate(pairs)]
+    for copy in copies:
+        copy.start()
     seat = seat_ref[0]
     chip, core = seat >> 1, seat & 1
-    offs = own_offsets(seq_ref, start_ref, seat)
-    for i in range(IMAGES):
-        labels[seq_ref[i] * 8 + lax.div(start_ref[i], BLOCK)] = i
-
     wide[...] = jnp.zeros_like(wide)
     for a in range(4):
         wide[128 * a + PDIM * a : 128 * a + PDIM * (a + 1), :] = mt_ref[...]
     for k in range(4):
         pair = (chip - k) & 3
-        for ref, parity in ((same_ref, core), (other_ref, 1 - core)):
-            part = ref[k, NSEQ * TEXT :, :].astype(F32)
+        for ref, parity in (((s0, s1, s2, s3)[k], core), ((o0, o1, o2, o3)[k], 1 - core)):
+            part = ref[NSEQ * TEXT :, :].astype(F32)
             at = pl.multiple_of((2 * pair + parity) * 8, 8)
             for i in range(IMAGES):
                 tiles[i, pl.ds(at, 8), :] = part[
@@ -164,9 +168,14 @@
                 ]
             at = pl.ds(pl.multiple_of(2 * PATCHES + TEXT * parity, TEXT), TEXT)
             for g in range(NSEQ):
-                keys[g, pair, at, :] = ref[k, g * TEXT : (g + 1) * TEXT, 0:256]
-                values[g, pair, at, :] = ref[k, g * TEXT : (g + 1) * TEXT, 256:512]
-
+                keys[g, pair, at, :] = ref[g * TEXT : (g + 1) * TEXT, 0:256]
+                values[g, pair, at, :] = ref[g * TEXT : (g + 1) * TEXT, 256:512]
+
+    copies[0].wait()
+    copies[1].wait()
+    offs = own_offsets(seq_ref, start_ref, seat)
+    for i in range(IMAGES):
+        labels[seq_ref[i] * 8 + lax.div(start_ref[i], BLOCK)] = i
     rows = lax.broadcasted_iota(jnp.int32, (BLOCK, BLOCK), 0)
     cols = lax.broadcasted_iota(jnp.int32, (BLOCK, BLOCK), 1)
     for g in range(NSEQ):
@@ -183,6 +192,8 @@
                 keys[g, b // 2, at, :] = kv[64 * b : 64 * (b + 1), 0:256]
                 values[g, b // 2, at, :] = kv[64 * b : 64 * (b + 1), 256:512]
         q_s[g, PATCHES:, :] = qt_ref[g * TEXT : (g + 1) * TEXT, :]
+    copies[2].wait()
+    for g in range(NSEQ):
         place = jnp.where(cols == position(rows, offs[g]), 1.0, 0.0).astype(BF)
         g_s[g] = dot_nn(place, grad_ref[g]).astype(BF)
 
@@ -287,6 +298,7 @@
 
 
 def attend(seq, start, seat, same, other, qt, mt, grad):
+    hbm = pl.BlockSpec(memory_space=pltpu.HBM)
     smem = pl.BlockSpec(memory_space=pltpu.SMEM)
     vmem = pl.BlockSpec(memory_space=pltpu.VMEM)
     return pl.pallas_call(
@@ -295,7 +307,7 @@
             jax.ShapeDtypeStruct((NSEQ, BLOCK, 256), BF),
             jax.ShapeDtypeStruct((IMAGES, 64, 128), BF),
         ),
-        in_specs=[smem] * 3 + [vmem] * 5,
+        in_specs=[hbm, hbm, smem] + [vmem] * 10 + [hbm],
         out_specs=(vmem,) * 2,
         scratch_shapes=[
             pltpu.SMEM((IMAGES,), jnp.int32),
@@ -312,10 +324,14 @@
             pltpu.VMEM((4, BLOCK, 128), F32),
             pltpu.VMEM((NSEQ, 4, PDIM, 2 * PATCHES), F32),
             pltpu.VMEM((4, PATCHES, HD), F32),
+            pltpu.VMEM((NSEQ, BLOCK, 256), BF),
+            pltpu.SMEM((IMAGES,), jnp.int32),
+            pltpu.SMEM((IMAGES,), jnp.int32),
+            pltpu.SemaphoreType.DMA((3,)),
         ],
         compiler_params=pltpu.CompilerParams(vmem_limit_bytes=52 * 2**20),
         name="attend",
-    )(seq, start, seat, same, other, qt, mt, grad)
+    )(pinned(seq), pinned(start), seat, *same, *other, qt, mt, pinned(grad))
 
 
 def finish_kernel(recv_ref, lat_ref, inv_ref, u_ref, out_ref):
@@ -358,7 +374,7 @@
         ],
         compiler_params=pltpu.CompilerParams(vmem_limit_bytes=32 * 2**20),
         name="pack",
-    )(image_seq, image_start, seat, text_rows, lat, w_patch)
+    )(pinned(image_seq), pinned(image_start), seat, pinned(text_rows), pinned(lat), pinned(w_patch))
     recv = lax.all_to_all(send, "dp", 0, 0)
 
     qt, block, mt = pl.pallas_call(
@@ -377,15 +393,13 @@
         ],
         compiler_params=pltpu.CompilerParams(vmem_limit_bytes=40 * 2**20),
         name="project",
-    )(recv, w_query, w_key, w_value, w_patch, norm_gain.reshape(1, D))
+    )(recv, w_query, w_key, pinned(w_value), w_patch, norm_gain.reshape(1, D))
     hops = [block] + [
         lax.ppermute(block, "seq", [(i, (i + 2 * k) % seats) for i in range(seats)])
         for k in range(1, seats // 2)
     ]
-    same = jnp.stack(hops)
-    other = lax.ppermute(same, "seq", [(i, i ^ 1) for i in range(seats)])
-
-    attended, z = attend(image_seq, image_start, seat, same, other, qt, mt, out_grad)
+    other = [lax.ppermute(hop, "seq", [(i, i ^ 1) for i in range(seats)]) for hop in hops]
+    attended, z = attend(image_seq, image_start, seat, hops, other, qt, mt, out_grad)
     parts = lax.all_to_all(z.reshape(groups * seats, 8, 128), ("dp", "seq"), 0, 0)
     grad = pl.pallas_call(
         finish_kernel,

time: 106 us -> 99.6 us (0.940)
  waiting for transfers between devices: 18.1 us -> 5.24 us
  starting transfers between devices: 4.25 us -> 15.7 us
  local copies, waits for them, and re-layouts: 6.61 us -> 0.74 us
  Pallas kernels: 14.1 us -> 15.2 us
    ppermute x3, waiting for transfers between devices: 15.6 us -> 4.06 us  [on_device(): lax.ppermute(block, 'seq', [(i, (i + 2 * k) % seats) for i in range(seats)])]
    ppermute x1 -> x4, starting transfers between devices: 0.57 us -> 12.1 us  [on_device(): lax.ppermute(hop, 'seq', [(i, i ^ 1) for i in range(seats)])]
    unnamed x30 -> x16, local copies, waits for them, and re-layouts: 6.61 us -> 0.74 us
    ppermute x1 -> x4, waiting for transfers between devices: 2.47 us -> 1.19 us  [on_device(): lax.ppermute(hop, 'seq', [(i, i ^ 1) for i in range(seats)])]
  transfers between devices with their start and end apart: 4 -> 7, of which waited for: 4 -> 3; matrix products, arithmetic and copies ran while one was open for 0% -> 0% of each run, Pallas kernels for 0% -> 0%
where the time goes in v3:
time: 99.6 us; the launch traced here: 99.4 us
  blocking collectives  61.7 us (62%)
  starting transfers between devices  15.7 us (16%)
  Pallas kernels  15.2 us (15%)
  waiting for transfers between devices  5.24 us (5%)
    all_to_all x1, blocking collectives, on_device(): recv = lax.all_to_all(send, 'dp', 0, 0)  37.3 us
    all_to_all x1, blocking collectives, on_device(): lax.all_to_all(z.reshape(groups * seats, 8, 128), ('dp', 'seq'), 0, 0)  24.4 us
    ppermute x4, starting transfers between devices, on_device(): lax.ppermute(hop, 'seq', [(i, i ^ 1) for i in range(seats)])  12.1 us
    pallas_call x1, Pallas kernels, attend(): pl.pallas_call(attend_kernel, out_shape=(jax.ShapeDtypeStruct((NSEQ, BLOC...  8.95 us
    ppermute x3, waiting for transfers between devices, on_device(): lax.ppermute(block, 'seq', [(i, (i + 2 * k) % seats) for i in range(seats)])  4.06 us
    ppermute x3, starting transfers between devices, on_device(): lax.ppermute(block, 'seq', [(i, (i + 2 * k) % seats) for i in range(seats)])  3.66 us
    pallas_call x1, Pallas kernels, on_device(): pl.pallas_call(project_kernel, out_shape=(jax.ShapeDtypeStruct((NSEQ * TE...  3.45 us
  transfers between devices with their start and end apart: 7, of which 3 were waited for; matrix products, arithmetic and copies ran while one was open for 0% of the time, Pallas kernels for 0%

profile of v3, /device:TPU:1, one launch (start us, length us, event | category | flops | bytes accessed | tf_op | source)
XLA Modules:
  0.0 99.4 jit_solution(4951228907659164645)
XLA Ops:
  0.6 0.0 copy-start.4
  0.6 1.7 %pack.1 = (bf16[16,272,256]{2,1,0:T(8,128)(2,1)S(1)}, f32[32,128]{1,0:T(8,128)S(1)}, f32[32,32]{1,0:T(8,128)S(1)}) custom-call(s32[16]{0:T(128)} %seq_hbm.3, s32[16]{0:T(128)} %start_hbm.3, s32[1]{0:T(128)} %bitcast.seat_ref, bf16[2,384,256]{2,1,0:T(8,128)(2,1)} %text_hbm.1, bf16[32,32]{1,0:T(8,128)(2,1)} %bitcast.6, bf16[32,4096]{1,0:T(8,128)(2,1)} %wp_ref.1), custom_call_target="tpu_custom_call" | custom-call | tf_op jit(solution)/shard_map/pack/pallas_call | solution.py:358
  2.3 0.0 copy-start
  2.3 0.0 copy-start.1
  2.3 0.0 copy-start.2
  2.3 37.3 %all_to_all.10.x_ref = bf16[16,272,256]{2,1,0:T(8,128)(2,1)S(1)} all-to-all(bf16[16,272,256]{2,1,0:T(8,128)(2,1)S(1)} %get-tuple-element.10), channel_id=1, replica_groups=mesh['seq'=8,'dp'=16] {'dp'}, dimensions={0} | all-to-all | bytes 4456448 | tf_op jit(solution)/shard_map/all_to_all | solution.py:378
  39.7 0.0 copy-done.4
  39.7 0.0 copy-done
  39.7 0.0 copy-done.1
  39.7 0.0 copy-done.2
  39.7 3.4 %project.1 = (bf16[256,256]{1,0:T(8,128)(2,1)S(1)}, bf16[288,512]{1,0:T(8,128)(2,1)S(1)}, bf16[32,768]{1,0:T(8,128)(2,1)S(1)}) custom-call(bf16[16,272,256]{2,1,0:T(8,128)(2,1)S(1)} %all_to_all.10.x_ref, bf16[4096,256]{1,0:T(8,128)(2,1)S(1)} %copy-done, bf16[4096,256]{1,0:T(8,128)(2,1)S(1)} %copy-done.1, bf16[4096,256]{1,0:T(8,128)(2,1)} %wv_hbm.1, ...), custom_call_target="tpu_custom_call" | custom-call | tf_op jit(solution)/shard_map/project/pallas_call | solution.py:380
  43.1 0.0 copy-start.3
  43.2 2.5 %collective-permute-start.2 = (bf16[288,512]{1,0:T(8,128)(2,1)S(1)}, bf16[288,512]{1,0:T(8,128)(2,1)S(1)}, u32[]{:S(2)}, u32[]{:S(2)}) collective-permute-start(bf16[288,512]{1,0:T(8,128)(2,1)S(1)} %get-tuple-element.11.s0), channel_id=1, source_target_pairs={{0,96},{16,112},{32,0},{48,16},{64,32},{80,48},{96,64},{112,80},{1... | collective-permute-start | bytes 884744 | tf_op jit(solution)/shard_map/ppermute | solution.py:398
  45.7 0.5 collective-permute-start.1
  46.2 0.6 collective-permute-start
  46.8 2.9 %collective-permute-start.3 = (bf16[288,512]{1,0:T(8,128)(2,1)S(1)}, bf16[288,512]{1,0:T(8,128)(2,1)S(1)}, u32[]{:S(2)}, u32[]{:S(2)}) collective-permute-start(bf16[288,512]{1,0:T(8,128)(2,1)S(1)} %get-tuple-element.11.s0), channel_id=1, source_target_pairs={{0,16},{16,0},{32,48},{48,32},{64,80},{80,64},{96,112},{112,96},{1... | collective-permute-start | bytes 884744 | tf_op jit(solution)/shard_map/ppermute | solution.py:401
  49.7 1.1 %collective-permute-done.2.s3 = bf16[288,512]{1,0:T(8,128)(2,1)S(1)} collective-permute-done((bf16[288,512]{1,0:T(8,128)(2,1)S(1)}, bf16[288,512]{1,0:T(8,128)(2,1)S(1)}, u32[]{:S(2)}, u32[]{:S(2)}) %collective-permute-start.2) | collective-permute-done | bytes 294944 | tf_op jit(solution)/shard_map/ppermute | solution.py:398
  50.9 8.4 %collective-permute-start.6 = (bf16[288,512]{1,0:T(8,128)(2,1)S(1)}, bf16[288,512]{1,0:T(8,128)(2,1)S(1)}, u32[]{:S(2)}, u32[]{:S(2)}) collective-permute-start(bf16[288,512]{1,0:T(8,128)(2,1)S(1)} %collective-permute-done.2.s3), channel_id=1, source_target_pairs={{0,16},{16,0},{32,48},{48,32},{64,80},{80,64},{96,112},{112,96},{1... | collective-permute-start | bytes 884744 | tf_op jit(solution)/shard_map/ppermute | solution.py:401
  59.3 0.0 collective-permute-done.1.s2
  59.3 0.2 collective-permute-start.5
  59.5 2.9 %collective-permute-done.s1 = bf16[288,512]{1,0:T(8,128)(2,1)S(1)} collective-permute-done((bf16[288,512]{1,0:T(8,128)(2,1)S(1)}, bf16[288,512]{1,0:T(8,128)(2,1)S(1)}, u32[]{:S(2)}, u32[]{:S(2)}) %collective-permute-start) | collective-permute-done | bytes 294944 | tf_op jit(solution)/shard_map/ppermute | solution.py:398
  62.5 0.5 collective-permute-start.4
  62.9 0.0 collective-permute-done.3.o0
  63.0 0.0 collective-permute-done.6.o3
  63.0 0.0 copy-start.5
  63.0 0.0 collective-permute-done.5.o2
  63.0 0.0 copy-start.6
  63.0 1.2 %collective-permute-done.4.o1 = bf16[288,512]{1,0:T(8,128)(2,1)S(1)} collective-permute-done((bf16[288,512]{1,0:T(8,128)(2,1)S(1)}, bf16[288,512]{1,0:T(8,128)(2,1)S(1)}, u32[]{:S(2)}, u32[]{:S(2)}) %collective-permute-start.4) | collective-permute-done | bytes 294944 | tf_op jit(solution)/shard_map/ppermute | solution.py:401
  64.2 0.0 copy-start.7
  64.2 0.0 copy-done.5
  64.2 0.0 copy-done.6
  64.2 0.7 copy-done.7
  64.9 9.0 %attend.1 = (bf16[2,384,256]{2,1,0:T(8,128)(2,1)}, bf16[16,64,128]{2,1,0:T(8,128)(2,1)S(1)}) custom-call(s32[16]{0:T(128)} %seq_hbm.3, s32[16]{0:T(128)} %start_hbm.3, s32[1]{0:T(128)} %bitcast.seat_ref, bf16[288,512]{1,0:T(8,128)(2,1)S(1)} %get-tuple-element.11.s0, bf16[288,512]{1,0:T(8,128)(2,1)S(1)} %collective-permute-done.s1, ...), custom_call_target="tpu_custom_call" | custom-call | tf_op jit(solution)/shard_map/attend/pallas_call | solution.py:304
  73.8 24.4 %all_to_all.11.recv_ref = bf16[128,8,128]{2,1,0:T(8,128)(2,1)S(1)} all-to-all(bf16[128,8,128]{2,1,0:T(8,128)(2,1)S(1)} %bitcast.5), channel_id=1, replica_groups=mesh['seq'=8,'dp'=16] {'dp','seq'}, dimensions={0} | all-to-all | bytes 524288 | tf_op jit(solution)/shard_map/all_to_all | solution.py:403
  98.2 0.0 copy-done.3
  98.3 1.1 %finish.1 = f32[32,32]{1,0:T(8,128)} custom-call(bf16[128,8,128]{2,1,0:T(8,128)(2,1)S(1)} %all_to_all.11.recv_ref, bf16[32,32]{1,0:T(8,128)(2,1)S(1)} %bitcast.7, f32[32,128]{1,0:T(8,128)S(1)} %get-tuple-element.16.inv_ref, f32[32,32]{1,0:T(8,128)S(1)} %get-tuple-element.17.u_ref), custom_call_target="tpu_custom_call" | custom-call | tf_op jit(solution)/shard_map/finish/pallas_call | solution.py:404
Async XLA Ops:
  0.6 39.0 %copy-start.4 = (f32[4096]{0:T(1024)S(1)}, f32[4096]{0:T(1024)}, u32[]{:S(2)}) copy-start(f32[4096]{0:T(1024)} %param.14) | copy-start | bytes 49156
  2.3 37.4 %copy-start = (bf16[4096,256]{1,0:T(8,128)(2,1)S(1)}, bf16[4096,256]{1,0:T(8,128)(2,1)}, u32[]{:S(2)}) copy-start(bf16[4096,256]{1,0:T(8,128)(2,1)} %wq_ref.1) | copy-start | bytes 6291460
  2.3 37.4 %copy-start.1 = (bf16[4096,256]{1,0:T(8,128)(2,1)S(1)}, bf16[4096,256]{1,0:T(8,128)(2,1)}, u32[]{:S(2)}) copy-start(bf16[4096,256]{1,0:T(8,128)(2,1)} %wk_ref.1) | copy-start | bytes 6291460
  2.3 37.3 %copy-start.2 = (bf16[32,4096]{1,0:T(8,128)(2,1)S(1)}, bf16[32,4096]{1,0:T(8,128)(2,1)}, u32[]{:S(2)}) copy-start(bf16[32,4096]{1,0:T(8,128)(2,1)} %wp_ref.1) | copy-start | bytes 786436
  43.1 55.1 %copy-start.3 = (bf16[1,32,32]{2,1,0:T(8,128)(2,1)S(1)}, bf16[1,32,32]{2,1,0:T(8,128)(2,1)}, u32[]{:S(2)}) copy-start(bf16[1,32,32]{2,1,0:T(8,128)(2,1)} %param.11) | copy-start | bytes 6148
  43.2 7.7 %collective-permute-start.2 = (bf16[288,512]{1,0:T(8,128)(2,1)S(1)}, bf16[288,512]{1,0:T(8,128)(2,1)S(1)}, u32[]{:S(2)}, u32[]{:S(2)}) collective-permute-start(bf16[288,512]{1,0:T(8,128)(2,1)S(1)} %get-tuple-element.11.s0), channel_id=1, source_target_pairs={{0,96},{16,112},{32,0},{48,16},{64,32},{80,48},{96,64},{112,80},{1... | collective-permute-start | bytes 884744 | tf_op jit(solution)/shard_map/ppermute | solution.py:398
  45.7 13.6 %collective-permute-start.1 = (bf16[288,512]{1,0:T(8,128)(2,1)S(1)}, bf16[288,512]{1,0:T(8,128)(2,1)S(1)}, u32[]{:S(2)}, u32[]{:S(2)}) collective-permute-start(bf16[288,512]{1,0:T(8,128)(2,1)S(1)} %get-tuple-element.11.s0), channel_id=1, source_target_pairs={{0,64},{16,80},{32,96},{48,112},{64,0},{80,16},{96,32},{112,48},{1... | collective-permute-start | bytes 884744 | tf_op jit(solution)/shard_map/ppermute | solution.py:398
  46.2 16.2 %collective-permute-start = (bf16[288,512]{1,0:T(8,128)(2,1)S(1)}, bf16[288,512]{1,0:T(8,128)(2,1)S(1)}, u32[]{:S(2)}, u32[]{:S(2)}) collective-permute-start(bf16[288,512]{1,0:T(8,128)(2,1)S(1)} %get-tuple-element.11.s0), channel_id=1, source_target_pairs={{0,32},{16,48},{32,64},{48,80},{64,96},{80,112},{96,0},{112,16},{1... | collective-permute-start | bytes 884744 | tf_op jit(solution)/shard_map/ppermute | solution.py:398
  46.8 16.1 %collective-permute-start.3 = (bf16[288,512]{1,0:T(8,128)(2,1)S(1)}, bf16[288,512]{1,0:T(8,128)(2,1)S(1)}, u32[]{:S(2)}, u32[]{:S(2)}) collective-permute-start(bf16[288,512]{1,0:T(8,128)(2,1)S(1)} %get-tuple-element.11.s0), channel_id=1, source_target_pairs={{0,16},{16,0},{32,48},{48,32},{64,80},{80,64},{96,112},{112,96},{1... | collective-permute-start | bytes 884744 | tf_op jit(solution)/shard_map/ppermute | solution.py:401
  50.9 12.1 %collective-permute-start.6 = (bf16[288,512]{1,0:T(8,128)(2,1)S(1)}, bf16[288,512]{1,0:T(8,128)(2,1)S(1)}, u32[]{:S(2)}, u32[]{:S(2)}) collective-permute-start(bf16[288,512]{1,0:T(8,128)(2,1)S(1)} %collective-permute-done.2.s3), channel_id=1, source_target_pairs={{0,16},{16,0},{32,48},{48,32},{64,80},{80,64},{96,112},{112,96},{1... | collective-permute-start | bytes 884744 | tf_op jit(solution)/shard_map/ppermute | solution.py:401
  59.3 3.7 %collective-permute-start.5 = (bf16[288,512]{1,0:T(8,128)(2,1)S(1)}, bf16[288,512]{1,0:T(8,128)(2,1)S(1)}, u32[]{:S(2)}, u32[]{:S(2)}) collective-permute-start(bf16[288,512]{1,0:T(8,128)(2,1)S(1)} %collective-permute-done.1.s2), channel_id=1, source_target_pairs={{0,16},{16,0},{32,48},{48,32},{64,80},{80,64},{96,112},{112,96},{1... | collective-permute-start | bytes 884744 | tf_op jit(solution)/shard_map/ppermute | solution.py:401
  62.5 1.7 %collective-permute-start.4 = (bf16[288,512]{1,0:T(8,128)(2,1)S(1)}, bf16[288,512]{1,0:T(8,128)(2,1)S(1)}, u32[]{:S(2)}, u32[]{:S(2)}) collective-permute-start(bf16[288,512]{1,0:T(8,128)(2,1)S(1)} %collective-permute-done.s1), channel_id=1, source_target_pairs={{0,16},{16,0},{32,48},{48,32},{64,80},{80,64},{96,112},{112,96},{1... | collective-permute-start | bytes 884744 | tf_op jit(solution)/shard_map/ppermute | solution.py:401
  63.0 1.2 %copy-start.5 = (bf16[288,512]{1,0:T(8,128)(2,1)}, bf16[288,512]{1,0:T(8,128)(2,1)S(1)}, u32[]{:S(2)}) copy-start(bf16[288,512]{1,0:T(8,128)(2,1)S(1)} %collective-permute-done.6.o3) | copy-start | bytes 884740
  63.0 1.2 %copy-start.6 = (bf16[288,512]{1,0:T(8,128)(2,1)}, bf16[288,512]{1,0:T(8,128)(2,1)S(1)}, u32[]{:S(2)}) copy-start(bf16[288,512]{1,0:T(8,128)(2,1)S(1)} %collective-permute-done.5.o2) | copy-start | bytes 884740
  64.2 0.7 copy-start.7

commit v4 on v3

--- a/solution.py
+++ b/solution.py
@@ -21,7 +21,8 @@
 LN2 = math.log(2.0)
 BF = jnp.bfloat16
 F32 = jnp.float32
-SEND_ROWS = NSEQ * TEXT + 16
+SIDE = 4
+HOPS = (1, 3, 2)
 KV_ROWS = NSEQ * TEXT + 32
 
 
@@ -44,13 +45,13 @@
 
 
 def pack_kernel(
-    seq_hbm, start_hbm, seat_ref, text_hbm, lat_hbm, wp_hbm,
-    send_ref, inv_ref, u_ref,
+    seq_hbm, start_hbm, seat_ref, text_hbm, lat_hbm, wp_hbm, gain_hbm,
+    first_ref, second_ref, inv_ref, u_ref, patch_ref, gain_ref,
     seq_ref, start_ref, text_ref, lat_ref, wp_ref, sems,
 ):
     pairs = (
         (seq_hbm, seq_ref), (start_hbm, start_ref), (lat_hbm, lat_ref), (wp_hbm, wp_ref),
-        (text_hbm, text_ref),
+        (text_hbm, text_ref), (gain_hbm, gain_ref),
     )
     copies = [pltpu.make_async_copy(a, b, sems.at[n]) for n, (a, b) in enumerate(pairs)]
     for copy in copies:
@@ -73,47 +74,58 @@
     offs = own_offsets(seq_ref, start_ref, seat_ref[0])
     copies[4].wait()
     row = lax.broadcasted_iota(jnp.int32, (TEXT, 256), 0)
-    texts = []
-    for g in range(NSEQ):
+    for g, ref in ((0, first_ref), (1, second_ref)):
         low = text_ref[g, 0:TEXT, :].astype(F32)
         high = text_ref[g, PATCHES:BLOCK, :].astype(F32)
-        texts.append(jnp.where(row < offs[g], low, high).astype(BF))
-    for d in range(send_ref.shape[0]):
-        for g in range(NSEQ):
-            send_ref[d, g * TEXT : (g + 1) * TEXT, :] = texts[g]
-        send_ref[d, NSEQ * TEXT :, :] = tail
+        ref[0:TEXT, :] = jnp.where(row < offs[g], low, high).astype(BF)
+    first_ref[TEXT:, :] = tail
+    second_ref[TEXT:, :] = jnp.zeros((16, 256), BF)
+    copies[5].wait()
+    patch_ref[...] = (wp.astype(F32) * gain_ref[...]).astype(BF)
+
+
+def fold_kernel(patch_ref, wq_hbm, wk_hbm, wv_hbm, wq_ref, wk_ref, wv_ref, mt_ref, sems):
+    pairs = ((wq_hbm, wq_ref), (wk_hbm, wk_ref), (wv_hbm, wv_ref))
+    copies = [pltpu.make_async_copy(a, b, sems.at[n]) for n, (a, b) in enumerate(pairs)]
+    for copy in copies:
+        copy.start()
+    for n, (_, ref) in enumerate(pairs):
+        copies[n].wait()
+        mt_ref[:, 256 * n : 256 * (n + 1)] = dot_nn(patch_ref[...], ref[...]).astype(BF)
 
 
 def project_kernel(
-    x_ref, wq_ref, wk_ref, wv_hbm, wp_ref, gain_ref, qt_ref, block_ref, mt_ref, left, wv_ref, sem
+    group_ref, f0, f1, f2, f3, t0, t1, t2, t3, gain_ref, wq_ref, wk_ref, wv_ref,
+    qt_ref, block_ref,
+    left, lat,
 ):
-    copy = pltpu.make_async_copy(wv_hbm, wv_ref, sem)
-    copy.start()
     rows = NSEQ * TEXT
-    ssq = jnp.zeros((rows, 128), F32)
-    tiles = []
-    for d in range(x_ref.shape[0]):
-        at = slice(256 * d, 256 * (d + 1))
-        gain = gain_ref[:, at]
-        x = x_ref[d, 0:rows, :].astype(F32)
+    z_here, y_here = group_ref[0] >> 2, group_ref[0] & 3
+    sums = [jnp.zeros((TEXT, 128), F32) for g in range(NSEQ)]
+
+    def place(ref, piece, g, z, y):
+        at = pl.ds(pl.multiple_of(256 * (SIDE * z + y), 256), 256)
+        x = ref[piece, 0:TEXT, :].astype(F32)
+        left[g * TEXT : (g + 1) * TEXT, at] = (x * gain_ref[:, at]).astype(BF)
         squares = x * x
-        ssq = ssq + squares[:, :128] + squares[:, 128:]
-        left[0:rows, at] = (x * gain).astype(BF)
-        left[rows:, at] = (wp_ref[:, at].astype(F32) * gain).astype(BF)
-        tiles.append(x_ref[d, rows : rows + 16, 0:128].astype(F32)[0:8])
+        sums[g] = sums[g] + squares[:, :128] + squares[:, 128:]
+
+    for n, far in enumerate((0,) + HOPS):
+        for m, near in enumerate((0,) + HOPS):
+            ref, z, y = (f0, f1, f2, f3)[n], (z_here - far) & 3, (y_here - near) & 3
+            place(ref, m, 0, z, y)
+            tile = ref[m, TEXT : TEXT + 16, 0:128].astype(F32)[0:8]
+            lat[pl.ds(pl.multiple_of(8 * z, 8), 8), pl.ds(pl.multiple_of(128 * y, 128), 128)] = tile
+            place((t0, t1, t2, t3)[n], m, 1, (z_here - near) & 3, (y_here - far) & 3)
+    ssq = jnp.concatenate(sums, axis=0)
     inv = lax.rsqrt(jnp.sum(ssq, axis=1, keepdims=True) * (1.0 / D) + epsilon)
-    lat = [jnp.concatenate(tiles[4 * n : 4 * (n + 1)], axis=1) for n in range(4)]
-    block_ref[rows:, :] = jnp.concatenate(lat, axis=0).astype(BF)
+    block_ref[rows:, :] = lat[...].astype(BF)
     query = dot_nn(left[...], wq_ref[...])
-    qt_ref[...] = (query[0:rows] * (inv * (SCALE / LN2))).astype(BF)
-    mt_ref[:, 0:256] = query[rows:].astype(BF)
+    qt_ref[...] = (query * (inv * (SCALE / LN2))).astype(BF)
     key = dot_nn(left[...], wk_ref[...])
-    block_ref[0:rows, 0:256] = (key[0:rows] * inv).astype(BF)
-    mt_ref[:, 256:512] = key[rows:].astype(BF)
-    copy.wait()
+    block_ref[0:rows, 0:256] = (key * inv).astype(BF)
     value = dot_nn(left[...], wv_ref[...])
-    block_ref[0:rows, 256:512] = (value[0:rows] * inv).astype(BF)
-    mt_ref[:, 512:768] = value[rows:].astype(BF)
+    block_ref[0:rows, 256:512] = (value * inv).astype(BF)
 
 
 def fold_max(s):
@@ -351,49 +363,85 @@
     seats = lax.axis_size("seq")
     groups = lax.axis_size("dp")
     seat = lax.axis_index("seq").astype(jnp.int32).reshape(1)
+    group = lax.axis_index("dp").astype(jnp.int32).reshape(1)
+    side = SIDE
+    assert groups == side * side
+
+    def shift_y(x, k):
+        pairs = [(i, i // side * side + (i + k) % side) for i in range(groups)]
+        return lax.ppermute(x, "dp", pairs)
+
+    def shift_z(x, k):
+        return lax.ppermute(x, "dp", [(i, (i + side * k) % groups) for i in range(groups)])
+
     lat = latents.reshape(PDIM, PDIM)
     smem = pl.BlockSpec(memory_space=pltpu.SMEM)
     vmem = pl.BlockSpec(memory_space=pltpu.VMEM)
     hbm = pl.BlockSpec(memory_space=pltpu.HBM)
-    send, inv, u = pl.pallas_call(
+    first, second, inv, u, patch, gain = pl.pallas_call(
         pack_kernel,
         out_shape=(
-            jax.ShapeDtypeStruct((groups, SEND_ROWS, 256), BF),
+            jax.ShapeDtypeStruct((TEXT + 16, 256), BF),
+            jax.ShapeDtypeStruct((TEXT + 16, 256), BF),
             jax.ShapeDtypeStruct((PDIM, 128), F32),
             jax.ShapeDtypeStruct((PDIM, PDIM), F32),
+            jax.ShapeDtypeStruct((PDIM, D), BF),
+            jax.ShapeDtypeStruct((1, D), F32),
         ),
-        in_specs=[hbm, hbm, smem, hbm, hbm, hbm],
-        out_specs=(vmem,) * 3,
+        in_specs=[hbm, hbm, smem, hbm, hbm, hbm, hbm],
+        out_specs=(vmem,) * 6,
         scratch_shapes=[
             pltpu.SMEM((IMAGES,), jnp.int32),
             pltpu.SMEM((IMAGES,), jnp.int32),
             pltpu.VMEM((NSEQ, BLOCK, 256), BF),
             pltpu.VMEM((PDIM, PDIM), BF),
             pltpu.VMEM((PDIM, D), BF),
-            pltpu.SemaphoreType.DMA((5,)),
+            pltpu.SemaphoreType.DMA((6,)),
         ],
         compiler_params=pltpu.CompilerParams(vmem_limit_bytes=32 * 2**20),
         name="pack",
-    )(pinned(image_seq), pinned(image_start), seat, pinned(text_rows), pinned(lat), pinned(w_patch))
-    recv = lax.all_to_all(send, "dp", 0, 0)
-
-    qt, block, mt = pl.pallas_call(
+    )(
+        pinned(image_seq), pinned(image_start), seat, pinned(text_rows), pinned(lat), pinned(w_patch),
+        pinned(norm_gain.reshape(1, D)),
+    )
+    near = []
+    for k in HOPS:
+        near += [shift_y(first, k), shift_z(second, k)]
+    near = lax.optimization_barrier(tuple(near))
+    first_y, second_z = lax.optimization_barrier(
+        (jnp.stack((first,) + near[0::2]), jnp.stack((second,) + near[1::2]))
+    )
+    far = []
+    for k in HOPS:
+        far += [shift_z(first_y, k), shift_y(second_z, k)]
+    far = lax.optimization_barrier(tuple(far))
+    firsts = (first_y,) + far[0::2]
+    seconds = (second_z,) + far[1::2]
+    weight = jax.ShapeDtypeStruct((D, 256), BF)
+    wq, wk, wv, mt = pl.pallas_call(
+        fold_kernel,
+        out_shape=(weight, weight, weight, jax.ShapeDtypeStruct((PDIM, 768), BF)),
+        in_specs=[vmem] + [hbm] * 3,
+        out_specs=(vmem,) * 4,
+        scratch_shapes=[pltpu.SemaphoreType.DMA((3,))],
+        compiler_params=pltpu.CompilerParams(vmem_limit_bytes=32 * 2**20),
+        name="fold",
+    )(patch, pinned(w_query), pinned(w_key), pinned(w_value))
+    qt, block = pl.pallas_call(
         project_kernel,
         out_shape=(
             jax.ShapeDtypeStruct((NSEQ * TEXT, 256), BF),
             jax.ShapeDtypeStruct((KV_ROWS, 512), BF),
-            jax.ShapeDtypeStruct((PDIM, 768), BF),
         ),
-        in_specs=[vmem, vmem, vmem, hbm, vmem, vmem],
-        out_specs=(vmem,) * 3,
+        in_specs=[smem] + [vmem] * 12,
+        out_specs=(vmem,) * 2,
         scratch_shapes=[
-            pltpu.VMEM((NSEQ * TEXT + PDIM, D), BF),
-            pltpu.VMEM((D, 256), BF),
-            pltpu.SemaphoreType.DMA,
+            pltpu.VMEM((NSEQ * TEXT, D), BF),
+            pltpu.VMEM((PDIM, 512), F32),
         ],
-        compiler_params=pltpu.CompilerParams(vmem_limit_bytes=40 * 2**20),
+        compiler_params=pltpu.CompilerParams(vmem_limit_bytes=32 * 2**20),
         name="project",
-    )(recv, w_query, w_key, pinned(w_value), w_patch, norm_gain.reshape(1, D))
+    )(group, *firsts, *seconds, gain, wq, wk, wv)
     hops = [block] + [
         lax.ppermute(block, "seq", [(i, (i + 2 * k) % seats) for i in range(seats)])
         for k in range(1, seats // 2)

time: 99.6 us -> 95.5 us (0.959)
  blocking collectives: 61.7 us -> 27.8 us
  starting transfers between devices: 15.7 us -> 35.7 us
  waiting for transfers between devices: 5.24 us -> 12.6 us
  Pallas kernels: 15.2 us -> 17.7 us
    all_to_all x1 -> x0, blocking collectives: 37.3 us -> none  [on_device(): recv = lax.all_to_all(send, 'dp', 0, 0)]
    ppermute x0 -> x12, starting transfers between devices: none -> 16.3 us  [the longest x6 8.48 us: shift_y(): return lax.ppermute(x, 'dp', pairs)]
    ppermute x0 -> x12, waiting for transfers between devices: none -> 11.1 us  [the longest x6 8.95 us: shift_z(): lax.ppermute(x, 'dp', [(i, (i + side * k) % groups) for i in range(groups)])]
    ppermute x3, waiting for transfers between devices: 4.06 us -> 0.31 us  [on_device(): lax.ppermute(block, 'seq', [(i, (i + 2 * k) % seats) for i in range(seats)])]
    ppermute x4, starting transfers between devices: 12.1 us -> 15.8 us  [on_device(): lax.ppermute(hop, 'seq', [(i, i ^ 1) for i in range(seats)])]
    pallas_call x1 -> x2, Pallas kernels: 1.66 us -> 5.16 us  [the longest x1 3.57 us: on_device(): pl.pallas_call(fold_kernel, out_shape=(weight, weight, weight, jax.ShapeD...]
    all_to_all x1, blocking collectives: 24.4 us -> 27.8 us  [on_device(): lax.all_to_all(z.reshape(groups * seats, 8, 128), ('dp', 'seq'), 0, 0)]
  transfers between devices with their start and end apart: 7 -> 19, of which waited for: 3 -> 10; matrix products, arithmetic and copies ran while one was open for 0% -> 0% of each run, Pallas kernels for 0% -> 4%
where the time goes in v4:
time: 95.5 us; the launch traced here: 95.3 us
  starting transfers between devices  35.7 us (37%)
  blocking collectives  27.8 us (29%)
  Pallas kernels  17.7 us (19%)
  waiting for transfers between devices  12.6 us (13%)
    all_to_all x1, blocking collectives, on_device(): lax.all_to_all(z.reshape(groups * seats, 8, 128), ('dp', 'seq'), 0, 0)  27.8 us
    ppermute x4, starting transfers between devices, on_device(): lax.ppermute(hop, 'seq', [(i, i ^ 1) for i in range(seats)])  15.8 us
    ppermute x6, waiting for transfers between devices, shift_z(): lax.ppermute(x, 'dp', [(i, (i + side * k) % groups) for i in range(groups)])  8.95 us
    pallas_call x1, Pallas kernels, attend(): pl.pallas_call(attend_kernel, out_shape=(jax.ShapeDtypeStruct((NSEQ, BLOC...  8.95 us
    ppermute x6, starting transfers between devices, shift_y(): return lax.ppermute(x, 'dp', pairs)  8.48 us
    ppermute x6, starting transfers between devices, shift_z(): lax.ppermute(x, 'dp', [(i, (i + side * k) % groups) for i in range(groups)])  7.78 us
    ppermute x3, starting transfers between devices, on_device(): lax.ppermute(block, 'seq', [(i, (i + 2 * k) % seats) for i in range(seats)])  3.67 us
    pallas_call x1, Pallas kernels, on_device(): pl.pallas_call(fold_kernel, out_shape=(weight, weight, weight, jax.ShapeD...  3.57 us
  transfers between devices with their start and end apart: 19, of which 10 were waited for; matrix products, arithmetic and copies ran while one was open for 0% of the time, Pallas kernels for 4%

profile of v4, /device:TPU:1, one launch (start us, length us, event | category | flops | bytes accessed | tf_op | source)
XLA Modules:
  0.0 95.3 jit_solution(17900873829348090888)
XLA Ops:
  0.6 1.6 %pack.1 = (bf16[144,256]{1,0:T(8,128)(2,1)S(1)}, bf16[144,256]{1,0:T(8,128)(2,1)S(1)}, f32[32,128]{1,0:T(8,128)S(1)}, f32[32,32]{1,0:T(8,128)S(1)}, bf16[32,4096]{1,0:T(8,128)(2,1)S(1)}, /*index=5*/f32[1,4096]{1,0:T(1,128)S(1)}) custom-call(s32[16]{0:T(128)} %seq_hbm.3, s32[16]{0:T(128)} %start_hbm.3, s32[1]{0:T(128)} %bitcast.seat_ref, ...), custom_call_target="tpu_custom_call" | custom-call | tf_op jit(solution)/shard_map/pack/pallas_call | solution.py:381
  2.2 3.8 %collective-permute-start.4 = (bf16[144,256]{1,0:T(8,128)(2,1)S(1)}, bf16[144,256]{1,0:T(8,128)(2,1)S(1)}, u32[]{:S(2)}, u32[]{:S(2)}) collective-permute-start(bf16[144,256]{1,0:T(8,128)(2,1)S(1)} %get-tuple-element.30), channel_id=1, source_target_pairs={{0,2},{1,3},{2,0},{3,1},{4,6},{5,7},{6,4},{7,5},{8,10},{9,11},{10,... | collective-permute-start | bytes 221192 | tf_op jit(solution)/shard_map/ppermute | solution.py:372
  6.1 0.8 collective-permute-start.2
  6.8 0.7 collective-permute-start
  7.5 3.6 %collective-permute-start.5 = (bf16[144,256]{1,0:T(8,128)(2,1)S(1)}, bf16[144,256]{1,0:T(8,128)(2,1)S(1)}, u32[]{:S(2)}, u32[]{:S(2)}) collective-permute-start(bf16[144,256]{1,0:T(8,128)(2,1)S(1)} %get-tuple-element.31), channel_id=1, source_target_pairs={{0,8},{1,9},{2,10},{3,11},{4,12},{5,13},{6,14},{7,15},{8,0},{9,1},... | collective-permute-start | bytes 221192 | tf_op jit(solution)/shard_map/ppermute | solution.py:375
  11.1 0.4 collective-permute-start.3
  11.6 0.0 collective-permute-done.4
  11.6 1.0 %collective-permute-start.1 = (bf16[144,256]{1,0:T(8,128)(2,1)S(1)}, bf16[144,256]{1,0:T(8,128)(2,1)S(1)}, u32[]{:S(2)}, u32[]{:S(2)}) collective-permute-start(bf16[144,256]{1,0:T(8,128)(2,1)S(1)} %get-tuple-element.31), channel_id=1, source_target_pairs={{0,4},{1,5},{2,6},{3,7},{4,8},{5,9},{6,10},{7,11},{8,12},{9,13},{1... | collective-permute-start | bytes 221192 | tf_op jit(solution)/shard_map/ppermute | solution.py:375
  12.6 0.0 collective-permute-done.2
  12.6 0.0 collective-permute-done
  12.6 0.3 collective-permute-done.5
  12.9 1.8 %collective-permute-done.3 = bf16[144,256]{1,0:T(8,128)(2,1)S(1)} collective-permute-done((bf16[144,256]{1,0:T(8,128)(2,1)S(1)}, bf16[144,256]{1,0:T(8,128)(2,1)S(1)}, u32[]{:S(2)}, u32[]{:S(2)}) %collective-permute-start.3) | collective-permute-done | bytes 73760 | tf_op jit(solution)/shard_map/ppermute | solution.py:375
  14.7 1.3 %collective-permute-done.1 = bf16[144,256]{1,0:T(8,128)(2,1)S(1)} collective-permute-done((bf16[144,256]{1,0:T(8,128)(2,1)S(1)}, bf16[144,256]{1,0:T(8,128)(2,1)S(1)}, u32[]{:S(2)}, u32[]{:S(2)}) %collective-permute-start.1) | collective-permute-done | bytes 73760 | tf_op jit(solution)/shard_map/ppermute | solution.py:375
  16.0 0.1 pad_maximum_fusion
  16.1 1.3 %collective-permute-start.10 = (bf16[4,144,256]{2,1,0:T(8,128)(2,1)S(1)}, bf16[4,144,256]{2,1,0:T(8,128)(2,1)S(1)}, u32[]{:S(2)}, u32[]{:S(2)}) collective-permute-start(bf16[4,144,256]{2,1,0:T(8,128)(2,1)S(1)} %get-tuple-element.38.f0), channel_id=1, source_target_pairs={{0,8},{1,9},{2,10},{3,11},{4,12},{5,13},{6,14},{7,15},{8,0},{9,1},... | collective-permute-start | bytes 884744 | tf_op jit(solution)/shard_map/ppermute | solution.py:375
  17.3 1.4 %collective-permute-start.8 = (bf16[4,144,256]{2,1,0:T(8,128)(2,1)S(1)}, bf16[4,144,256]{2,1,0:T(8,128)(2,1)S(1)}, u32[]{:S(2)}, u32[]{:S(2)}) collective-permute-start(bf16[4,144,256]{2,1,0:T(8,128)(2,1)S(1)} %get-tuple-element.38.f0), channel_id=1, source_target_pairs={{0,12},{1,13},{2,14},{3,15},{4,0},{5,1},{6,2},{7,3},{8,4},{9,5},{1... | collective-permute-start | bytes 884744 | tf_op jit(solution)/shard_map/ppermute | solution.py:375
  18.7 0.1 collective-permute-start.6
  18.8 1.2 %collective-permute-start.11 = (bf16[4,144,256]{2,1,0:T(8,128)(2,1)S(1)}, bf16[4,144,256]{2,1,0:T(8,128)(2,1)S(1)}, u32[]{:S(2)}, u32[]{:S(2)}) collective-permute-start(bf16[4,144,256]{2,1,0:T(8,128)(2,1)S(1)} %get-tuple-element.39.t0), channel_id=1, source_target_pairs={{0,2},{1,3},{2,0},{3,1},{4,6},{5,7},{6,4},{7,5},{8,10},{9,11},{10,... | collective-permute-start | bytes 884744 | tf_op jit(solution)/shard_map/ppermute | solution.py:372
  19.9 1.6 %collective-permute-start.9 = (bf16[4,144,256]{2,1,0:T(8,128)(2,1)S(1)}, bf16[4,144,256]{2,1,0:T(8,128)(2,1)S(1)}, u32[]{:S(2)}, u32[]{:S(2)}) collective-permute-start(bf16[4,144,256]{2,1,0:T(8,128)(2,1)S(1)} %get-tuple-element.39.t0), channel_id=1, source_target_pairs={{0,3},{1,0},{2,1},{3,2},{4,7},{5,4},{6,5},{7,6},{8,11},{9,8},{10,9... | collective-permute-start | bytes 884744 | tf_op jit(solution)/shard_map/ppermute | solution.py:372
  21.6 1.7 %collective-permute-done.10.f3 = bf16[4,144,256]{2,1,0:T(8,128)(2,1)S(1)} collective-permute-done((bf16[4,144,256]{2,1,0:T(8,128)(2,1)S(1)}, bf16[4,144,256]{2,1,0:T(8,128)(2,1)S(1)}, u32[]{:S(2)}, u32[]{:S(2)}) %collective-permute-start.10) | collective-permute-done | bytes 294944 | tf_op jit(solution)/shard_map/ppermute | solution.py:375
  23.3 0.4 collective-permute-start.7
  23.7 3.6 %fold.1 = (bf16[4096,256]{1,0:T(8,128)(2,1)S(1)}, bf16[4096,256]{1,0:T(8,128)(2,1)S(1)}, bf16[4096,256]{1,0:T(8,128)(2,1)S(1)}, bf16[32,768]{1,0:T(8,128)(2,1)S(1)}) custom-call(bf16[32,4096]{1,0:T(8,128)(2,1)S(1)} %get-tuple-element.47.patch_ref, bf16[4096,256]{1,0:T(8,128)(2,1)} %wq_hbm.1, bf16[4096,256]{1,0:T(8,128)(2,1)} %wk_hbm.1, bf16[4096,256]{1,0:T(8,128)(2,1)} %wv_hbm.1), custom_call_target="tpu_custom_call" | custom-call | tf_op jit(solution)/shard_map/fold/pallas_call | solution.py:421
  27.3 2.5 %collective-permute-done.8.f2 = bf16[4,144,256]{2,1,0:T(8,128)(2,1)S(1)} collective-permute-done((bf16[4,144,256]{2,1,0:T(8,128)(2,1)S(1)}, bf16[4,144,256]{2,1,0:T(8,128)(2,1)S(1)}, u32[]{:S(2)}, u32[]{:S(2)}) %collective-permute-start.8) | collective-permute-done | bytes 294944 | tf_op jit(solution)/shard_map/ppermute | solution.py:375
  29.8 1.4 %collective-permute-done.6.f1 = bf16[4,144,256]{2,1,0:T(8,128)(2,1)S(1)} collective-permute-done((bf16[4,144,256]{2,1,0:T(8,128)(2,1)S(1)}, bf16[4,144,256]{2,1,0:T(8,128)(2,1)S(1)}, u32[]{:S(2)}, u32[]{:S(2)}) %collective-permute-start.6) | collective-permute-done | bytes 294944 | tf_op jit(solution)/shard_map/ppermute | solution.py:375
  31.1 0.0 collective-permute-done.11.t3
  31.1 1.5 %collective-permute-done.9.t2 = bf16[4,144,256]{2,1,0:T(8,128)(2,1)S(1)} collective-permute-done((bf16[4,144,256]{2,1,0:T(8,128)(2,1)S(1)}, bf16[4,144,256]{2,1,0:T(8,128)(2,1)S(1)}, u32[]{:S(2)}, u32[]{:S(2)}) %collective-permute-start.9) | collective-permute-done | bytes 294944 | tf_op jit(solution)/shard_map/ppermute | solution.py:372
  32.6 0.6 collective-permute-done.7.t1
  33.2 2.5 %project.1 = (bf16[256,256]{1,0:T(8,128)(2,1)S(1)}, bf16[288,512]{1,0:T(8,128)(2,1)S(1)}) custom-call(s32[1]{0:T(128)} %bitcast.1.group_ref, bf16[4,144,256]{2,1,0:T(8,128)(2,1)S(1)} %get-tuple-element.38.f0, bf16[4,144,256]{2,1,0:T(8,128)(2,1)S(1)} %collective-permute-done.6.f1, bf16[4,144,256]{2,1,0:T(8,128)(2,1)S(1)} %collective-permute-done.8.f2, ...), custom_call_target="tpu_custom_call" | custom-call | tf_op jit(solution)/shard_map/project/pallas_call | solution.py:430
  35.8 0.0 copy-start
  35.8 2.5 %collective-permute-start.14 = (bf16[288,512]{1,0:T(8,128)(2,1)S(1)}, bf16[288,512]{1,0:T(8,128)(2,1)S(1)}, u32[]{:S(2)}, u32[]{:S(2)}) collective-permute-start(bf16[288,512]{1,0:T(8,128)(2,1)S(1)} %get-tuple-element.51.s0), channel_id=1, source_target_pairs={{0,96},{16,112},{32,0},{48,16},{64,32},{80,48},{96,64},{112,80},{1... | collective-permute-start | bytes 884744 | tf_op jit(solution)/shard_map/ppermute | solution.py:446
  38.3 0.5 collective-permute-start.13
  38.8 0.6 collective-permute-start.12
  39.4 5.8 %collective-permute-start.15 = (bf16[288,512]{1,0:T(8,128)(2,1)S(1)}, bf16[288,512]{1,0:T(8,128)(2,1)S(1)}, u32[]{:S(2)}, u32[]{:S(2)}) collective-permute-start(bf16[288,512]{1,0:T(8,128)(2,1)S(1)} %get-tuple-element.51.s0), channel_id=1, source_target_pairs={{0,16},{16,0},{32,48},{48,32},{64,80},{80,64},{96,112},{112,96},{1... | collective-permute-start | bytes 884744 | tf_op jit(solution)/shard_map/ppermute | solution.py:449
  45.2 0.3 collective-permute-done.14.s3
  45.5 6.3 %collective-permute-start.18 = (bf16[288,512]{1,0:T(8,128)(2,1)S(1)}, bf16[288,512]{1,0:T(8,128)(2,1)S(1)}, u32[]{:S(2)}, u32[]{:S(2)}) collective-permute-start(bf16[288,512]{1,0:T(8,128)(2,1)S(1)} %collective-permute-done.14.s3), channel_id=1, source_target_pairs={{0,16},{16,0},{32,48},{48,32},{64,80},{80,64},{96,112},{112,96},{1... | collective-permute-start | bytes 884744 | tf_op jit(solution)/shard_map/ppermute | solution.py:449
  51.9 0.0 collective-permute-done.13.s2
  51.9 0.7 collective-permute-start.17
  52.5 0.0 collective-permute-done.12.s1
  52.5 3.0 %collective-permute-start.16 = (bf16[288,512]{1,0:T(8,128)(2,1)S(1)}, bf16[288,512]{1,0:T(8,128)(2,1)S(1)}, u32[]{:S(2)}, u32[]{:S(2)}) collective-permute-start(bf16[288,512]{1,0:T(8,128)(2,1)S(1)} %collective-permute-done.12.s1), channel_id=1, source_target_pairs={{0,16},{16,0},{32,48},{48,32},{64,80},{80,64},{96,112},{112,96},{1... | collective-permute-start | bytes 884744 | tf_op jit(solution)/shard_map/ppermute | solution.py:449
  55.6 0.0 collective-permute-done.15.o0
  55.6 0.0 collective-permute-done.18.o3
  55.6 0.0 collective-permute-done.17.o2
  55.6 1.2 %collective-permute-done.16.o1 = bf16[288,512]{1,0:T(8,128)(2,1)S(1)} collective-permute-done((bf16[288,512]{1,0:T(8,128)(2,1)S(1)}, bf16[288,512]{1,0:T(8,128)(2,1)S(1)}, u32[]{:S(2)}, u32[]{:S(2)}) %collective-permute-start.16) | collective-permute-done | bytes 294944 | tf_op jit(solution)/shard_map/ppermute | solution.py:449
  56.8 0.0 copy-done.2
  56.8 0.7 copy-done.3
  57.5 8.9 %attend.1 = (bf16[2,384,256]{2,1,0:T(8,128)(2,1)}, bf16[16,64,128]{2,1,0:T(8,128)(2,1)S(1)}) custom-call(s32[16]{0:T(128)} %seq_hbm.3, s32[16]{0:T(128)} %start_hbm.3, s32[1]{0:T(128)} %bitcast.seat_ref, bf16[288,512]{1,0:T(8,128)(2,1)S(1)} %get-tuple-element.51.s0, bf16[288,512]{1,0:T(8,128)(2,1)S(1)} %collective-permute-done.12.s1, ...), custom_call_target="tpu_custom_call" | custom-call | tf_op jit(solution)/shard_map/attend/pallas_call | solution.py:316
  66.4 27.8 %all_to_all.5.recv_ref = bf16[128,8,128]{2,1,0:T(8,128)(2,1)S(1)} all-to-all(bf16[128,8,128]{2,1,0:T(8,128)(2,1)S(1)} %bitcast.14), channel_id=1, replica_groups=mesh['seq'=8,'dp'=16] {'dp','seq'}, dimensions={0} | all-to-all | bytes 524288 | tf_op jit(solution)/shard_map/all_to_all | solution.py:451
  94.2 1.1 %finish.1 = f32[32,32]{1,0:T(8,128)} custom-call(bf16[128,8,128]{2,1,0:T(8,128)(2,1)S(1)} %all_to_all.5.recv_ref, bf16[32,32]{1,0:T(8,128)(2,1)S(1)} %bitcast.18, f32[32,128]{1,0:T(8,128)S(1)} %get-tuple-element.56.inv_ref, f32[32,32]{1,0:T(8,128)S(1)} %get-tuple-element.57.u_ref), custom_call_target="tpu_custom_call" | custom-call | tf_op jit(solution)/shard_map/finish/pallas_call | solution.py:452
  (5 shorter events, 0.0 us)
Async XLA Ops:
  2.2 9.3 %collective-permute-start.4 = (bf16[144,256]{1,0:T(8,128)(2,1)S(1)}, bf16[144,256]{1,0:T(8,128)(2,1)S(1)}, u32[]{:S(2)}, u32[]{:S(2)}) collective-permute-start(bf16[144,256]{1,0:T(8,128)(2,1)S(1)} %get-tuple-element.30), channel_id=1, source_target_pairs={{0,2},{1,3},{2,0},{3,1},{4,6},{5,7},{6,4},{7,5},{8,10},{9,11},{10,... | collective-permute-start | bytes 221192 | tf_op jit(solution)/shard_map/ppermute | solution.py:372
  6.1 6.5 %collective-permute-start.2 = (bf16[144,256]{1,0:T(8,128)(2,1)S(1)}, bf16[144,256]{1,0:T(8,128)(2,1)S(1)}, u32[]{:S(2)}, u32[]{:S(2)}) collective-permute-start(bf16[144,256]{1,0:T(8,128)(2,1)S(1)} %get-tuple-element.30), channel_id=1, source_target_pairs={{0,3},{1,0},{2,1},{3,2},{4,7},{5,4},{6,5},{7,6},{8,11},{9,8},{10,9... | collective-permute-start | bytes 221192 | tf_op jit(solution)/shard_map/ppermute | solution.py:372
  6.8 5.8 %collective-permute-start = (bf16[144,256]{1,0:T(8,128)(2,1)S(1)}, bf16[144,256]{1,0:T(8,128)(2,1)S(1)}, u32[]{:S(2)}, u32[]{:S(2)}) collective-permute-start(bf16[144,256]{1,0:T(8,128)(2,1)S(1)} %get-tuple-element.30), channel_id=1, source_target_pairs={{0,1},{1,2},{2,3},{3,0},{4,5},{5,6},{6,7},{7,4},{8,9},{9,10},{10,1... | collective-permute-start | bytes 221192 | tf_op jit(solution)/shard_map/ppermute | solution.py:372
  7.5 5.3 %collective-permute-start.5 = (bf16[144,256]{1,0:T(8,128)(2,1)S(1)}, bf16[144,256]{1,0:T(8,128)(2,1)S(1)}, u32[]{:S(2)}, u32[]{:S(2)}) collective-permute-start(bf16[144,256]{1,0:T(8,128)(2,1)S(1)} %get-tuple-element.31), channel_id=1, source_target_pairs={{0,8},{1,9},{2,10},{3,11},{4,12},{5,13},{6,14},{7,15},{8,0},{9,1},... | collective-permute-start | bytes 221192 | tf_op jit(solution)/shard_map/ppermute | solution.py:375
  11.1 3.6 %collective-permute-start.3 = (bf16[144,256]{1,0:T(8,128)(2,1)S(1)}, bf16[144,256]{1,0:T(8,128)(2,1)S(1)}, u32[]{:S(2)}, u32[]{:S(2)}) collective-permute-start(bf16[144,256]{1,0:T(8,128)(2,1)S(1)} %get-tuple-element.31), channel_id=1, source_target_pairs={{0,12},{1,13},{2,14},{3,15},{4,0},{5,1},{6,2},{7,3},{8,4},{9,5},{1... | collective-permute-start | bytes 221192 | tf_op jit(solution)/shard_map/ppermute | solution.py:375
  11.6 4.4 %collective-permute-start.1 = (bf16[144,256]{1,0:T(8,128)(2,1)S(1)}, bf16[144,256]{1,0:T(8,128)(2,1)S(1)}, u32[]{:S(2)}, u32[]{:S(2)}) collective-permute-start(bf16[144,256]{1,0:T(8,128)(2,1)S(1)} %get-tuple-element.31), channel_id=1, source_target_pairs={{0,4},{1,5},{2,6},{3,7},{4,8},{5,9},{6,10},{7,11},{8,12},{9,13},{1... | collective-permute-start | bytes 221192 | tf_op jit(solution)/shard_map/ppermute | solution.py:375
  16.1 7.3 %collective-permute-start.10 = (bf16[4,144,256]{2,1,0:T(8,128)(2,1)S(1)}, bf16[4,144,256]{2,1,0:T(8,128)(2,1)S(1)}, u32[]{:S(2)}, u32[]{:S(2)}) collective-permute-start(bf16[4,144,256]{2,1,0:T(8,128)(2,1)S(1)} %get-tuple-element.38.f0), channel_id=1, source_target_pairs={{0,8},{1,9},{2,10},{3,11},{4,12},{5,13},{6,14},{7,15},{8,0},{9,1},... | collective-permute-start | bytes 884744 | tf_op jit(solution)/shard_map/ppermute | solution.py:375
  17.3 12.4 %collective-permute-start.8 = (bf16[4,144,256]{2,1,0:T(8,128)(2,1)S(1)}, bf16[4,144,256]{2,1,0:T(8,128)(2,1)S(1)}, u32[]{:S(2)}, u32[]{:S(2)}) collective-permute-start(bf16[4,144,256]{2,1,0:T(8,128)(2,1)S(1)} %get-tuple-element.38.f0), channel_id=1, source_target_pairs={{0,12},{1,13},{2,14},{3,15},{4,0},{5,1},{6,2},{7,3},{8,4},{9,5},{1... | collective-permute-start | bytes 884744 | tf_op jit(solution)/shard_map/ppermute | solution.py:375
  18.7 12.4 %collective-permute-start.6 = (bf16[4,144,256]{2,1,0:T(8,128)(2,1)S(1)}, bf16[4,144,256]{2,1,0:T(8,128)(2,1)S(1)}, u32[]{:S(2)}, u32[]{:S(2)}) collective-permute-start(bf16[4,144,256]{2,1,0:T(8,128)(2,1)S(1)} %get-tuple-element.38.f0), channel_id=1, source_target_pairs={{0,4},{1,5},{2,6},{3,7},{4,8},{5,9},{6,10},{7,11},{8,12},{9,13},{1... | collective-permute-start | bytes 884744 | tf_op jit(solution)/shard_map/ppermute | solution.py:375
  18.8 12.3 %collective-permute-start.11 = (bf16[4,144,256]{2,1,0:T(8,128)(2,1)S(1)}, bf16[4,144,256]{2,1,0:T(8,128)(2,1)S(1)}, u32[]{:S(2)}, u32[]{:S(2)}) collective-permute-start(bf16[4,144,256]{2,1,0:T(8,128)(2,1)S(1)} %get-tuple-element.39.t0), channel_id=1, source_target_pairs={{0,2},{1,3},{2,0},{3,1},{4,6},{5,7},{6,4},{7,5},{8,10},{9,11},{10,... | collective-permute-start | bytes 884744 | tf_op jit(solution)/shard_map/ppermute | solution.py:372
  19.9 12.7 %collective-permute-start.9 = (bf16[4,144,256]{2,1,0:T(8,128)(2,1)S(1)}, bf16[4,144,256]{2,1,0:T(8,128)(2,1)S(1)}, u32[]{:S(2)}, u32[]{:S(2)}) collective-permute-start(bf16[4,144,256]{2,1,0:T(8,128)(2,1)S(1)} %get-tuple-element.39.t0), channel_id=1, source_target_pairs={{0,3},{1,0},{2,1},{3,2},{4,7},{5,4},{6,5},{7,6},{8,11},{9,8},{10,9... | collective-permute-start | bytes 884744 | tf_op jit(solution)/shard_map/ppermute | solution.py:372
  23.3 9.9 %collective-permute-start.7 = (bf16[4,144,256]{2,1,0:T(8,128)(2,1)S(1)}, bf16[4,144,256]{2,1,0:T(8,128)(2,1)S(1)}, u32[]{:S(2)}, u32[]{:S(2)}) collective-permute-start(bf16[4,144,256]{2,1,0:T(8,128)(2,1)S(1)} %get-tuple-element.39.t0), channel_id=1, source_target_pairs={{0,1},{1,2},{2,3},{3,0},{4,5},{5,6},{6,7},{7,4},{8,9},{9,10},{10,1... | collective-permute-start | bytes 884744 | tf_op jit(solution)/shard_map/ppermute | solution.py:372
  35.8 58.5 %copy-start = (bf16[1,32,32]{2,1,0:T(8,128)(2,1)S(1)}, bf16[1,32,32]{2,1,0:T(8,128)(2,1)}, u32[]{:S(2)}) copy-start(bf16[1,32,32]{2,1,0:T(8,128)(2,1)} %param.11) | copy-start | bytes 6148
  35.8 9.8 %collective-permute-start.14 = (bf16[288,512]{1,0:T(8,128)(2,1)S(1)}, bf16[288,512]{1,0:T(8,128)(2,1)S(1)}, u32[]{:S(2)}, u32[]{:S(2)}) collective-permute-start(bf16[288,512]{1,0:T(8,128)(2,1)S(1)} %get-tuple-element.51.s0), channel_id=1, source_target_pairs={{0,96},{16,112},{32,0},{48,16},{64,32},{80,48},{96,64},{112,80},{1... | collective-permute-start | bytes 884744 | tf_op jit(solution)/shard_map/ppermute | solution.py:446
  38.3 13.6 %collective-permute-start.13 = (bf16[288,512]{1,0:T(8,128)(2,1)S(1)}, bf16[288,512]{1,0:T(8,128)(2,1)S(1)}, u32[]{:S(2)}, u32[]{:S(2)}) collective-permute-start(bf16[288,512]{1,0:T(8,128)(2,1)S(1)} %get-tuple-element.51.s0), channel_id=1, source_target_pairs={{0,64},{16,80},{32,96},{48,112},{64,0},{80,16},{96,32},{112,48},{1... | collective-permute-start | bytes 884744 | tf_op jit(solution)/shard_map/ppermute | solution.py:446
  38.8 13.7 %collective-permute-start.12 = (bf16[288,512]{1,0:T(8,128)(2,1)S(1)}, bf16[288,512]{1,0:T(8,128)(2,1)S(1)}, u32[]{:S(2)}, u32[]{:S(2)}) collective-permute-start(bf16[288,512]{1,0:T(8,128)(2,1)S(1)} %get-tuple-element.51.s0), channel_id=1, source_target_pairs={{0,32},{16,48},{32,64},{48,80},{64,96},{80,112},{96,0},{112,16},{1... | collective-permute-start | bytes 884744 | tf_op jit(solution)/shard_map/ppermute | solution.py:446
  39.4 16.1 %collective-permute-start.15 = (bf16[288,512]{1,0:T(8,128)(2,1)S(1)}, bf16[288,512]{1,0:T(8,128)(2,1)S(1)}, u32[]{:S(2)}, u32[]{:S(2)}) collective-permute-start(bf16[288,512]{1,0:T(8,128)(2,1)S(1)} %get-tuple-element.51.s0), channel_id=1, source_target_pairs={{0,16},{16,0},{32,48},{48,32},{64,80},{80,64},{96,112},{112,96},{1... | collective-permute-start | bytes 884744 | tf_op jit(solution)/shard_map/ppermute | solution.py:449
  45.5 10.0 %collective-permute-start.18 = (bf16[288,512]{1,0:T(8,128)(2,1)S(1)}, bf16[288,512]{1,0:T(8,128)(2,1)S(1)}, u32[]{:S(2)}, u32[]{:S(2)}) collective-permute-start(bf16[288,512]{1,0:T(8,128)(2,1)S(1)} %collective-permute-done.14.s3), channel_id=1, source_target_pairs={{0,16},{16,0},{32,48},{48,32},{64,80},{80,64},{96,112},{112,96},{1... | collective-permute-start | bytes 884744 | tf_op jit(solution)/shard_map/ppermute | solution.py:449
  51.9 3.7 %collective-permute-start.17 = (bf16[288,512]{1,0:T(8,128)(2,1)S(1)}, bf16[288,512]{1,0:T(8,128)(2,1)S(1)}, u32[]{:S(2)}, u32[]{:S(2)}) collective-permute-start(bf16[288,512]{1,0:T(8,128)(2,1)S(1)} %collective-permute-done.13.s2), channel_id=1, source_target_pairs={{0,16},{16,0},{32,48},{48,32},{64,80},{80,64},{96,112},{112,96},{1... | collective-permute-start | bytes 884744 | tf_op jit(solution)/shard_map/ppermute | solution.py:449
  52.5 4.2 %collective-permute-start.16 = (bf16[288,512]{1,0:T(8,128)(2,1)S(1)}, bf16[288,512]{1,0:T(8,128)(2,1)S(1)}, u32[]{:S(2)}, u32[]{:S(2)}) collective-permute-start(bf16[288,512]{1,0:T(8,128)(2,1)S(1)} %collective-permute-done.12.s1), channel_id=1, source_target_pairs={{0,16},{16,0},{32,48},{48,32},{64,80},{80,64},{96,112},{112,96},{1... | collective-permute-start | bytes 884744 | tf_op jit(solution)/shard_map/ppermute | solution.py:449
  55.6 1.2 %copy-start.1 = (bf16[288,512]{1,0:T(8,128)(2,1)}, bf16[288,512]{1,0:T(8,128)(2,1)S(1)}, u32[]{:S(2)}) copy-start(bf16[288,512]{1,0:T(8,128)(2,1)S(1)} %collective-permute-done.18.o3) | copy-start | bytes 884740
  55.6 1.2 %copy-start.2 = (bf16[288,512]{1,0:T(8,128)(2,1)}, bf16[288,512]{1,0:T(8,128)(2,1)S(1)}, u32[]{:S(2)}) copy-start(bf16[288,512]{1,0:T(8,128)(2,1)S(1)} %collective-permute-done.17.o2) | copy-start | bytes 884740
  56.8 0.7 copy-start.3

commit v5 on v4

--- a/solution.py
+++ b/solution.py
@@ -79,7 +79,6 @@
         high = text_ref[g, PATCHES:BLOCK, :].astype(F32)
         ref[0:TEXT, :] = jnp.where(row < offs[g], low, high).astype(BF)
     first_ref[TEXT:, :] = tail
-    second_ref[TEXT:, :] = jnp.zeros((16, 256), BF)
     copies[5].wait()
     patch_ref[...] = (wp.astype(F32) * gain_ref[...]).astype(BF)
 
@@ -95,9 +94,9 @@
 
 
 def project_kernel(
-    group_ref, f0, f1, f2, f3, t0, t1, t2, t3, gain_ref, wq_ref, wk_ref, wv_ref,
-    qt_ref, block_ref,
-    left, lat,
+    group_ref, f0, f1, f2, f3, t0, t1, t2, t3, gain_ref, wk_ref, wv_ref,
+    block_ref, left, inv_ref,
+    lat,
 ):
     rows = NSEQ * TEXT
     z_here, y_here = group_ref[0] >> 2, group_ref[0] & 3
@@ -120,12 +119,16 @@
     ssq = jnp.concatenate(sums, axis=0)
     inv = lax.rsqrt(jnp.sum(ssq, axis=1, keepdims=True) * (1.0 / D) + epsilon)
     block_ref[rows:, :] = lat[...].astype(BF)
-    query = dot_nn(left[...], wq_ref[...])
-    qt_ref[...] = (query * (inv * (SCALE / LN2))).astype(BF)
+    inv_ref[...] = jnp.broadcast_to(inv, inv_ref.shape)
     key = dot_nn(left[...], wk_ref[...])
     block_ref[0:rows, 0:256] = (key * inv).astype(BF)
     value = dot_nn(left[...], wv_ref[...])
     block_ref[0:rows, 256:512] = (value * inv).astype(BF)
+
+
+def query_kernel(left, inv_ref, wq_ref, qt_ref):
+    query = dot_nn(left[...], wq_ref[...])
+    qt_ref[...] = (query * (inv_ref[:, 0:1] * (SCALE / LN2))).astype(BF)
 
 
 def fold_max(s):
@@ -190,6 +193,8 @@
         labels[seq_ref[i] * 8 + lax.div(start_ref[i], BLOCK)] = i
     rows = lax.broadcasted_iota(jnp.int32, (BLOCK, BLOCK), 0)
     cols = lax.broadcasted_iota(jnp.int32, (BLOCK, BLOCK), 1)
+    down = lax.broadcasted_iota(jnp.int32, (BLOCK, 1), 0)
+    across = lax.broadcasted_iota(jnp.int32, (1, BLOCK), 1)
     for g in range(NSEQ):
         own_tile = tiles[labels[g * 8 + seat]].astype(BF)
         in_order = jnp.concatenate([tiles[labels[g * 8 + b]] for b in range(8)], axis=0).astype(BF)
@@ -206,7 +211,7 @@
         q_s[g, PATCHES:, :] = qt_ref[g * TEXT : (g + 1) * TEXT, :]
     copies[2].wait()
     for g in range(NSEQ):
-        place = jnp.where(cols == position(rows, offs[g]), 1.0, 0.0).astype(BF)
+        place = jnp.where(cols == position(down, offs[g]), 1.0, 0.0).astype(BF)
         g_s[g] = dot_nn(place, grad_ref[g]).astype(BF)
 
     def each(count, body):
@@ -216,20 +221,20 @@
 
         lax.fori_loop(0, count, step, 0)
 
-    q_row = lax.broadcasted_iota(jnp.int32, (BLOCK, 2 * BLOCK), 0)
-    k_col = lax.broadcasted_iota(jnp.int32, (BLOCK, 2 * BLOCK), 1)
+    k_col = lax.broadcasted_iota(jnp.int32, (1, 2 * BLOCK), 1)
     in_image = k_col < 2 * PATCHES
     second = jnp.where(in_image, k_col >> 8, (k_col - 2 * PATCHES) >> 7)
     k_row = jnp.where(in_image, k_col & (PATCHES - 1), PATCHES + (k_col & (TEXT - 1)))
+    seen = []
+    for off in offs:
+        reach = jnp.where(down < PATCHES, off + (PATCHES - 1), position(down, off))
+        seen.append((position(k_row, off) + BLOCK * (second - core), reach))
 
     def score(p, diagonal=False):
         for n, (g, h) in enumerate(CHAINS):
             s = dot_nt(q_s[g, :, heads(h)], keys[g, p, :, heads(h)])
             if diagonal:
-                off = offs[g]
-                reach = jnp.where(q_row < PATCHES, off + (PATCHES - 1), position(q_row, off))
-                place = position(k_row, off) + BLOCK * (second - core)
-                s = jnp.where(place <= reach, s, -jnp.inf)
+                s = jnp.where(seen[g][0] <= seen[g][1], s, -jnp.inf)
                 m_s[n] = fold_max(s)
             else:
                 m_s[n] = jnp.maximum(m_s[n], fold_max(s))
@@ -273,7 +278,7 @@
             x.append(dot_nt(mv, scaled).astype(BF))
         xs.append(jnp.concatenate(x, axis=1))
         out_c = jnp.concatenate(outs, axis=1)
-        back = jnp.where(rows == position(cols, offs[g]), 1.0, 0.0).astype(BF)
+        back = jnp.where(rows == position(across, offs[g]), 1.0, 0.0).astype(BF)
         out_ref[g] = dot_nn(back, out_c).astype(BF)
     zq[...] = jnp.zeros_like(zq)
     zt[...] = jnp.zeros_like(zt)
@@ -341,7 +346,7 @@
             pltpu.SMEM((IMAGES,), jnp.int32),
             pltpu.SemaphoreType.DMA((3,)),
         ],
-        compiler_params=pltpu.CompilerParams(vmem_limit_bytes=52 * 2**20),
+        compiler_params=pltpu.CompilerParams(vmem_limit_bytes=44 * 2**20),
         name="attend",
     )(pinned(seq), pinned(start), seat, *same, *other, qt, mt, pinned(grad))
 
@@ -382,7 +387,7 @@
         pack_kernel,
         out_shape=(
             jax.ShapeDtypeStruct((TEXT + 16, 256), BF),
-            jax.ShapeDtypeStruct((TEXT + 16, 256), BF),
+            jax.ShapeDtypeStruct((TEXT, 256), BF),
             jax.ShapeDtypeStruct((PDIM, 128), F32),
             jax.ShapeDtypeStruct((PDIM, PDIM), F32),
             jax.ShapeDtypeStruct((PDIM, D), BF),
@@ -427,21 +432,27 @@
         compiler_params=pltpu.CompilerParams(vmem_limit_bytes=32 * 2**20),
         name="fold",
     )(patch, pinned(w_query), pinned(w_key), pinned(w_value))
-    qt, block = pl.pallas_call(
+    block, left, text_inv = pl.pallas_call(
         project_kernel,
         out_shape=(
-            jax.ShapeDtypeStruct((NSEQ * TEXT, 256), BF),
             jax.ShapeDtypeStruct((KV_ROWS, 512), BF),
+            jax.ShapeDtypeStruct((NSEQ * TEXT, D), BF),
+            jax.ShapeDtypeStruct((NSEQ * TEXT, 128), F32),
         ),
-        in_specs=[smem] + [vmem] * 12,
-        out_specs=(vmem,) * 2,
-        scratch_shapes=[
-            pltpu.VMEM((NSEQ * TEXT, D), BF),
-            pltpu.VMEM((PDIM, 512), F32),
-        ],
+        in_specs=[smem] + [vmem] * 11,
+        out_specs=(vmem,) * 3,
+        scratch_shapes=[pltpu.VMEM((PDIM, 512), F32)],
         compiler_params=pltpu.CompilerParams(vmem_limit_bytes=32 * 2**20),
         name="project",
-    )(group, *firsts, *seconds, gain, wq, wk, wv)
+    )(group, *firsts, *seconds, gain, wk, wv)
+    qt = pl.pallas_call(
+        query_kernel,
+        out_shape=jax.ShapeDtypeStruct((NSEQ * TEXT, 256), BF),
+        in_specs=[vmem] * 3,
+        out_specs=vmem,
+        compiler_params=pltpu.CompilerParams(vmem_limit_bytes=32 * 2**20),
+        name="query",
+    )(left, text_inv, wq)
     hops = [block] + [
         lax.ppermute(block, "seq", [(i, (i + 2 * k) % seats) for i in range(seats)])
         for k in range(1, seats // 2)

time: 95.5 us -> 90.1 us (0.943)
  starting transfers between devices: 35.7 us -> 33.9 us
  blocking collectives: 27.8 us -> 26 us
  Pallas kernels: 17.7 us -> 16.7 us
    ppermute x6, waiting for transfers between devices: 8.95 us -> 5.77 us  [shift_z(): lax.ppermute(x, 'dp', [(i, (i + side * k) % groups) for i in range(groups)])]
    ppermute x6, waiting for transfers between devices: 2.13 us -> 4.4 us  [shift_y(): return lax.ppermute(x, 'dp', pairs)]
    all_to_all x1, blocking collectives: 27.8 us -> 26 us  [on_device(): lax.all_to_all(z.reshape(groups * seats, 8, 128), ('dp', 'seq'), 0, 0)]
    ppermute x3, waiting for transfers between devices: 0.31 us -> 1.81 us  [on_device(): lax.ppermute(block, 'seq', [(i, (i + 2 * k) % seats) for i in range(seats)])]
    ppermute x4, starting transfers between devices: 15.8 us -> 14.3 us  [on_device(): lax.ppermute(hop, 'seq', [(i, i ^ 1) for i in range(seats)])]
    pallas_call x1, Pallas kernels: 8.95 us -> 7.83 us  [attend(): pl.pallas_call(attend_kernel, out_shape=(jax.ShapeDtypeStruct((NSEQ, BLOC...]
    pallas_call x1 -> x2, Pallas kernels: 2.5 us -> 2.6 us  [the longest x1 1.9 us: on_device(): pl.pallas_call(project_kernel, out_shape=(jax.ShapeDtypeStruct((KV_ROWS,...]
  transfers between devices with their start and end apart: 19 -> 19, of which waited for: 10 -> 10; matrix products, arithmetic and copies ran while one was open for 0% -> 0% of each run, Pallas kernels for 4% -> 5%
where the time goes in v5:
time: 90.1 us; the launch traced here: 89.9 us
  starting transfers between devices  33.9 us (38%)
  blocking collectives  26 us (29%)
  Pallas kernels  16.7 us (19%)
  waiting for transfers between devices  12.4 us (14%)
    all_to_all x1, blocking collectives, on_device(): lax.all_to_all(z.reshape(groups * seats, 8, 128), ('dp', 'seq'), 0, 0)  26 us
    ppermute x4, starting transfers between devices, on_device(): lax.ppermute(hop, 'seq', [(i, i ^ 1) for i in range(seats)])  14.3 us
    ppermute x6, starting transfers between devices, shift_z(): lax.ppermute(x, 'dp', [(i, (i + side * k) % groups) for i in range(groups)])  8.34 us
    pallas_call x1, Pallas kernels, attend(): pl.pallas_call(attend_kernel, out_shape=(jax.ShapeDtypeStruct((NSEQ, BLOC...  7.83 us
    ppermute x6, starting transfers between devices, shift_y(): return lax.ppermute(x, 'dp', pairs)  7.62 us
    ppermute x6, waiting for transfers between devices, shift_z(): lax.ppermute(x, 'dp', [(i, (i + side * k) % groups) for i in range(groups)])  5.77 us
    ppermute x6, waiting for transfers between devices, shift_y(): return lax.ppermute(x, 'dp', pairs)  4.4 us
    ppermute x3, starting transfers between devices, on_device(): lax.ppermute(block, 'seq', [(i, (i + 2 * k) % seats) for i in range(seats)])  3.67 us
  transfers between devices with their start and end apart: 19, of which 10 were waited for; matrix products, arithmetic and copies ran while one was open for 0% of the time, Pallas kernels for 5%

profile of v5, /device:TPU:1, one launch (start us, length us, event | category | flops | bytes accessed | tf_op | source)
XLA Modules:
  0.0 89.9 jit_solution(7464518435583677209)
XLA Ops:
  0.6 1.6 %pack.1 = (bf16[144,256]{1,0:T(8,128)(2,1)S(1)}, bf16[128,256]{1,0:T(8,128)(2,1)S(1)}, f32[32,128]{1,0:T(8,128)S(1)}, f32[32,32]{1,0:T(8,128)S(1)}, bf16[32,4096]{1,0:T(8,128)(2,1)S(1)}, /*index=5*/f32[1,4096]{1,0:T(1,128)S(1)}) custom-call(s32[16]{0:T(128)} %seq_hbm.3, s32[16]{0:T(128)} %start_hbm.3, s32[1]{0:T(128)} %bitcast.seat_ref, ...), custom_call_target="tpu_custom_call" | custom-call | tf_op jit(solution)/shard_map/pack/pallas_call | solution.py:386
  2.2 4.5 %collective-permute-start.5 = (bf16[128,256]{1,0:T(8,128)(2,1)S(1)}, bf16[128,256]{1,0:T(8,128)(2,1)S(1)}, u32[]{:S(2)}, u32[]{:S(2)}) collective-permute-start(bf16[128,256]{1,0:T(8,128)(2,1)S(1)} %get-tuple-element.32), channel_id=1, source_target_pairs={{0,8},{1,9},{2,10},{3,11},{4,12},{5,13},{6,14},{7,15},{8,0},{9,1},... | collective-permute-start | bytes 196616 | tf_op jit(solution)/shard_map/ppermute | solution.py:380
  6.7 2.9 %collective-permute-start.4 = (bf16[144,256]{1,0:T(8,128)(2,1)S(1)}, bf16[144,256]{1,0:T(8,128)(2,1)S(1)}, u32[]{:S(2)}, u32[]{:S(2)}) collective-permute-start(bf16[144,256]{1,0:T(8,128)(2,1)S(1)} %get-tuple-element.31), channel_id=1, source_target_pairs={{0,2},{1,3},{2,0},{3,1},{4,6},{5,7},{6,4},{7,5},{8,10},{9,11},{10,... | collective-permute-start | bytes 221192 | tf_op jit(solution)/shard_map/ppermute | solution.py:377
  9.7 0.8 collective-permute-start.2
  10.4 0.7 collective-permute-start
  11.1 0.4 collective-permute-start.3
  11.6 0.0 collective-permute-done.5
  11.6 1.0 %collective-permute-start.1 = (bf16[128,256]{1,0:T(8,128)(2,1)S(1)}, bf16[128,256]{1,0:T(8,128)(2,1)S(1)}, u32[]{:S(2)}, u32[]{:S(2)}) collective-permute-start(bf16[128,256]{1,0:T(8,128)(2,1)S(1)} %get-tuple-element.32), channel_id=1, source_target_pairs={{0,4},{1,5},{2,6},{3,7},{4,8},{5,9},{6,10},{7,11},{8,12},{9,13},{1... | collective-permute-start | bytes 196616 | tf_op jit(solution)/shard_map/ppermute | solution.py:380
  12.6 1.9 %collective-permute-done.3 = bf16[128,256]{1,0:T(8,128)(2,1)S(1)} collective-permute-done((bf16[128,256]{1,0:T(8,128)(2,1)S(1)}, bf16[128,256]{1,0:T(8,128)(2,1)S(1)}, u32[]{:S(2)}, u32[]{:S(2)}) %collective-permute-start.3) | collective-permute-done | bytes 65568 | tf_op jit(solution)/shard_map/ppermute | solution.py:380
  14.5 1.4 %collective-permute-done.1 = bf16[128,256]{1,0:T(8,128)(2,1)S(1)} collective-permute-done((bf16[128,256]{1,0:T(8,128)(2,1)S(1)}, bf16[128,256]{1,0:T(8,128)(2,1)S(1)}, u32[]{:S(2)}, u32[]{:S(2)}) %collective-permute-start.1) | collective-permute-done | bytes 65568 | tf_op jit(solution)/shard_map/ppermute | solution.py:380
  15.9 0.0 collective-permute-done.4
  15.9 0.0 collective-permute-done.2
  15.9 0.0 collective-permute-done
  16.0 0.9 %collective-permute-start.11 = (bf16[4,128,256]{2,1,0:T(8,128)(2,1)S(1)}, bf16[4,128,256]{2,1,0:T(8,128)(2,1)S(1)}, u32[]{:S(2)}, u32[]{:S(2)}) collective-permute-start(bf16[4,128,256]{2,1,0:T(8,128)(2,1)S(1)} %pad_maximum_fusion.1.t0), channel_id=1, source_target_pairs={{0,2},{1,3},{2,0},{3,1},{4,6},{5,7},{6,4},{7,5},{8,10},{9,11},{10,... | collective-permute-start | bytes 786440 | tf_op jit(solution)/shard_map/ppermute | solution.py:377
  16.9 0.7 collective-permute-start.10
  17.7 1.6 %collective-permute-start.8 = (bf16[4,144,256]{2,1,0:T(8,128)(2,1)S(1)}, bf16[4,144,256]{2,1,0:T(8,128)(2,1)S(1)}, u32[]{:S(2)}, u32[]{:S(2)}) collective-permute-start(bf16[4,144,256]{2,1,0:T(8,128)(2,1)S(1)} %pad_maximum_fusion.f0), channel_id=1, source_target_pairs={{0,12},{1,13},{2,14},{3,15},{4,0},{5,1},{6,2},{7,3},{8,4},{9,5},{1... | collective-permute-start | bytes 884744 | tf_op jit(solution)/shard_map/ppermute | solution.py:380
  19.3 0.0 collective-permute-start.6
  19.3 1.9 %collective-permute-start.9 = (bf16[4,128,256]{2,1,0:T(8,128)(2,1)S(1)}, bf16[4,128,256]{2,1,0:T(8,128)(2,1)S(1)}, u32[]{:S(2)}, u32[]{:S(2)}) collective-permute-start(bf16[4,128,256]{2,1,0:T(8,128)(2,1)S(1)} %pad_maximum_fusion.1.t0), channel_id=1, source_target_pairs={{0,3},{1,0},{2,1},{3,2},{4,7},{5,4},{6,5},{7,6},{8,11},{9,8},{10,9... | collective-permute-start | bytes 786440 | tf_op jit(solution)/shard_map/ppermute | solution.py:377
  21.2 1.6 %collective-permute-done.11.t3 = bf16[4,128,256]{2,1,0:T(8,128)(2,1)S(1)} collective-permute-done((bf16[4,128,256]{2,1,0:T(8,128)(2,1)S(1)}, bf16[4,128,256]{2,1,0:T(8,128)(2,1)S(1)}, u32[]{:S(2)}, u32[]{:S(2)}) %collective-permute-start.11) | collective-permute-done | bytes 262176 | tf_op jit(solution)/shard_map/ppermute | solution.py:377
  22.8 0.4 collective-permute-start.7
  23.2 3.6 %fold.1 = (bf16[4096,256]{1,0:T(8,128)(2,1)S(1)}, bf16[4096,256]{1,0:T(8,128)(2,1)S(1)}, bf16[4096,256]{1,0:T(8,128)(2,1)S(1)}, bf16[32,768]{1,0:T(8,128)(2,1)S(1)}) custom-call(bf16[32,4096]{1,0:T(8,128)(2,1)S(1)} %get-tuple-element.48.patch_ref, bf16[4096,256]{1,0:T(8,128)(2,1)} %wq_hbm.1, bf16[4096,256]{1,0:T(8,128)(2,1)} %wk_hbm.1, bf16[4096,256]{1,0:T(8,128)(2,1)} %wv_hbm.1), custom_call_target="tpu_custom_call" | custom-call | tf_op jit(solution)/shard_map/fold/pallas_call | solution.py:426
  26.8 0.6 collective-permute-done.9.t2
  27.4 2.2 %collective-permute-done.7.t1 = bf16[4,128,256]{2,1,0:T(8,128)(2,1)S(1)} collective-permute-done((bf16[4,128,256]{2,1,0:T(8,128)(2,1)S(1)}, bf16[4,128,256]{2,1,0:T(8,128)(2,1)S(1)}, u32[]{:S(2)}, u32[]{:S(2)}) %collective-permute-start.7) | collective-permute-done | bytes 262176 | tf_op jit(solution)/shard_map/ppermute | solution.py:377
  29.6 0.0 collective-permute-done.10.f3
  29.6 0.9 %collective-permute-done.8.f2 = bf16[4,144,256]{2,1,0:T(8,128)(2,1)S(1)} collective-permute-done((bf16[4,144,256]{2,1,0:T(8,128)(2,1)S(1)}, bf16[4,144,256]{2,1,0:T(8,128)(2,1)S(1)}, u32[]{:S(2)}, u32[]{:S(2)}) %collective-permute-start.8) | collective-permute-done | bytes 294944 | tf_op jit(solution)/shard_map/ppermute | solution.py:380
  30.5 1.6 %collective-permute-done.6.f1 = bf16[4,144,256]{2,1,0:T(8,128)(2,1)S(1)} collective-permute-done((bf16[4,144,256]{2,1,0:T(8,128)(2,1)S(1)}, bf16[4,144,256]{2,1,0:T(8,128)(2,1)S(1)}, u32[]{:S(2)}, u32[]{:S(2)}) %collective-permute-start.6) | collective-permute-done | bytes 294944 | tf_op jit(solution)/shard_map/ppermute | solution.py:380
  32.1 1.9 %project.1 = (bf16[288,512]{1,0:T(8,128)(2,1)S(1)}, bf16[256,4096]{1,0:T(8,128)(2,1)S(1)}, f32[256,128]{1,0:T(8,128)S(1)}) custom-call(s32[1]{0:T(128)} %bitcast.1.group_ref, bf16[4,144,256]{2,1,0:T(8,128)(2,1)S(1)} %pad_maximum_fusion.f0, bf16[4,144,256]{2,1,0:T(8,128)(2,1)S(1)} %collective-permute-done.6.f1, ...), custom_call_target="tpu_custom_call" | custom-call | tf_op jit(solution)/shard_map/project/pallas_call | solution.py:435
  34.0 2.5 %collective-permute-start.14 = (bf16[288,512]{1,0:T(8,128)(2,1)S(1)}, bf16[288,512]{1,0:T(8,128)(2,1)S(1)}, u32[]{:S(2)}, u32[]{:S(2)}) collective-permute-start(bf16[288,512]{1,0:T(8,128)(2,1)S(1)} %get-tuple-element.51.s0), channel_id=1, source_target_pairs={{0,96},{16,112},{32,0},{48,16},{64,32},{80,48},{96,64},{112,80},{1... | collective-permute-start | bytes 884744 | tf_op jit(solution)/shard_map/ppermute | solution.py:457
  36.5 0.5 collective-permute-start.13
  37.0 0.6 collective-permute-start.12
  37.6 4.6 %collective-permute-start.15 = (bf16[288,512]{1,0:T(8,128)(2,1)S(1)}, bf16[288,512]{1,0:T(8,128)(2,1)S(1)}, u32[]{:S(2)}, u32[]{:S(2)}) collective-permute-start(bf16[288,512]{1,0:T(8,128)(2,1)S(1)} %get-tuple-element.51.s0), channel_id=1, source_target_pairs={{0,16},{16,0},{32,48},{48,32},{64,80},{80,64},{96,112},{112,96},{1... | collective-permute-start | bytes 884744 | tf_op jit(solution)/shard_map/ppermute | solution.py:460
  42.3 0.9 %collective-permute-done.14.s3 = bf16[288,512]{1,0:T(8,128)(2,1)S(1)} collective-permute-done((bf16[288,512]{1,0:T(8,128)(2,1)S(1)}, bf16[288,512]{1,0:T(8,128)(2,1)S(1)}, u32[]{:S(2)}, u32[]{:S(2)}) %collective-permute-start.14) | collective-permute-done | bytes 294944 | tf_op jit(solution)/shard_map/ppermute | solution.py:457
  43.2 6.9 %collective-permute-start.18 = (bf16[288,512]{1,0:T(8,128)(2,1)S(1)}, bf16[288,512]{1,0:T(8,128)(2,1)S(1)}, u32[]{:S(2)}, u32[]{:S(2)}) collective-permute-start(bf16[288,512]{1,0:T(8,128)(2,1)S(1)} %collective-permute-done.14.s3), channel_id=1, source_target_pairs={{0,16},{16,0},{32,48},{48,32},{64,80},{80,64},{96,112},{112,96},{1... | collective-permute-start | bytes 884744 | tf_op jit(solution)/shard_map/ppermute | solution.py:460
  50.1 0.0 collective-permute-done.13.s2
  50.1 0.7 collective-permute-start.17
  50.8 0.9 collective-permute-done.12.s1
  51.6 2.1 %collective-permute-start.16 = (bf16[288,512]{1,0:T(8,128)(2,1)S(1)}, bf16[288,512]{1,0:T(8,128)(2,1)S(1)}, u32[]{:S(2)}, u32[]{:S(2)}) collective-permute-start(bf16[288,512]{1,0:T(8,128)(2,1)S(1)} %collective-permute-done.12.s1), channel_id=1, source_target_pairs={{0,16},{16,0},{32,48},{48,32},{64,80},{80,64},{96,112},{112,96},{1... | collective-permute-start | bytes 884744 | tf_op jit(solution)/shard_map/ppermute | solution.py:460
  53.8 0.7 query.1.qt_ref
  54.5 0.0 copy-start
  54.5 0.0 collective-permute-done.15.o0
  54.5 0.0 collective-permute-done.18.o3
  54.5 0.0 collective-permute-done.17.o2
  54.5 0.5 collective-permute-done.16.o1
  55.0 7.8 %attend.1 = (bf16[2,384,256]{2,1,0:T(8,128)(2,1)}, bf16[16,64,128]{2,1,0:T(8,128)(2,1)S(1)}) custom-call(s32[16]{0:T(128)} %seq_hbm.3, s32[16]{0:T(128)} %start_hbm.3, s32[1]{0:T(128)} %bitcast.seat_ref, bf16[288,512]{1,0:T(8,128)(2,1)S(1)} %get-tuple-element.51.s0, bf16[288,512]{1,0:T(8,128)(2,1)S(1)} %collective-permute-done.12.s1, ...), custom_call_target="tpu_custom_call" | custom-call | tf_op jit(solution)/shard_map/attend/pallas_call | solution.py:321
  62.8 26.0 %all_to_all.5.recv_ref = bf16[128,8,128]{2,1,0:T(8,128)(2,1)S(1)} all-to-all(bf16[128,8,128]{2,1,0:T(8,128)(2,1)S(1)} %bitcast.14), channel_id=1, replica_groups=mesh['seq'=8,'dp'=16] {'dp','seq'}, dimensions={0} | all-to-all | bytes 524288 | tf_op jit(solution)/shard_map/all_to_all | solution.py:462
  88.8 0.0 copy-done
  88.8 1.1 %finish.1 = f32[32,32]{1,0:T(8,128)} custom-call(bf16[128,8,128]{2,1,0:T(8,128)(2,1)S(1)} %all_to_all.5.recv_ref, bf16[32,32]{1,0:T(8,128)(2,1)S(1)} %bitcast.18, f32[32,128]{1,0:T(8,128)S(1)} %get-tuple-element.58.inv_ref, f32[32,32]{1,0:T(8,128)S(1)} %get-tuple-element.59.u_ref), custom_call_target="tpu_custom_call" | custom-call | tf_op jit(solution)/shard_map/finish/pallas_call | solution.py:463
  (2 shorter events, 0.1 us)
Async XLA Ops:
  2.2 9.3 %collective-permute-start.5 = (bf16[128,256]{1,0:T(8,128)(2,1)S(1)}, bf16[128,256]{1,0:T(8,128)(2,1)S(1)}, u32[]{:S(2)}, u32[]{:S(2)}) collective-permute-start(bf16[128,256]{1,0:T(8,128)(2,1)S(1)} %get-tuple-element.32), channel_id=1, source_target_pairs={{0,8},{1,9},{2,10},{3,11},{4,12},{5,13},{6,14},{7,15},{8,0},{9,1},... | collective-permute-start | bytes 196616 | tf_op jit(solution)/shard_map/ppermute | solution.py:380
  6.7 9.1 %collective-permute-start.4 = (bf16[144,256]{1,0:T(8,128)(2,1)S(1)}, bf16[144,256]{1,0:T(8,128)(2,1)S(1)}, u32[]{:S(2)}, u32[]{:S(2)}) collective-permute-start(bf16[144,256]{1,0:T(8,128)(2,1)S(1)} %get-tuple-element.31), channel_id=1, source_target_pairs={{0,2},{1,3},{2,0},{3,1},{4,6},{5,7},{6,4},{7,5},{8,10},{9,11},{10,... | collective-permute-start | bytes 221192 | tf_op jit(solution)/shard_map/ppermute | solution.py:377
  9.7 6.2 %collective-permute-start.2 = (bf16[144,256]{1,0:T(8,128)(2,1)S(1)}, bf16[144,256]{1,0:T(8,128)(2,1)S(1)}, u32[]{:S(2)}, u32[]{:S(2)}) collective-permute-start(bf16[144,256]{1,0:T(8,128)(2,1)S(1)} %get-tuple-element.31), channel_id=1, source_target_pairs={{0,3},{1,0},{2,1},{3,2},{4,7},{5,4},{6,5},{7,6},{8,11},{9,8},{10,9... | collective-permute-start | bytes 221192 | tf_op jit(solution)/shard_map/ppermute | solution.py:377
  10.4 5.5 %collective-permute-start = (bf16[144,256]{1,0:T(8,128)(2,1)S(1)}, bf16[144,256]{1,0:T(8,128)(2,1)S(1)}, u32[]{:S(2)}, u32[]{:S(2)}) collective-permute-start(bf16[144,256]{1,0:T(8,128)(2,1)S(1)} %get-tuple-element.31), channel_id=1, source_target_pairs={{0,1},{1,2},{2,3},{3,0},{4,5},{5,6},{6,7},{7,4},{8,9},{9,10},{10,1... | collective-permute-start | bytes 221192 | tf_op jit(solution)/shard_map/ppermute | solution.py:377
  11.1 3.4 %collective-permute-start.3 = (bf16[128,256]{1,0:T(8,128)(2,1)S(1)}, bf16[128,256]{1,0:T(8,128)(2,1)S(1)}, u32[]{:S(2)}, u32[]{:S(2)}) collective-permute-start(bf16[128,256]{1,0:T(8,128)(2,1)S(1)} %get-tuple-element.32), channel_id=1, source_target_pairs={{0,12},{1,13},{2,14},{3,15},{4,0},{5,1},{6,2},{7,3},{8,4},{9,5},{1... | collective-permute-start | bytes 196616 | tf_op jit(solution)/shard_map/ppermute | solution.py:380
  11.6 4.3 %collective-permute-start.1 = (bf16[128,256]{1,0:T(8,128)(2,1)S(1)}, bf16[128,256]{1,0:T(8,128)(2,1)S(1)}, u32[]{:S(2)}, u32[]{:S(2)}) collective-permute-start(bf16[128,256]{1,0:T(8,128)(2,1)S(1)} %get-tuple-element.32), channel_id=1, source_target_pairs={{0,4},{1,5},{2,6},{3,7},{4,8},{5,9},{6,10},{7,11},{8,12},{9,13},{1... | collective-permute-start | bytes 196616 | tf_op jit(solution)/shard_map/ppermute | solution.py:380
  16.0 6.8 %collective-permute-start.11 = (bf16[4,128,256]{2,1,0:T(8,128)(2,1)S(1)}, bf16[4,128,256]{2,1,0:T(8,128)(2,1)S(1)}, u32[]{:S(2)}, u32[]{:S(2)}) collective-permute-start(bf16[4,128,256]{2,1,0:T(8,128)(2,1)S(1)} %pad_maximum_fusion.1.t0), channel_id=1, source_target_pairs={{0,2},{1,3},{2,0},{3,1},{4,6},{5,7},{6,4},{7,5},{8,10},{9,11},{10,... | collective-permute-start | bytes 786440 | tf_op jit(solution)/shard_map/ppermute | solution.py:377
  16.9 12.7 %collective-permute-start.10 = (bf16[4,144,256]{2,1,0:T(8,128)(2,1)S(1)}, bf16[4,144,256]{2,1,0:T(8,128)(2,1)S(1)}, u32[]{:S(2)}, u32[]{:S(2)}) collective-permute-start(bf16[4,144,256]{2,1,0:T(8,128)(2,1)S(1)} %pad_maximum_fusion.f0), channel_id=1, source_target_pairs={{0,8},{1,9},{2,10},{3,11},{4,12},{5,13},{6,14},{7,15},{8,0},{9,1},... | collective-permute-start | bytes 884744 | tf_op jit(solution)/shard_map/ppermute | solution.py:380
  17.7 12.8 %collective-permute-start.8 = (bf16[4,144,256]{2,1,0:T(8,128)(2,1)S(1)}, bf16[4,144,256]{2,1,0:T(8,128)(2,1)S(1)}, u32[]{:S(2)}, u32[]{:S(2)}) collective-permute-start(bf16[4,144,256]{2,1,0:T(8,128)(2,1)S(1)} %pad_maximum_fusion.f0), channel_id=1, source_target_pairs={{0,12},{1,13},{2,14},{3,15},{4,0},{5,1},{6,2},{7,3},{8,4},{9,5},{1... | collective-permute-start | bytes 884744 | tf_op jit(solution)/shard_map/ppermute | solution.py:380
  19.3 12.8 %collective-permute-start.6 = (bf16[4,144,256]{2,1,0:T(8,128)(2,1)S(1)}, bf16[4,144,256]{2,1,0:T(8,128)(2,1)S(1)}, u32[]{:S(2)}, u32[]{:S(2)}) collective-permute-start(bf16[4,144,256]{2,1,0:T(8,128)(2,1)S(1)} %pad_maximum_fusion.f0), channel_id=1, source_target_pairs={{0,4},{1,5},{2,6},{3,7},{4,8},{5,9},{6,10},{7,11},{8,12},{9,13},{1... | collective-permute-start | bytes 884744 | tf_op jit(solution)/shard_map/ppermute | solution.py:380
  19.3 8.1 %collective-permute-start.9 = (bf16[4,128,256]{2,1,0:T(8,128)(2,1)S(1)}, bf16[4,128,256]{2,1,0:T(8,128)(2,1)S(1)}, u32[]{:S(2)}, u32[]{:S(2)}) collective-permute-start(bf16[4,128,256]{2,1,0:T(8,128)(2,1)S(1)} %pad_maximum_fusion.1.t0), channel_id=1, source_target_pairs={{0,3},{1,0},{2,1},{3,2},{4,7},{5,4},{6,5},{7,6},{8,11},{9,8},{10,9... | collective-permute-start | bytes 786440 | tf_op jit(solution)/shard_map/ppermute | solution.py:377
  22.8 6.8 %collective-permute-start.7 = (bf16[4,128,256]{2,1,0:T(8,128)(2,1)S(1)}, bf16[4,128,256]{2,1,0:T(8,128)(2,1)S(1)}, u32[]{:S(2)}, u32[]{:S(2)}) collective-permute-start(bf16[4,128,256]{2,1,0:T(8,128)(2,1)S(1)} %pad_maximum_fusion.1.t0), channel_id=1, source_target_pairs={{0,1},{1,2},{2,3},{3,0},{4,5},{5,6},{6,7},{7,4},{8,9},{9,10},{10,1... | collective-permute-start | bytes 786440 | tf_op jit(solution)/shard_map/ppermute | solution.py:377
  34.0 9.2 %collective-permute-start.14 = (bf16[288,512]{1,0:T(8,128)(2,1)S(1)}, bf16[288,512]{1,0:T(8,128)(2,1)S(1)}, u32[]{:S(2)}, u32[]{:S(2)}) collective-permute-start(bf16[288,512]{1,0:T(8,128)(2,1)S(1)} %get-tuple-element.51.s0), channel_id=1, source_target_pairs={{0,96},{16,112},{32,0},{48,16},{64,32},{80,48},{96,64},{112,80},{1... | collective-permute-start | bytes 884744 | tf_op jit(solution)/shard_map/ppermute | solution.py:457
  36.5 13.6 %collective-permute-start.13 = (bf16[288,512]{1,0:T(8,128)(2,1)S(1)}, bf16[288,512]{1,0:T(8,128)(2,1)S(1)}, u32[]{:S(2)}, u32[]{:S(2)}) collective-permute-start(bf16[288,512]{1,0:T(8,128)(2,1)S(1)} %get-tuple-element.51.s0), channel_id=1, source_target_pairs={{0,64},{16,80},{32,96},{48,112},{64,0},{80,16},{96,32},{112,48},{1... | collective-permute-start | bytes 884744 | tf_op jit(solution)/shard_map/ppermute | solution.py:457
  37.0 14.6 %collective-permute-start.12 = (bf16[288,512]{1,0:T(8,128)(2,1)S(1)}, bf16[288,512]{1,0:T(8,128)(2,1)S(1)}, u32[]{:S(2)}, u32[]{:S(2)}) collective-permute-start(bf16[288,512]{1,0:T(8,128)(2,1)S(1)} %get-tuple-element.51.s0), channel_id=1, source_target_pairs={{0,32},{16,48},{32,64},{48,80},{64,96},{80,112},{96,0},{112,16},{1... | collective-permute-start | bytes 884744 | tf_op jit(solution)/shard_map/ppermute | solution.py:457
  37.6 16.9 %collective-permute-start.15 = (bf16[288,512]{1,0:T(8,128)(2,1)S(1)}, bf16[288,512]{1,0:T(8,128)(2,1)S(1)}, u32[]{:S(2)}, u32[]{:S(2)}) collective-permute-start(bf16[288,512]{1,0:T(8,128)(2,1)S(1)} %get-tuple-element.51.s0), channel_id=1, source_target_pairs={{0,16},{16,0},{32,48},{48,32},{64,80},{80,64},{96,112},{112,96},{1... | collective-permute-start | bytes 884744 | tf_op jit(solution)/shard_map/ppermute | solution.py:460
  43.2 11.3 %collective-permute-start.18 = (bf16[288,512]{1,0:T(8,128)(2,1)S(1)}, bf16[288,512]{1,0:T(8,128)(2,1)S(1)}, u32[]{:S(2)}, u32[]{:S(2)}) collective-permute-start(bf16[288,512]{1,0:T(8,128)(2,1)S(1)} %collective-permute-done.14.s3), channel_id=1, source_target_pairs={{0,16},{16,0},{32,48},{48,32},{64,80},{80,64},{96,112},{112,96},{1... | collective-permute-start | bytes 884744 | tf_op jit(solution)/shard_map/ppermute | solution.py:460
  50.1 4.4 %collective-permute-start.17 = (bf16[288,512]{1,0:T(8,128)(2,1)S(1)}, bf16[288,512]{1,0:T(8,128)(2,1)S(1)}, u32[]{:S(2)}, u32[]{:S(2)}) collective-permute-start(bf16[288,512]{1,0:T(8,128)(2,1)S(1)} %collective-permute-done.13.s2), channel_id=1, source_target_pairs={{0,16},{16,0},{32,48},{48,32},{64,80},{80,64},{96,112},{112,96},{1... | collective-permute-start | bytes 884744 | tf_op jit(solution)/shard_map/ppermute | solution.py:460
  51.6 3.3 %collective-permute-start.16 = (bf16[288,512]{1,0:T(8,128)(2,1)S(1)}, bf16[288,512]{1,0:T(8,128)(2,1)S(1)}, u32[]{:S(2)}, u32[]{:S(2)}) collective-permute-start(bf16[288,512]{1,0:T(8,128)(2,1)S(1)} %collective-permute-done.12.s1), channel_id=1, source_target_pairs={{0,16},{16,0},{32,48},{48,32},{64,80},{80,64},{96,112},{112,96},{1... | collective-permute-start | bytes 884744 | tf_op jit(solution)/shard_map/ppermute | solution.py:460
  54.5 34.4 %copy-start = (bf16[1,32,32]{2,1,0:T(8,128)(2,1)S(1)}, bf16[1,32,32]{2,1,0:T(8,128)(2,1)}, u32[]{:S(2)}) copy-start(bf16[1,32,32]{2,1,0:T(8,128)(2,1)} %param.11) | copy-start | bytes 6148

commit v6 on v5

--- a/solution.py
+++ b/solution.py
@@ -45,13 +45,13 @@
 
 
 def pack_kernel(
-    seq_hbm, start_hbm, seat_ref, text_hbm, lat_hbm, wp_hbm, gain_hbm,
-    first_ref, second_ref, inv_ref, u_ref, patch_ref, gain_ref,
+    seq_hbm, start_hbm, seat_ref, text_hbm, lat_hbm, wp_hbm,
+    first_ref, second_ref, inv_ref, embedded_ref,
     seq_ref, start_ref, text_ref, lat_ref, wp_ref, sems,
 ):
     pairs = (
         (seq_hbm, seq_ref), (start_hbm, start_ref), (lat_hbm, lat_ref), (wp_hbm, wp_ref),
-        (text_hbm, text_ref), (gain_hbm, gain_ref),
+        (text_hbm, text_ref),
     )
     copies = [pltpu.make_async_copy(a, b, sems.at[n]) for n, (a, b) in enumerate(pairs)]
     for copy in copies:
@@ -64,7 +64,7 @@
     emb_f = embedded.astype(F32)
     inv = lax.rsqrt(jnp.sum(emb_f * emb_f, axis=1, keepdims=True) * (1.0 / D) + epsilon)
     inv_ref[...] = jnp.broadcast_to(inv, inv_ref.shape)
-    u_ref[...] = dot_nt(embedded, wp)
+    embedded_ref[...] = embedded
     scaled = lat.astype(F32) * inv
     packed = jnp.concatenate([scaled[8 * a : 8 * (a + 1)] for a in range(4)], axis=1)
     tail = jnp.concatenate([packed, jnp.zeros((8, 128), F32)], axis=0)
@@ -79,18 +79,27 @@
         high = text_ref[g, PATCHES:BLOCK, :].astype(F32)
         ref[0:TEXT, :] = jnp.where(row < offs[g], low, high).astype(BF)
     first_ref[TEXT:, :] = tail
-    copies[5].wait()
-    patch_ref[...] = (wp.astype(F32) * gain_ref[...]).astype(BF)
-
-
-def fold_kernel(patch_ref, wq_hbm, wk_hbm, wv_hbm, wq_ref, wk_ref, wv_ref, mt_ref, sems):
-    pairs = ((wq_hbm, wq_ref), (wk_hbm, wk_ref), (wv_hbm, wv_ref))
+
+
+def fold_kernel(
+    embedded_ref, wp_hbm, gain_hbm, wq_hbm, wk_hbm, wv_hbm,
+    wq_ref, wk_ref, wv_ref, mt_ref, u_ref, gain_ref,
+    wp_ref, sems,
+):
+    pairs = (
+        (wp_hbm, wp_ref), (gain_hbm, gain_ref), (wq_hbm, wq_ref), (wk_hbm, wk_ref), (wv_hbm, wv_ref)
+    )
     copies = [pltpu.make_async_copy(a, b, sems.at[n]) for n, (a, b) in enumerate(pairs)]
     for copy in copies:
         copy.start()
-    for n, (_, ref) in enumerate(pairs):
-        copies[n].wait()
-        mt_ref[:, 256 * n : 256 * (n + 1)] = dot_nn(patch_ref[...], ref[...]).astype(BF)
+    copies[0].wait()
+    copies[1].wait()
+    wp = wp_ref[...]
+    u_ref[...] = dot_nt(embedded_ref[...], wp)
+    patch = (wp.astype(F32) * gain_ref[...]).astype(BF)
+    for n, ref in enumerate((wq_ref, wk_ref, wv_ref)):
+        copies[n + 2].wait()
+        mt_ref[:, 256 * n : 256 * (n + 1)] = dot_nn(patch, ref[...]).astype(BF)
 
 
 def project_kernel(
@@ -383,31 +392,28 @@
     smem = pl.BlockSpec(memory_space=pltpu.SMEM)
     vmem = pl.BlockSpec(memory_space=pltpu.VMEM)
     hbm = pl.BlockSpec(memory_space=pltpu.HBM)
-    first, second, inv, u, patch, gain = pl.pallas_call(
+    first, second, inv, embedded = pl.pallas_call(
         pack_kernel,
         out_shape=(
             jax.ShapeDtypeStruct((TEXT + 16, 256), BF),
             jax.ShapeDtypeStruct((TEXT, 256), BF),
             jax.ShapeDtypeStruct((PDIM, 128), F32),
-            jax.ShapeDtypeStruct((PDIM, PDIM), F32),
             jax.ShapeDtypeStruct((PDIM, D), BF),
-            jax.ShapeDtypeStruct((1, D), F32),
         ),
-        in_specs=[hbm, hbm, smem, hbm, hbm, hbm, hbm],
-        out_specs=(vmem,) * 6,
+        in_specs=[hbm, hbm, smem, hbm, hbm, hbm],
+        out_specs=(vmem,) * 4,
         scratch_shapes=[
             pltpu.SMEM((IMAGES,), jnp.int32),
             pltpu.SMEM((IMAGES,), jnp.int32),
             pltpu.VMEM((NSEQ, BLOCK, 256), BF),
             pltpu.VMEM((PDIM, PDIM), BF),
             pltpu.VMEM((PDIM, D), BF),
-            pltpu.SemaphoreType.DMA((6,)),
+            pltpu.SemaphoreType.DMA((5,)),
         ],
         compiler_params=pltpu.CompilerParams(vmem_limit_bytes=32 * 2**20),
         name="pack",
     )(
         pinned(image_seq), pinned(image_start), seat, pinned(text_rows), pinned(lat), pinned(w_patch),
-        pinned(norm_gain.reshape(1, D)),
     )
     near = []
     for k in HOPS:
@@ -423,15 +429,25 @@
     firsts = (first_y,) + far[0::2]
     seconds = (second_z,) + far[1::2]
     weight = jax.ShapeDtypeStruct((D, 256), BF)
-    wq, wk, wv, mt = pl.pallas_call(
+    wq, wk, wv, mt, u, gain = pl.pallas_call(
         fold_kernel,
-        out_shape=(weight, weight, weight, jax.ShapeDtypeStruct((PDIM, 768), BF)),
-        in_specs=[vmem] + [hbm] * 3,
-        out_specs=(vmem,) * 4,
-        scratch_shapes=[pltpu.SemaphoreType.DMA((3,))],
+        out_shape=(
+            weight,
+            weight,
+            weight,
+            jax.ShapeDtypeStruct((PDIM, 768), BF),
+            jax.ShapeDtypeStruct((PDIM, PDIM), F32),
+            jax.ShapeDtypeStruct((1, D), F32),
+        ),
+        in_specs=[vmem] + [hbm] * 5,
+        out_specs=(vmem,) * 6,
+        scratch_shapes=[pltpu.VMEM((PDIM, D), BF), pltpu.SemaphoreType.DMA((5,))],
         compiler_params=pltpu.CompilerParams(vmem_limit_bytes=32 * 2**20),
         name="fold",
-    )(patch, pinned(w_query), pinned(w_key), pinned(w_value))
+    )(
+        embedded, pinned(w_patch), pinned(norm_gain.reshape(1, D)),
+        pinned(w_query), pinned(w_key), pinned(w_value),
+    )
     block, left, text_inv = pl.pallas_call(
         project_kernel,
         out_shape=(

time: 90.1 us -> 90 us (level)
  no operation moved by 1% of the time
where the time goes in v6:
time: 90 us; the launch traced here: 89.8 us
  starting transfers between devices  34 us (38%)
  blocking collectives  26 us (29%)
  Pallas kernels  16.7 us (19%)
  waiting for transfers between devices  12.2 us (14%)
    all_to_all x1, blocking collectives, on_device(): lax.all_to_all(z.reshape(groups * seats, 8, 128), ('dp', 'seq'), 0, 0)  26 us
    ppermute x4, starting transfers between devices, on_device(): lax.ppermute(hop, 'seq', [(i, i ^ 1) for i in range(seats)])  14.4 us
    ppermute x6, starting transfers between devices, shift_z(): lax.ppermute(x, 'dp', [(i, (i + side * k) % groups) for i in range(groups)])  8.34 us
    pallas_call x1, Pallas kernels, attend(): pl.pallas_call(attend_kernel, out_shape=(jax.ShapeDtypeStruct((NSEQ, BLOC...  7.83 us
    ppermute x6, starting transfers between devices, shift_y(): return lax.ppermute(x, 'dp', pairs)  7.62 us
    ppermute x6, waiting for transfers between devices, shift_z(): lax.ppermute(x, 'dp', [(i, (i + side * k) % groups) for i in range(groups)])  5.76 us
    ppermute x6, waiting for transfers between devices, shift_y(): return lax.ppermute(x, 'dp', pairs)  4.28 us
    pallas_call x1, Pallas kernels, on_device(): pl.pallas_call(fold_kernel, out_shape=(weight, weight, weight, jax.ShapeD...  3.7 us
  transfers between devices with their start and end apart: 19, of which 10 were waited for; matrix products, arithmetic and copies ran while one was open for 0% of the time, Pallas kernels for 5%

profile of v6, /device:TPU:1, one launch (start us, length us, event | category | flops | bytes accessed | tf_op | source)
XLA Modules:
  0.0 89.8 jit_solution(8175788131543887139)
XLA Ops:
  0.6 1.5 %pack.1 = (bf16[144,256]{1,0:T(8,128)(2,1)S(1)}, bf16[128,256]{1,0:T(8,128)(2,1)S(1)}, f32[32,128]{1,0:T(8,128)S(1)}, bf16[32,4096]{1,0:T(8,128)(2,1)S(1)}) custom-call(s32[16]{0:T(128)} %seq_hbm.3, s32[16]{0:T(128)} %start_hbm.3, s32[1]{0:T(128)} %bitcast.seat_ref, bf16[2,384,256]{2,1,0:T(8,128)(2,1)} %text_hbm.1, bf16[32,32]{1,0:T(8,128)(2,1)} %bitcast.17, ...), custom_call_target="tpu_custom_call" | custom-call | tf_op jit(solution)/shard_map/pack/pallas_call | solution.py:395
  2.1 4.5 %collective-permute-start.5 = (bf16[128,256]{1,0:T(8,128)(2,1)S(1)}, bf16[128,256]{1,0:T(8,128)(2,1)S(1)}, u32[]{:S(2)}, u32[]{:S(2)}) collective-permute-start(bf16[128,256]{1,0:T(8,128)(2,1)S(1)} %get-tuple-element.32), channel_id=1, source_target_pairs={{0,8},{1,9},{2,10},{3,11},{4,12},{5,13},{6,14},{7,15},{8,0},{9,1},... | collective-permute-start | bytes 196616 | tf_op jit(solution)/shard_map/ppermute | solution.py:389
  6.6 2.9 %collective-permute-start.4 = (bf16[144,256]{1,0:T(8,128)(2,1)S(1)}, bf16[144,256]{1,0:T(8,128)(2,1)S(1)}, u32[]{:S(2)}, u32[]{:S(2)}) collective-permute-start(bf16[144,256]{1,0:T(8,128)(2,1)S(1)} %get-tuple-element.31), channel_id=1, source_target_pairs={{0,2},{1,3},{2,0},{3,1},{4,6},{5,7},{6,4},{7,5},{8,10},{9,11},{10,... | collective-permute-start | bytes 221192 | tf_op jit(solution)/shard_map/ppermute | solution.py:386
  9.6 0.8 collective-permute-start.2
  10.3 0.7 collective-permute-start
  11.0 0.4 collective-permute-start.3
  11.5 0.0 collective-permute-done.5
  11.5 1.0 %collective-permute-start.1 = (bf16[128,256]{1,0:T(8,128)(2,1)S(1)}, bf16[128,256]{1,0:T(8,128)(2,1)S(1)}, u32[]{:S(2)}, u32[]{:S(2)}) collective-permute-start(bf16[128,256]{1,0:T(8,128)(2,1)S(1)} %get-tuple-element.32), channel_id=1, source_target_pairs={{0,4},{1,5},{2,6},{3,7},{4,8},{5,9},{6,10},{7,11},{8,12},{9,13},{1... | collective-permute-start | bytes 196616 | tf_op jit(solution)/shard_map/ppermute | solution.py:389
  12.5 1.9 %collective-permute-done.3 = bf16[128,256]{1,0:T(8,128)(2,1)S(1)} collective-permute-done((bf16[128,256]{1,0:T(8,128)(2,1)S(1)}, bf16[128,256]{1,0:T(8,128)(2,1)S(1)}, u32[]{:S(2)}, u32[]{:S(2)}) %collective-permute-start.3) | collective-permute-done | bytes 65568 | tf_op jit(solution)/shard_map/ppermute | solution.py:389
  14.4 1.4 %collective-permute-done.1 = bf16[128,256]{1,0:T(8,128)(2,1)S(1)} collective-permute-done((bf16[128,256]{1,0:T(8,128)(2,1)S(1)}, bf16[128,256]{1,0:T(8,128)(2,1)S(1)}, u32[]{:S(2)}, u32[]{:S(2)}) %collective-permute-start.1) | collective-permute-done | bytes 65568 | tf_op jit(solution)/shard_map/ppermute | solution.py:389
  15.8 0.0 collective-permute-done.4
  15.8 0.0 collective-permute-done.2
  15.8 0.0 collective-permute-done
  15.9 0.9 %collective-permute-start.11 = (bf16[4,128,256]{2,1,0:T(8,128)(2,1)S(1)}, bf16[4,128,256]{2,1,0:T(8,128)(2,1)S(1)}, u32[]{:S(2)}, u32[]{:S(2)}) collective-permute-start(bf16[4,128,256]{2,1,0:T(8,128)(2,1)S(1)} %pad_maximum_fusion.1.t0), channel_id=1, source_target_pairs={{0,2},{1,3},{2,0},{3,1},{4,6},{5,7},{6,4},{7,5},{8,10},{9,11},{10,... | collective-permute-start | bytes 786440 | tf_op jit(solution)/shard_map/ppermute | solution.py:386
  16.8 0.7 collective-permute-start.10
  17.6 1.6 %collective-permute-start.8 = (bf16[4,144,256]{2,1,0:T(8,128)(2,1)S(1)}, bf16[4,144,256]{2,1,0:T(8,128)(2,1)S(1)}, u32[]{:S(2)}, u32[]{:S(2)}) collective-permute-start(bf16[4,144,256]{2,1,0:T(8,128)(2,1)S(1)} %pad_maximum_fusion.f0), channel_id=1, source_target_pairs={{0,12},{1,13},{2,14},{3,15},{4,0},{5,1},{6,2},{7,3},{8,4},{9,5},{1... | collective-permute-start | bytes 884744 | tf_op jit(solution)/shard_map/ppermute | solution.py:389
  19.2 0.0 collective-permute-start.6
  19.2 1.9 %collective-permute-start.9 = (bf16[4,128,256]{2,1,0:T(8,128)(2,1)S(1)}, bf16[4,128,256]{2,1,0:T(8,128)(2,1)S(1)}, u32[]{:S(2)}, u32[]{:S(2)}) collective-permute-start(bf16[4,128,256]{2,1,0:T(8,128)(2,1)S(1)} %pad_maximum_fusion.1.t0), channel_id=1, source_target_pairs={{0,3},{1,0},{2,1},{3,2},{4,7},{5,4},{6,5},{7,6},{8,11},{9,8},{10,9... | collective-permute-start | bytes 786440 | tf_op jit(solution)/shard_map/ppermute | solution.py:386
  21.1 1.6 %collective-permute-done.11.t3 = bf16[4,128,256]{2,1,0:T(8,128)(2,1)S(1)} collective-permute-done((bf16[4,128,256]{2,1,0:T(8,128)(2,1)S(1)}, bf16[4,128,256]{2,1,0:T(8,128)(2,1)S(1)}, u32[]{:S(2)}, u32[]{:S(2)}) %collective-permute-start.11) | collective-permute-done | bytes 262176 | tf_op jit(solution)/shard_map/ppermute | solution.py:386
  22.7 0.4 collective-permute-start.7
  23.1 3.7 %fold.1 = (bf16[4096,256]{1,0:T(8,128)(2,1)S(1)}, bf16[4096,256]{1,0:T(8,128)(2,1)S(1)}, bf16[4096,256]{1,0:T(8,128)(2,1)S(1)}, bf16[32,768]{1,0:T(8,128)(2,1)S(...) custom-call(bf16[32,4096]{1,0:T(8,128)(2,1)S(1)} %get-tuple-element.47.embedded_ref, bf16[32,4096]{1,0:T(8,128)(2,1)} %wp_hbm.3, ...), custom_call_target="tpu_custom_call" | custom-call | tf_op jit(solution)/shard_map/fold/pallas_call | solution.py:432
  26.8 0.5 collective-permute-done.9.t2
  27.3 2.2 %collective-permute-done.7.t1 = bf16[4,128,256]{2,1,0:T(8,128)(2,1)S(1)} collective-permute-done((bf16[4,128,256]{2,1,0:T(8,128)(2,1)S(1)}, bf16[4,128,256]{2,1,0:T(8,128)(2,1)S(1)}, u32[]{:S(2)}, u32[]{:S(2)}) %collective-permute-start.7) | collective-permute-done | bytes 262176 | tf_op jit(solution)/shard_map/ppermute | solution.py:386
  29.5 0.0 collective-permute-done.10.f3
  29.5 0.9 %collective-permute-done.8.f2 = bf16[4,144,256]{2,1,0:T(8,128)(2,1)S(1)} collective-permute-done((bf16[4,144,256]{2,1,0:T(8,128)(2,1)S(1)}, bf16[4,144,256]{2,1,0:T(8,128)(2,1)S(1)}, u32[]{:S(2)}, u32[]{:S(2)}) %collective-permute-start.8) | collective-permute-done | bytes 294944 | tf_op jit(solution)/shard_map/ppermute | solution.py:389
  30.4 1.6 %collective-permute-done.6.f1 = bf16[4,144,256]{2,1,0:T(8,128)(2,1)S(1)} collective-permute-done((bf16[4,144,256]{2,1,0:T(8,128)(2,1)S(1)}, bf16[4,144,256]{2,1,0:T(8,128)(2,1)S(1)}, u32[]{:S(2)}, u32[]{:S(2)}) %collective-permute-start.6) | collective-permute-done | bytes 294944 | tf_op jit(solution)/shard_map/ppermute | solution.py:389
  32.0 1.9 %project.1 = (bf16[288,512]{1,0:T(8,128)(2,1)S(1)}, bf16[256,4096]{1,0:T(8,128)(2,1)S(1)}, f32[256,128]{1,0:T(8,128)S(1)}) custom-call(s32[1]{0:T(128)} %bitcast.1.group_ref, bf16[4,144,256]{2,1,0:T(8,128)(2,1)S(1)} %pad_maximum_fusion.f0, bf16[4,144,256]{2,1,0:T(8,128)(2,1)S(1)} %collective-permute-done.6.f1, ...), custom_call_target="tpu_custom_call" | custom-call | tf_op jit(solution)/shard_map/project/pallas_call | solution.py:451
  33.9 2.5 %collective-permute-start.14 = (bf16[288,512]{1,0:T(8,128)(2,1)S(1)}, bf16[288,512]{1,0:T(8,128)(2,1)S(1)}, u32[]{:S(2)}, u32[]{:S(2)}) collective-permute-start(bf16[288,512]{1,0:T(8,128)(2,1)S(1)} %get-tuple-element.51.s0), channel_id=1, source_target_pairs={{0,96},{16,112},{32,0},{48,16},{64,32},{80,48},{96,64},{112,80},{1... | collective-permute-start | bytes 884744 | tf_op jit(solution)/shard_map/ppermute | solution.py:473
  36.4 0.5 collective-permute-start.13
  36.9 0.6 collective-permute-start.12
  37.5 4.6 %collective-permute-start.15 = (bf16[288,512]{1,0:T(8,128)(2,1)S(1)}, bf16[288,512]{1,0:T(8,128)(2,1)S(1)}, u32[]{:S(2)}, u32[]{:S(2)}) collective-permute-start(bf16[288,512]{1,0:T(8,128)(2,1)S(1)} %get-tuple-element.51.s0), channel_id=1, source_target_pairs={{0,16},{16,0},{32,48},{48,32},{64,80},{80,64},{96,112},{112,96},{1... | collective-permute-start | bytes 884744 | tf_op jit(solution)/shard_map/ppermute | solution.py:476
  42.2 0.9 collective-permute-done.14.s3
  43.0 6.9 %collective-permute-start.18 = (bf16[288,512]{1,0:T(8,128)(2,1)S(1)}, bf16[288,512]{1,0:T(8,128)(2,1)S(1)}, u32[]{:S(2)}, u32[]{:S(2)}) collective-permute-start(bf16[288,512]{1,0:T(8,128)(2,1)S(1)} %collective-permute-done.14.s3), channel_id=1, source_target_pairs={{0,16},{16,0},{32,48},{48,32},{64,80},{80,64},{96,112},{112,96},{1... | collective-permute-start | bytes 884744 | tf_op jit(solution)/shard_map/ppermute | solution.py:476
  50.0 0.0 collective-permute-done.13.s2
  50.0 0.7 collective-permute-start.17
  50.6 0.9 collective-permute-done.12.s1
  51.5 2.1 %collective-permute-start.16 = (bf16[288,512]{1,0:T(8,128)(2,1)S(1)}, bf16[288,512]{1,0:T(8,128)(2,1)S(1)}, u32[]{:S(2)}, u32[]{:S(2)}) collective-permute-start(bf16[288,512]{1,0:T(8,128)(2,1)S(1)} %collective-permute-done.12.s1), channel_id=1, source_target_pairs={{0,16},{16,0},{32,48},{48,32},{64,80},{80,64},{96,112},{112,96},{1... | collective-permute-start | bytes 884744 | tf_op jit(solution)/shard_map/ppermute | solution.py:476
  53.7 0.7 query.1.qt_ref
  54.4 0.0 copy-start
  54.4 0.0 collective-permute-done.15.o0
  54.4 0.0 collective-permute-done.18.o3
  54.4 0.0 collective-permute-done.17.o2
  54.4 0.5 collective-permute-done.16.o1
  54.9 7.8 %attend.1 = (bf16[2,384,256]{2,1,0:T(8,128)(2,1)}, bf16[16,64,128]{2,1,0:T(8,128)(2,1)S(1)}) custom-call(s32[16]{0:T(128)} %seq_hbm.3, s32[16]{0:T(128)} %start_hbm.3, s32[1]{0:T(128)} %bitcast.seat_ref, bf16[288,512]{1,0:T(8,128)(2,1)S(1)} %get-tuple-element.51.s0, bf16[288,512]{1,0:T(8,128)(2,1)S(1)} %collective-permute-done.12.s1, ...), custom_call_target="tpu_custom_call" | custom-call | tf_op jit(solution)/shard_map/attend/pallas_call | solution.py:330
  62.7 26.0 %all_to_all.5.recv_ref = bf16[128,8,128]{2,1,0:T(8,128)(2,1)S(1)} all-to-all(bf16[128,8,128]{2,1,0:T(8,128)(2,1)S(1)} %bitcast.14), channel_id=1, replica_groups=mesh['seq'=8,'dp'=16] {'dp','seq'}, dimensions={0} | all-to-all | bytes 524288 | tf_op jit(solution)/shard_map/all_to_all | solution.py:478
  88.7 0.0 copy-done
  88.7 1.1 %finish.1 = f32[32,32]{1,0:T(8,128)} custom-call(bf16[128,8,128]{2,1,0:T(8,128)(2,1)S(1)} %all_to_all.5.recv_ref, bf16[32,32]{1,0:T(8,128)(2,1)S(1)} %bitcast.18, f32[32,128]{1,0:T(8,128)S(1)} %get-tuple-element.58.inv_ref, f32[32,32]{1,0:T(8,128)S(1)} %get-tuple-element.59.u_ref), custom_call_target="tpu_custom_call" | custom-call | tf_op jit(solution)/shard_map/finish/pallas_call | solution.py:479
  (2 shorter events, 0.1 us)
Async XLA Ops:
  2.1 9.3 %collective-permute-start.5 = (bf16[128,256]{1,0:T(8,128)(2,1)S(1)}, bf16[128,256]{1,0:T(8,128)(2,1)S(1)}, u32[]{:S(2)}, u32[]{:S(2)}) collective-permute-start(bf16[128,256]{1,0:T(8,128)(2,1)S(1)} %get-tuple-element.32), channel_id=1, source_target_pairs={{0,8},{1,9},{2,10},{3,11},{4,12},{5,13},{6,14},{7,15},{8,0},{9,1},... | collective-permute-start | bytes 196616 | tf_op jit(solution)/shard_map/ppermute | solution.py:389
  6.6 9.2 %collective-permute-start.4 = (bf16[144,256]{1,0:T(8,128)(2,1)S(1)}, bf16[144,256]{1,0:T(8,128)(2,1)S(1)}, u32[]{:S(2)}, u32[]{:S(2)}) collective-permute-start(bf16[144,256]{1,0:T(8,128)(2,1)S(1)} %get-tuple-element.31), channel_id=1, source_target_pairs={{0,2},{1,3},{2,0},{3,1},{4,6},{5,7},{6,4},{7,5},{8,10},{9,11},{10,... | collective-permute-start | bytes 221192 | tf_op jit(solution)/shard_map/ppermute | solution.py:386
  9.6 6.2 %collective-permute-start.2 = (bf16[144,256]{1,0:T(8,128)(2,1)S(1)}, bf16[144,256]{1,0:T(8,128)(2,1)S(1)}, u32[]{:S(2)}, u32[]{:S(2)}) collective-permute-start(bf16[144,256]{1,0:T(8,128)(2,1)S(1)} %get-tuple-element.31), channel_id=1, source_target_pairs={{0,3},{1,0},{2,1},{3,2},{4,7},{5,4},{6,5},{7,6},{8,11},{9,8},{10,9... | collective-permute-start | bytes 221192 | tf_op jit(solution)/shard_map/ppermute | solution.py:386
  10.3 5.5 %collective-permute-start = (bf16[144,256]{1,0:T(8,128)(2,1)S(1)}, bf16[144,256]{1,0:T(8,128)(2,1)S(1)}, u32[]{:S(2)}, u32[]{:S(2)}) collective-permute-start(bf16[144,256]{1,0:T(8,128)(2,1)S(1)} %get-tuple-element.31), channel_id=1, source_target_pairs={{0,1},{1,2},{2,3},{3,0},{4,5},{5,6},{6,7},{7,4},{8,9},{9,10},{10,1... | collective-permute-start | bytes 221192 | tf_op jit(solution)/shard_map/ppermute | solution.py:386
  11.0 3.4 %collective-permute-start.3 = (bf16[128,256]{1,0:T(8,128)(2,1)S(1)}, bf16[128,256]{1,0:T(8,128)(2,1)S(1)}, u32[]{:S(2)}, u32[]{:S(2)}) collective-permute-start(bf16[128,256]{1,0:T(8,128)(2,1)S(1)} %get-tuple-element.32), channel_id=1, source_target_pairs={{0,12},{1,13},{2,14},{3,15},{4,0},{5,1},{6,2},{7,3},{8,4},{9,5},{1... | collective-permute-start | bytes 196616 | tf_op jit(solution)/shard_map/ppermute | solution.py:389
  11.5 4.3 %collective-permute-start.1 = (bf16[128,256]{1,0:T(8,128)(2,1)S(1)}, bf16[128,256]{1,0:T(8,128)(2,1)S(1)}, u32[]{:S(2)}, u32[]{:S(2)}) collective-permute-start(bf16[128,256]{1,0:T(8,128)(2,1)S(1)} %get-tuple-element.32), channel_id=1, source_target_pairs={{0,4},{1,5},{2,6},{3,7},{4,8},{5,9},{6,10},{7,11},{8,12},{9,13},{1... | collective-permute-start | bytes 196616 | tf_op jit(solution)/shard_map/ppermute | solution.py:389
  15.9 6.8 %collective-permute-start.11 = (bf16[4,128,256]{2,1,0:T(8,128)(2,1)S(1)}, bf16[4,128,256]{2,1,0:T(8,128)(2,1)S(1)}, u32[]{:S(2)}, u32[]{:S(2)}) collective-permute-start(bf16[4,128,256]{2,1,0:T(8,128)(2,1)S(1)} %pad_maximum_fusion.1.t0), channel_id=1, source_target_pairs={{0,2},{1,3},{2,0},{3,1},{4,6},{5,7},{6,4},{7,5},{8,10},{9,11},{10,... | collective-permute-start | bytes 786440 | tf_op jit(solution)/shard_map/ppermute | solution.py:386
  16.8 12.7 %collective-permute-start.10 = (bf16[4,144,256]{2,1,0:T(8,128)(2,1)S(1)}, bf16[4,144,256]{2,1,0:T(8,128)(2,1)S(1)}, u32[]{:S(2)}, u32[]{:S(2)}) collective-permute-start(bf16[4,144,256]{2,1,0:T(8,128)(2,1)S(1)} %pad_maximum_fusion.f0), channel_id=1, source_target_pairs={{0,8},{1,9},{2,10},{3,11},{4,12},{5,13},{6,14},{7,15},{8,0},{9,1},... | collective-permute-start | bytes 884744 | tf_op jit(solution)/shard_map/ppermute | solution.py:389
  17.6 12.8 %collective-permute-start.8 = (bf16[4,144,256]{2,1,0:T(8,128)(2,1)S(1)}, bf16[4,144,256]{2,1,0:T(8,128)(2,1)S(1)}, u32[]{:S(2)}, u32[]{:S(2)}) collective-permute-start(bf16[4,144,256]{2,1,0:T(8,128)(2,1)S(1)} %pad_maximum_fusion.f0), channel_id=1, source_target_pairs={{0,12},{1,13},{2,14},{3,15},{4,0},{5,1},{6,2},{7,3},{8,4},{9,5},{1... | collective-permute-start | bytes 884744 | tf_op jit(solution)/shard_map/ppermute | solution.py:389
  19.2 12.8 %collective-permute-start.6 = (bf16[4,144,256]{2,1,0:T(8,128)(2,1)S(1)}, bf16[4,144,256]{2,1,0:T(8,128)(2,1)S(1)}, u32[]{:S(2)}, u32[]{:S(2)}) collective-permute-start(bf16[4,144,256]{2,1,0:T(8,128)(2,1)S(1)} %pad_maximum_fusion.f0), channel_id=1, source_target_pairs={{0,4},{1,5},{2,6},{3,7},{4,8},{5,9},{6,10},{7,11},{8,12},{9,13},{1... | collective-permute-start | bytes 884744 | tf_op jit(solution)/shard_map/ppermute | solution.py:389
  19.2 8.1 %collective-permute-start.9 = (bf16[4,128,256]{2,1,0:T(8,128)(2,1)S(1)}, bf16[4,128,256]{2,1,0:T(8,128)(2,1)S(1)}, u32[]{:S(2)}, u32[]{:S(2)}) collective-permute-start(bf16[4,128,256]{2,1,0:T(8,128)(2,1)S(1)} %pad_maximum_fusion.1.t0), channel_id=1, source_target_pairs={{0,3},{1,0},{2,1},{3,2},{4,7},{5,4},{6,5},{7,6},{8,11},{9,8},{10,9... | collective-permute-start | bytes 786440 | tf_op jit(solution)/shard_map/ppermute | solution.py:386
  22.7 6.8 %collective-permute-start.7 = (bf16[4,128,256]{2,1,0:T(8,128)(2,1)S(1)}, bf16[4,128,256]{2,1,0:T(8,128)(2,1)S(1)}, u32[]{:S(2)}, u32[]{:S(2)}) collective-permute-start(bf16[4,128,256]{2,1,0:T(8,128)(2,1)S(1)} %pad_maximum_fusion.1.t0), channel_id=1, source_target_pairs={{0,1},{1,2},{2,3},{3,0},{4,5},{5,6},{6,7},{7,4},{8,9},{9,10},{10,1... | collective-permute-start | bytes 786440 | tf_op jit(solution)/shard_map/ppermute | solution.py:386
  33.9 9.2 %collective-permute-start.14 = (bf16[288,512]{1,0:T(8,128)(2,1)S(1)}, bf16[288,512]{1,0:T(8,128)(2,1)S(1)}, u32[]{:S(2)}, u32[]{:S(2)}) collective-permute-start(bf16[288,512]{1,0:T(8,128)(2,1)S(1)} %get-tuple-element.51.s0), channel_id=1, source_target_pairs={{0,96},{16,112},{32,0},{48,16},{64,32},{80,48},{96,64},{112,80},{1... | collective-permute-start | bytes 884744 | tf_op jit(solution)/shard_map/ppermute | solution.py:473
  36.4 13.6 %collective-permute-start.13 = (bf16[288,512]{1,0:T(8,128)(2,1)S(1)}, bf16[288,512]{1,0:T(8,128)(2,1)S(1)}, u32[]{:S(2)}, u32[]{:S(2)}) collective-permute-start(bf16[288,512]{1,0:T(8,128)(2,1)S(1)} %get-tuple-element.51.s0), channel_id=1, source_target_pairs={{0,64},{16,80},{32,96},{48,112},{64,0},{80,16},{96,32},{112,48},{1... | collective-permute-start | bytes 884744 | tf_op jit(solution)/shard_map/ppermute | solution.py:473
  36.9 14.6 %collective-permute-start.12 = (bf16[288,512]{1,0:T(8,128)(2,1)S(1)}, bf16[288,512]{1,0:T(8,128)(2,1)S(1)}, u32[]{:S(2)}, u32[]{:S(2)}) collective-permute-start(bf16[288,512]{1,0:T(8,128)(2,1)S(1)} %get-tuple-element.51.s0), channel_id=1, source_target_pairs={{0,32},{16,48},{32,64},{48,80},{64,96},{80,112},{96,0},{112,16},{1... | collective-permute-start | bytes 884744 | tf_op jit(solution)/shard_map/ppermute | solution.py:473
  37.5 16.8 %collective-permute-start.15 = (bf16[288,512]{1,0:T(8,128)(2,1)S(1)}, bf16[288,512]{1,0:T(8,128)(2,1)S(1)}, u32[]{:S(2)}, u32[]{:S(2)}) collective-permute-start(bf16[288,512]{1,0:T(8,128)(2,1)S(1)} %get-tuple-element.51.s0), channel_id=1, source_target_pairs={{0,16},{16,0},{32,48},{48,32},{64,80},{80,64},{96,112},{112,96},{1... | collective-permute-start | bytes 884744 | tf_op jit(solution)/shard_map/ppermute | solution.py:476
  43.0 11.4 %collective-permute-start.18 = (bf16[288,512]{1,0:T(8,128)(2,1)S(1)}, bf16[288,512]{1,0:T(8,128)(2,1)S(1)}, u32[]{:S(2)}, u32[]{:S(2)}) collective-permute-start(bf16[288,512]{1,0:T(8,128)(2,1)S(1)} %collective-permute-done.14.s3), channel_id=1, source_target_pairs={{0,16},{16,0},{32,48},{48,32},{64,80},{80,64},{96,112},{112,96},{1... | collective-permute-start | bytes 884744 | tf_op jit(solution)/shard_map/ppermute | solution.py:476
  50.0 4.4 %collective-permute-start.17 = (bf16[288,512]{1,0:T(8,128)(2,1)S(1)}, bf16[288,512]{1,0:T(8,128)(2,1)S(1)}, u32[]{:S(2)}, u32[]{:S(2)}) collective-permute-start(bf16[288,512]{1,0:T(8,128)(2,1)S(1)} %collective-permute-done.13.s2), channel_id=1, source_target_pairs={{0,16},{16,0},{32,48},{48,32},{64,80},{80,64},{96,112},{112,96},{1... | collective-permute-start | bytes 884744 | tf_op jit(solution)/shard_map/ppermute | solution.py:476
  51.5 3.3 %collective-permute-start.16 = (bf16[288,512]{1,0:T(8,128)(2,1)S(1)}, bf16[288,512]{1,0:T(8,128)(2,1)S(1)}, u32[]{:S(2)}, u32[]{:S(2)}) collective-permute-start(bf16[288,512]{1,0:T(8,128)(2,1)S(1)} %collective-permute-done.12.s1), channel_id=1, source_target_pairs={{0,16},{16,0},{32,48},{48,32},{64,80},{80,64},{96,112},{112,96},{1... | collective-permute-start | bytes 884744 | tf_op jit(solution)/shard_map/ppermute | solution.py:476
  54.4 34.4 %copy-start = (bf16[1,32,32]{2,1,0:T(8,128)(2,1)S(1)}, bf16[1,32,32]{2,1,0:T(8,128)(2,1)}, u32[]{:S(2)}) copy-start(bf16[1,32,32]{2,1,0:T(8,128)(2,1)} %param.11) | copy-start | bytes 6148

commit v7 on v6

--- a/solution.py
+++ b/solution.py
@@ -223,12 +223,20 @@
         place = jnp.where(cols == position(down, offs[g]), 1.0, 0.0).astype(BF)
         g_s[g] = dot_nn(place, grad_ref[g]).astype(BF)
 
-    def each(count, body):
+    def each(count, body, most):
         def step(p, carry):
             body(p)
             return carry
 
-        lax.fori_loop(0, count, step, 0)
+        def flat():
+            for p in range(most):
+                body(p)
+
+        pl.when(count == most)(flat)
+        def rolled():
+            lax.fori_loop(0, count, step, 0)
+
+        pl.when(count < most)(rolled)
 
     k_col = lax.broadcasted_iota(jnp.int32, (1, 2 * BLOCK), 1)
     in_image = k_col < 2 * PATCHES
@@ -250,7 +258,7 @@
             scores[n, p] = s
 
     score(chip, True)
-    each(chip, score)
+    each(chip, score, 3)
 
     o_s[...] = jnp.zeros_like(o_s)
     l_s[...] = jnp.zeros_like(l_s)
@@ -266,7 +274,7 @@
             o_s[n] += dot_nn(lifted, values[g, p, :, heads(h)])
             probs[n, p] = lifted
 
-    each(chip + 1, weigh)
+    each(chip + 1, weigh, 4)
 
     xs = []
     for g in range(NSEQ):
@@ -310,7 +318,7 @@
                 stack += [ds[:, 0 : 2 * PATCHES], ds_text, probs[n, p, :, 0 : 2 * PATCHES]]
             zt[g, p] = dot_nn(xs[g], jnp.concatenate(stack, axis=0))
 
-    each(chip + 1, differentiate)
+    each(chip + 1, differentiate, 4)
 
     for g in range(NSEQ):
         own = jnp.zeros((PDIM, PATCHES), F32)

time: 90 us -> 88.7 us (0.986)
  blocking collectives: 26 us -> 24.5 us
    all_to_all x1, blocking collectives: 26 us -> 24.5 us  [on_device(): lax.all_to_all(z.reshape(groups * seats, 8, 128), ('dp', 'seq'), 0, 0)]
where the time goes in v7:
time: 88.7 us; the launch traced here: 88.6 us
  starting transfers between devices  34 us (38%)
  blocking collectives  24.5 us (28%)
  Pallas kernels  17 us (19%)
  waiting for transfers between devices  12.2 us (14%)
    all_to_all x1, blocking collectives, on_device(): lax.all_to_all(z.reshape(groups * seats, 8, 128), ('dp', 'seq'), 0, 0)  24.5 us
    ppermute x4, starting transfers between devices, on_device(): lax.ppermute(hop, 'seq', [(i, i ^ 1) for i in range(seats)])  14.4 us
    ppermute x6, starting transfers between devices, shift_z(): lax.ppermute(x, 'dp', [(i, (i + side * k) % groups) for i in range(groups)])  8.34 us
    pallas_call x1, Pallas kernels, attend(): pl.pallas_call(attend_kernel, out_shape=(jax.ShapeDtypeStruct((NSEQ, BLOC...  8.06 us
    ppermute x6, starting transfers between devices, shift_y(): return lax.ppermute(x, 'dp', pairs)  7.62 us
    ppermute x6, waiting for transfers between devices, shift_z(): lax.ppermute(x, 'dp', [(i, (i + side * k) % groups) for i in range(groups)])  5.76 us
    ppermute x6, waiting for transfers between devices, shift_y(): return lax.ppermute(x, 'dp', pairs)  4.28 us
    pallas_call x1, Pallas kernels, on_device(): pl.pallas_call(fold_kernel, out_shape=(weight, weight, weight, jax.ShapeD...  3.7 us
  transfers between devices with their start and end apart: 19, of which 10 were waited for; matrix products, arithmetic and copies ran while one was open for 0% of the time, Pallas kernels for 5%

profile of v7, /device:TPU:1, one launch (start us, length us, event | category | flops | bytes accessed | tf_op | source)
XLA Modules:
  0.0 88.6 jit_solution(17543945183180712030)
XLA Ops:
  0.6 1.5 %pack.1 = (bf16[144,256]{1,0:T(8,128)(2,1)S(1)}, bf16[128,256]{1,0:T(8,128)(2,1)S(1)}, f32[32,128]{1,0:T(8,128)S(1)}, bf16[32,4096]{1,0:T(8,128)(2,1)S(1)}) custom-call(s32[16]{0:T(128)} %seq_hbm.3, s32[16]{0:T(128)} %start_hbm.3, s32[1]{0:T(128)} %bitcast.seat_ref, bf16[2,384,256]{2,1,0:T(8,128)(2,1)} %text_hbm.1, bf16[32,32]{1,0:T(8,128)(2,1)} %bitcast.17, ...), custom_call_target="tpu_custom_call" | custom-call | tf_op jit(solution)/shard_map/pack/pallas_call | solution.py:403
  2.1 4.5 %collective-permute-start.5 = (bf16[128,256]{1,0:T(8,128)(2,1)S(1)}, bf16[128,256]{1,0:T(8,128)(2,1)S(1)}, u32[]{:S(2)}, u32[]{:S(2)}) collective-permute-start(bf16[128,256]{1,0:T(8,128)(2,1)S(1)} %get-tuple-element.32), channel_id=1, source_target_pairs={{0,8},{1,9},{2,10},{3,11},{4,12},{5,13},{6,14},{7,15},{8,0},{9,1},... | collective-permute-start | bytes 196616 | tf_op jit(solution)/shard_map/ppermute | solution.py:397
  6.6 2.9 %collective-permute-start.4 = (bf16[144,256]{1,0:T(8,128)(2,1)S(1)}, bf16[144,256]{1,0:T(8,128)(2,1)S(1)}, u32[]{:S(2)}, u32[]{:S(2)}) collective-permute-start(bf16[144,256]{1,0:T(8,128)(2,1)S(1)} %get-tuple-element.31), channel_id=1, source_target_pairs={{0,2},{1,3},{2,0},{3,1},{4,6},{5,7},{6,4},{7,5},{8,10},{9,11},{10,... | collective-permute-start | bytes 221192 | tf_op jit(solution)/shard_map/ppermute | solution.py:394
  9.6 0.8 collective-permute-start.2
  10.3 0.7 collective-permute-start
  11.0 0.4 collective-permute-start.3
  11.5 0.0 collective-permute-done.5
  11.5 1.0 %collective-permute-start.1 = (bf16[128,256]{1,0:T(8,128)(2,1)S(1)}, bf16[128,256]{1,0:T(8,128)(2,1)S(1)}, u32[]{:S(2)}, u32[]{:S(2)}) collective-permute-start(bf16[128,256]{1,0:T(8,128)(2,1)S(1)} %get-tuple-element.32), channel_id=1, source_target_pairs={{0,4},{1,5},{2,6},{3,7},{4,8},{5,9},{6,10},{7,11},{8,12},{9,13},{1... | collective-permute-start | bytes 196616 | tf_op jit(solution)/shard_map/ppermute | solution.py:397
  12.5 1.9 %collective-permute-done.3 = bf16[128,256]{1,0:T(8,128)(2,1)S(1)} collective-permute-done((bf16[128,256]{1,0:T(8,128)(2,1)S(1)}, bf16[128,256]{1,0:T(8,128)(2,1)S(1)}, u32[]{:S(2)}, u32[]{:S(2)}) %collective-permute-start.3) | collective-permute-done | bytes 65568 | tf_op jit(solution)/shard_map/ppermute | solution.py:397
  14.4 1.4 %collective-permute-done.1 = bf16[128,256]{1,0:T(8,128)(2,1)S(1)} collective-permute-done((bf16[128,256]{1,0:T(8,128)(2,1)S(1)}, bf16[128,256]{1,0:T(8,128)(2,1)S(1)}, u32[]{:S(2)}, u32[]{:S(2)}) %collective-permute-start.1) | collective-permute-done | bytes 65568 | tf_op jit(solution)/shard_map/ppermute | solution.py:397
  15.8 0.0 collective-permute-done.4
  15.8 0.0 collective-permute-done.2
  15.8 0.0 collective-permute-done
  15.9 0.9 %collective-permute-start.11 = (bf16[4,128,256]{2,1,0:T(8,128)(2,1)S(1)}, bf16[4,128,256]{2,1,0:T(8,128)(2,1)S(1)}, u32[]{:S(2)}, u32[]{:S(2)}) collective-permute-start(bf16[4,128,256]{2,1,0:T(8,128)(2,1)S(1)} %pad_maximum_fusion.1.t0), channel_id=1, source_target_pairs={{0,2},{1,3},{2,0},{3,1},{4,6},{5,7},{6,4},{7,5},{8,10},{9,11},{10,... | collective-permute-start | bytes 786440 | tf_op jit(solution)/shard_map/ppermute | solution.py:394
  16.8 0.7 collective-permute-start.10
  17.6 1.6 %collective-permute-start.8 = (bf16[4,144,256]{2,1,0:T(8,128)(2,1)S(1)}, bf16[4,144,256]{2,1,0:T(8,128)(2,1)S(1)}, u32[]{:S(2)}, u32[]{:S(2)}) collective-permute-start(bf16[4,144,256]{2,1,0:T(8,128)(2,1)S(1)} %pad_maximum_fusion.f0), channel_id=1, source_target_pairs={{0,12},{1,13},{2,14},{3,15},{4,0},{5,1},{6,2},{7,3},{8,4},{9,5},{1... | collective-permute-start | bytes 884744 | tf_op jit(solution)/shard_map/ppermute | solution.py:397
  19.2 0.0 collective-permute-start.6
  19.2 1.9 %collective-permute-start.9 = (bf16[4,128,256]{2,1,0:T(8,128)(2,1)S(1)}, bf16[4,128,256]{2,1,0:T(8,128)(2,1)S(1)}, u32[]{:S(2)}, u32[]{:S(2)}) collective-permute-start(bf16[4,128,256]{2,1,0:T(8,128)(2,1)S(1)} %pad_maximum_fusion.1.t0), channel_id=1, source_target_pairs={{0,3},{1,0},{2,1},{3,2},{4,7},{5,4},{6,5},{7,6},{8,11},{9,8},{10,9... | collective-permute-start | bytes 786440 | tf_op jit(solution)/shard_map/ppermute | solution.py:394
  21.1 1.6 %collective-permute-done.11.t3 = bf16[4,128,256]{2,1,0:T(8,128)(2,1)S(1)} collective-permute-done((bf16[4,128,256]{2,1,0:T(8,128)(2,1)S(1)}, bf16[4,128,256]{2,1,0:T(8,128)(2,1)S(1)}, u32[]{:S(2)}, u32[]{:S(2)}) %collective-permute-start.11) | collective-permute-done | bytes 262176 | tf_op jit(solution)/shard_map/ppermute | solution.py:394
  22.7 0.4 collective-permute-start.7
  23.1 3.7 %fold.1 = (bf16[4096,256]{1,0:T(8,128)(2,1)S(1)}, bf16[4096,256]{1,0:T(8,128)(2,1)S(1)}, bf16[4096,256]{1,0:T(8,128)(2,1)S(1)}, bf16[32,768]{1,0:T(8,128)(2,1)S(...) custom-call(bf16[32,4096]{1,0:T(8,128)(2,1)S(1)} %get-tuple-element.47.embedded_ref, bf16[32,4096]{1,0:T(8,128)(2,1)} %wp_hbm.3, ...), custom_call_target="tpu_custom_call" | custom-call | tf_op jit(solution)/shard_map/fold/pallas_call | solution.py:440
  26.8 0.5 collective-permute-done.9.t2
  27.3 2.2 %collective-permute-done.7.t1 = bf16[4,128,256]{2,1,0:T(8,128)(2,1)S(1)} collective-permute-done((bf16[4,128,256]{2,1,0:T(8,128)(2,1)S(1)}, bf16[4,128,256]{2,1,0:T(8,128)(2,1)S(1)}, u32[]{:S(2)}, u32[]{:S(2)}) %collective-permute-start.7) | collective-permute-done | bytes 262176 | tf_op jit(solution)/shard_map/ppermute | solution.py:394
  29.5 0.0 collective-permute-done.10.f3
  29.5 0.9 %collective-permute-done.8.f2 = bf16[4,144,256]{2,1,0:T(8,128)(2,1)S(1)} collective-permute-done((bf16[4,144,256]{2,1,0:T(8,128)(2,1)S(1)}, bf16[4,144,256]{2,1,0:T(8,128)(2,1)S(1)}, u32[]{:S(2)}, u32[]{:S(2)}) %collective-permute-start.8) | collective-permute-done | bytes 294944 | tf_op jit(solution)/shard_map/ppermute | solution.py:397
  30.4 1.6 %collective-permute-done.6.f1 = bf16[4,144,256]{2,1,0:T(8,128)(2,1)S(1)} collective-permute-done((bf16[4,144,256]{2,1,0:T(8,128)(2,1)S(1)}, bf16[4,144,256]{2,1,0:T(8,128)(2,1)S(1)}, u32[]{:S(2)}, u32[]{:S(2)}) %collective-permute-start.6) | collective-permute-done | bytes 294944 | tf_op jit(solution)/shard_map/ppermute | solution.py:397
  32.0 1.9 %project.1 = (bf16[288,512]{1,0:T(8,128)(2,1)S(1)}, bf16[256,4096]{1,0:T(8,128)(2,1)S(1)}, f32[256,128]{1,0:T(8,128)S(1)}) custom-call(s32[1]{0:T(128)} %bitcast.1.group_ref, bf16[4,144,256]{2,1,0:T(8,128)(2,1)S(1)} %pad_maximum_fusion.f0, bf16[4,144,256]{2,1,0:T(8,128)(2,1)S(1)} %collective-permute-done.6.f1, ...), custom_call_target="tpu_custom_call" | custom-call | tf_op jit(solution)/shard_map/project/pallas_call | solution.py:459
  33.9 2.5 %collective-permute-start.14 = (bf16[288,512]{1,0:T(8,128)(2,1)S(1)}, bf16[288,512]{1,0:T(8,128)(2,1)S(1)}, u32[]{:S(2)}, u32[]{:S(2)}) collective-permute-start(bf16[288,512]{1,0:T(8,128)(2,1)S(1)} %get-tuple-element.51.s0), channel_id=1, source_target_pairs={{0,96},{16,112},{32,0},{48,16},{64,32},{80,48},{96,64},{112,80},{1... | collective-permute-start | bytes 884744 | tf_op jit(solution)/shard_map/ppermute | solution.py:481
  36.4 0.5 collective-permute-start.13
  36.9 0.6 collective-permute-start.12
  37.5 4.6 %collective-permute-start.15 = (bf16[288,512]{1,0:T(8,128)(2,1)S(1)}, bf16[288,512]{1,0:T(8,128)(2,1)S(1)}, u32[]{:S(2)}, u32[]{:S(2)}) collective-permute-start(bf16[288,512]{1,0:T(8,128)(2,1)S(1)} %get-tuple-element.51.s0), channel_id=1, source_target_pairs={{0,16},{16,0},{32,48},{48,32},{64,80},{80,64},{96,112},{112,96},{1... | collective-permute-start | bytes 884744 | tf_op jit(solution)/shard_map/ppermute | solution.py:484
  42.2 0.9 collective-permute-done.14.s3
  43.0 6.9 %collective-permute-start.18 = (bf16[288,512]{1,0:T(8,128)(2,1)S(1)}, bf16[288,512]{1,0:T(8,128)(2,1)S(1)}, u32[]{:S(2)}, u32[]{:S(2)}) collective-permute-start(bf16[288,512]{1,0:T(8,128)(2,1)S(1)} %collective-permute-done.14.s3), channel_id=1, source_target_pairs={{0,16},{16,0},{32,48},{48,32},{64,80},{80,64},{96,112},{112,96},{1... | collective-permute-start | bytes 884744 | tf_op jit(solution)/shard_map/ppermute | solution.py:484
  50.0 0.0 collective-permute-done.13.s2
  50.0 0.7 collective-permute-start.17
  50.6 0.9 collective-permute-done.12.s1
  51.5 2.1 %collective-permute-start.16 = (bf16[288,512]{1,0:T(8,128)(2,1)S(1)}, bf16[288,512]{1,0:T(8,128)(2,1)S(1)}, u32[]{:S(2)}, u32[]{:S(2)}) collective-permute-start(bf16[288,512]{1,0:T(8,128)(2,1)S(1)} %collective-permute-done.12.s1), channel_id=1, source_target_pairs={{0,16},{16,0},{32,48},{48,32},{64,80},{80,64},{96,112},{112,96},{1... | collective-permute-start | bytes 884744 | tf_op jit(solution)/shard_map/ppermute | solution.py:484
  53.7 0.7 query.1.qt_ref
  54.4 0.0 copy-start
  54.4 0.0 collective-permute-done.15.o0
  54.4 0.0 collective-permute-done.18.o3
  54.4 0.0 collective-permute-done.17.o2
  54.4 0.5 collective-permute-done.16.o1
  54.9 8.1 %attend.1 = (bf16[2,384,256]{2,1,0:T(8,128)(2,1)}, bf16[16,64,128]{2,1,0:T(8,128)(2,1)S(1)}) custom-call(s32[16]{0:T(128)} %seq_hbm.3, s32[16]{0:T(128)} %start_hbm.3, s32[1]{0:T(128)} %bitcast.seat_ref, bf16[288,512]{1,0:T(8,128)(2,1)S(1)} %get-tuple-element.51.s0, bf16[288,512]{1,0:T(8,128)(2,1)S(1)} %collective-permute-done.12.s1, ...), custom_call_target="tpu_custom_call" | custom-call | tf_op jit(solution)/shard_map/attend/pallas_call | solution.py:338
  62.9 24.5 %all_to_all.5.recv_ref = bf16[128,8,128]{2,1,0:T(8,128)(2,1)S(1)} all-to-all(bf16[128,8,128]{2,1,0:T(8,128)(2,1)S(1)} %bitcast.14), channel_id=1, replica_groups=mesh['seq'=8,'dp'=16] {'dp','seq'}, dimensions={0} | all-to-all | bytes 524288 | tf_op jit(solution)/shard_map/all_to_all | solution.py:486
  87.4 0.0 copy-done
  87.5 1.1 %finish.1 = f32[32,32]{1,0:T(8,128)} custom-call(bf16[128,8,128]{2,1,0:T(8,128)(2,1)S(1)} %all_to_all.5.recv_ref, bf16[32,32]{1,0:T(8,128)(2,1)S(1)} %bitcast.18, f32[32,128]{1,0:T(8,128)S(1)} %get-tuple-element.58.inv_ref, f32[32,32]{1,0:T(8,128)S(1)} %get-tuple-element.59.u_ref), custom_call_target="tpu_custom_call" | custom-call | tf_op jit(solution)/shard_map/finish/pallas_call | solution.py:487
  (2 shorter events, 0.1 us)
Async XLA Ops:
  2.1 9.3 %collective-permute-start.5 = (bf16[128,256]{1,0:T(8,128)(2,1)S(1)}, bf16[128,256]{1,0:T(8,128)(2,1)S(1)}, u32[]{:S(2)}, u32[]{:S(2)}) collective-permute-start(bf16[128,256]{1,0:T(8,128)(2,1)S(1)} %get-tuple-element.32), channel_id=1, source_target_pairs={{0,8},{1,9},{2,10},{3,11},{4,12},{5,13},{6,14},{7,15},{8,0},{9,1},... | collective-permute-start | bytes 196616 | tf_op jit(solution)/shard_map/ppermute | solution.py:397
  6.6 9.2 %collective-permute-start.4 = (bf16[144,256]{1,0:T(8,128)(2,1)S(1)}, bf16[144,256]{1,0:T(8,128)(2,1)S(1)}, u32[]{:S(2)}, u32[]{:S(2)}) collective-permute-start(bf16[144,256]{1,0:T(8,128)(2,1)S(1)} %get-tuple-element.31), channel_id=1, source_target_pairs={{0,2},{1,3},{2,0},{3,1},{4,6},{5,7},{6,4},{7,5},{8,10},{9,11},{10,... | collective-permute-start | bytes 221192 | tf_op jit(solution)/shard_map/ppermute | solution.py:394
  9.6 6.2 %collective-permute-start.2 = (bf16[144,256]{1,0:T(8,128)(2,1)S(1)}, bf16[144,256]{1,0:T(8,128)(2,1)S(1)}, u32[]{:S(2)}, u32[]{:S(2)}) collective-permute-start(bf16[144,256]{1,0:T(8,128)(2,1)S(1)} %get-tuple-element.31), channel_id=1, source_target_pairs={{0,3},{1,0},{2,1},{3,2},{4,7},{5,4},{6,5},{7,6},{8,11},{9,8},{10,9... | collective-permute-start | bytes 221192 | tf_op jit(solution)/shard_map/ppermute | solution.py:394
  10.3 5.5 %collective-permute-start = (bf16[144,256]{1,0:T(8,128)(2,1)S(1)}, bf16[144,256]{1,0:T(8,128)(2,1)S(1)}, u32[]{:S(2)}, u32[]{:S(2)}) collective-permute-start(bf16[144,256]{1,0:T(8,128)(2,1)S(1)} %get-tuple-element.31), channel_id=1, source_target_pairs={{0,1},{1,2},{2,3},{3,0},{4,5},{5,6},{6,7},{7,4},{8,9},{9,10},{10,1... | collective-permute-start | bytes 221192 | tf_op jit(solution)/shard_map/ppermute | solution.py:394
  11.0 3.4 %collective-permute-start.3 = (bf16[128,256]{1,0:T(8,128)(2,1)S(1)}, bf16[128,256]{1,0:T(8,128)(2,1)S(1)}, u32[]{:S(2)}, u32[]{:S(2)}) collective-permute-start(bf16[128,256]{1,0:T(8,128)(2,1)S(1)} %get-tuple-element.32), channel_id=1, source_target_pairs={{0,12},{1,13},{2,14},{3,15},{4,0},{5,1},{6,2},{7,3},{8,4},{9,5},{1... | collective-permute-start | bytes 196616 | tf_op jit(solution)/shard_map/ppermute | solution.py:397
  11.5 4.3 %collective-permute-start.1 = (bf16[128,256]{1,0:T(8,128)(2,1)S(1)}, bf16[128,256]{1,0:T(8,128)(2,1)S(1)}, u32[]{:S(2)}, u32[]{:S(2)}) collective-permute-start(bf16[128,256]{1,0:T(8,128)(2,1)S(1)} %get-tuple-element.32), channel_id=1, source_target_pairs={{0,4},{1,5},{2,6},{3,7},{4,8},{5,9},{6,10},{7,11},{8,12},{9,13},{1... | collective-permute-start | bytes 196616 | tf_op jit(solution)/shard_map/ppermute | solution.py:397
  15.9 6.8 %collective-permute-start.11 = (bf16[4,128,256]{2,1,0:T(8,128)(2,1)S(1)}, bf16[4,128,256]{2,1,0:T(8,128)(2,1)S(1)}, u32[]{:S(2)}, u32[]{:S(2)}) collective-permute-start(bf16[4,128,256]{2,1,0:T(8,128)(2,1)S(1)} %pad_maximum_fusion.1.t0), channel_id=1, source_target_pairs={{0,2},{1,3},{2,0},{3,1},{4,6},{5,7},{6,4},{7,5},{8,10},{9,11},{10,... | collective-permute-start | bytes 786440 | tf_op jit(solution)/shard_map/ppermute | solution.py:394
  16.8 12.7 %collective-permute-start.10 = (bf16[4,144,256]{2,1,0:T(8,128)(2,1)S(1)}, bf16[4,144,256]{2,1,0:T(8,128)(2,1)S(1)}, u32[]{:S(2)}, u32[]{:S(2)}) collective-permute-start(bf16[4,144,256]{2,1,0:T(8,128)(2,1)S(1)} %pad_maximum_fusion.f0), channel_id=1, source_target_pairs={{0,8},{1,9},{2,10},{3,11},{4,12},{5,13},{6,14},{7,15},{8,0},{9,1},... | collective-permute-start | bytes 884744 | tf_op jit(solution)/shard_map/ppermute | solution.py:397
  17.6 12.8 %collective-permute-start.8 = (bf16[4,144,256]{2,1,0:T(8,128)(2,1)S(1)}, bf16[4,144,256]{2,1,0:T(8,128)(2,1)S(1)}, u32[]{:S(2)}, u32[]{:S(2)}) collective-permute-start(bf16[4,144,256]{2,1,0:T(8,128)(2,1)S(1)} %pad_maximum_fusion.f0), channel_id=1, source_target_pairs={{0,12},{1,13},{2,14},{3,15},{4,0},{5,1},{6,2},{7,3},{8,4},{9,5},{1... | collective-permute-start | bytes 884744 | tf_op jit(solution)/shard_map/ppermute | solution.py:397
  19.2 12.8 %collective-permute-start.6 = (bf16[4,144,256]{2,1,0:T(8,128)(2,1)S(1)}, bf16[4,144,256]{2,1,0:T(8,128)(2,1)S(1)}, u32[]{:S(2)}, u32[]{:S(2)}) collective-permute-start(bf16[4,144,256]{2,1,0:T(8,128)(2,1)S(1)} %pad_maximum_fusion.f0), channel_id=1, source_target_pairs={{0,4},{1,5},{2,6},{3,7},{4,8},{5,9},{6,10},{7,11},{8,12},{9,13},{1... | collective-permute-start | bytes 884744 | tf_op jit(solution)/shard_map/ppermute | solution.py:397
  19.2 8.1 %collective-permute-start.9 = (bf16[4,128,256]{2,1,0:T(8,128)(2,1)S(1)}, bf16[4,128,256]{2,1,0:T(8,128)(2,1)S(1)}, u32[]{:S(2)}, u32[]{:S(2)}) collective-permute-start(bf16[4,128,256]{2,1,0:T(8,128)(2,1)S(1)} %pad_maximum_fusion.1.t0), channel_id=1, source_target_pairs={{0,3},{1,0},{2,1},{3,2},{4,7},{5,4},{6,5},{7,6},{8,11},{9,8},{10,9... | collective-permute-start | bytes 786440 | tf_op jit(solution)/shard_map/ppermute | solution.py:394
  22.7 6.8 %collective-permute-start.7 = (bf16[4,128,256]{2,1,0:T(8,128)(2,1)S(1)}, bf16[4,128,256]{2,1,0:T(8,128)(2,1)S(1)}, u32[]{:S(2)}, u32[]{:S(2)}) collective-permute-start(bf16[4,128,256]{2,1,0:T(8,128)(2,1)S(1)} %pad_maximum_fusion.1.t0), channel_id=1, source_target_pairs={{0,1},{1,2},{2,3},{3,0},{4,5},{5,6},{6,7},{7,4},{8,9},{9,10},{10,1... | collective-permute-start | bytes 786440 | tf_op jit(solution)/shard_map/ppermute | solution.py:394
  33.9 9.2 %collective-permute-start.14 = (bf16[288,512]{1,0:T(8,128)(2,1)S(1)}, bf16[288,512]{1,0:T(8,128)(2,1)S(1)}, u32[]{:S(2)}, u32[]{:S(2)}) collective-permute-start(bf16[288,512]{1,0:T(8,128)(2,1)S(1)} %get-tuple-element.51.s0), channel_id=1, source_target_pairs={{0,96},{16,112},{32,0},{48,16},{64,32},{80,48},{96,64},{112,80},{1... | collective-permute-start | bytes 884744 | tf_op jit(solution)/shard_map/ppermute | solution.py:481
  36.4 13.6 %collective-permute-start.13 = (bf16[288,512]{1,0:T(8,128)(2,1)S(1)}, bf16[288,512]{1,0:T(8,128)(2,1)S(1)}, u32[]{:S(2)}, u32[]{:S(2)}) collective-permute-start(bf16[288,512]{1,0:T(8,128)(2,1)S(1)} %get-tuple-element.51.s0), channel_id=1, source_target_pairs={{0,64},{16,80},{32,96},{48,112},{64,0},{80,16},{96,32},{112,48},{1... | collective-permute-start | bytes 884744 | tf_op jit(solution)/shard_map/ppermute | solution.py:481
  36.9 14.6 %collective-permute-start.12 = (bf16[288,512]{1,0:T(8,128)(2,1)S(1)}, bf16[288,512]{1,0:T(8,128)(2,1)S(1)}, u32[]{:S(2)}, u32[]{:S(2)}) collective-permute-start(bf16[288,512]{1,0:T(8,128)(2,1)S(1)} %get-tuple-element.51.s0), channel_id=1, source_target_pairs={{0,32},{16,48},{32,64},{48,80},{64,96},{80,112},{96,0},{112,16},{1... | collective-permute-start | bytes 884744 | tf_op jit(solution)/shard_map/ppermute | solution.py:481
  37.5 16.8 %collective-permute-start.15 = (bf16[288,512]{1,0:T(8,128)(2,1)S(1)}, bf16[288,512]{1,0:T(8,128)(2,1)S(1)}, u32[]{:S(2)}, u32[]{:S(2)}) collective-permute-start(bf16[288,512]{1,0:T(8,128)(2,1)S(1)} %get-tuple-element.51.s0), channel_id=1, source_target_pairs={{0,16},{16,0},{32,48},{48,32},{64,80},{80,64},{96,112},{112,96},{1... | collective-permute-start | bytes 884744 | tf_op jit(solution)/shard_map/ppermute | solution.py:484
  43.0 11.4 %collective-permute-start.18 = (bf16[288,512]{1,0:T(8,128)(2,1)S(1)}, bf16[288,512]{1,0:T(8,128)(2,1)S(1)}, u32[]{:S(2)}, u32[]{:S(2)}) collective-permute-start(bf16[288,512]{1,0:T(8,128)(2,1)S(1)} %collective-permute-done.14.s3), channel_id=1, source_target_pairs={{0,16},{16,0},{32,48},{48,32},{64,80},{80,64},{96,112},{112,96},{1... | collective-permute-start | bytes 884744 | tf_op jit(solution)/shard_map/ppermute | solution.py:484
  50.0 4.4 %collective-permute-start.17 = (bf16[288,512]{1,0:T(8,128)(2,1)S(1)}, bf16[288,512]{1,0:T(8,128)(2,1)S(1)}, u32[]{:S(2)}, u32[]{:S(2)}) collective-permute-start(bf16[288,512]{1,0:T(8,128)(2,1)S(1)} %collective-permute-done.13.s2), channel_id=1, source_target_pairs={{0,16},{16,0},{32,48},{48,32},{64,80},{80,64},{96,112},{112,96},{1... | collective-permute-start | bytes 884744 | tf_op jit(solution)/shard_map/ppermute | solution.py:484
  51.5 3.3 %collective-permute-start.16 = (bf16[288,512]{1,0:T(8,128)(2,1)S(1)}, bf16[288,512]{1,0:T(8,128)(2,1)S(1)}, u32[]{:S(2)}, u32[]{:S(2)}) collective-permute-start(bf16[288,512]{1,0:T(8,128)(2,1)S(1)} %collective-permute-done.12.s1), channel_id=1, source_target_pairs={{0,16},{16,0},{32,48},{48,32},{64,80},{80,64},{96,112},{112,96},{1... | collective-permute-start | bytes 884744 | tf_op jit(solution)/shard_map/ppermute | solution.py:484
  54.4 33.1 %copy-start = (bf16[1,32,32]{2,1,0:T(8,128)(2,1)S(1)}, bf16[1,32,32]{2,1,0:T(8,128)(2,1)}, u32[]{:S(2)}) copy-start(bf16[1,32,32]{2,1,0:T(8,128)(2,1)} %param.11) | copy-start | bytes 6148
